TPU v7x, 32 devices: a whole 2x2x4 slice. The times are simulated.
32 devices in a mesh: grp: 4 (over z), gy: 2 (over y), gx: 4 (over x, core).
Axes of the slice: x: 2, y: 2, z: 4, core: 2. Of those that a mesh axis runs over, the one named last changes fastest.
Arguments:
- residual: float32 [64, 32, 512], P('grp', 'gy', 'gx'), may hold values from -6 to 6
- mobility: float32 [64, 32, 512], P('grp', 'gy', 'gx'), may hold values from 0.1 to 10
Outputs:
- correction: float32 [64, 32, 512], P('grp', 'gy', 'gx')
All inputs are finite; a program needn't handle non-finite values.
Results may differ from a plain program's by a relative error of at most 0.0001.
Values sent between devices are 32-bit elements; how exact they have to be, the bound alone decides.
No kernel may reach another device: no remote copies, remote signals or barrier semaphores. Data moves between devices by JAX's collectives and lax.ppermute only.
A program may use at most 64 MiB of HBM per device.

v0:
```python
import jax
import jax.numpy as jnp
from jax import lax
from jax.sharding import PartitionSpec as P

LEVELS = 5
SWEEPS = 2
COARSE = 8


RELAX_WEIGHT = 0.8


def extended(cells, sides, width):
    for axis, dim in sides:
        count = lax.axis_size(axis)
        ends = count - 1
        head = lax.slice_in_dim(cells, 0, width, axis=dim)
        tail = lax.slice_in_dim(cells, cells.shape[dim] - width, cells.shape[dim], axis=dim)
        cells = jnp.concatenate(
            [
                lax.ppermute(tail, axis, [(i, (i + 1) % count) for i in range(ends)]),
                cells,
                lax.ppermute(head, axis, [((i + 1) % count, i) for i in range(ends)]),
            ],
            axis=dim,
        )
    return cells


def interior(values):
    return values[1:-1, 1:-1, 1:-1]


def neighbours(padded):
    return (
        padded[:-2, 1:-1, 1:-1],
        padded[1:-1, :-2, 1:-1],
        padded[1:-1, 1:-1, :-2],
        padded[2:, 1:-1, 1:-1],
        padded[1:-1, 2:, 1:-1],
        padded[1:-1, 1:-1, 2:],
    )


def face_coefficients(padded_mobility):
    centre = interior(padded_mobility)
    weights = tuple((0.5 * (centre + neighbour) for neighbour in neighbours(padded_mobility)))
    diagonal = weights[0] + weights[1] + weights[2] + weights[3] + weights[4] + weights[5]
    return (weights, diagonal)


def operate(padded, weights, diagonal, factor):
    summed = diagonal * interior(padded)
    for weight, neighbour in zip(weights, neighbours(padded)):
        summed = summed - weight * neighbour
    return factor * summed


def relaxed(padded, source, weights, diagonal, factor):
    return interior(padded) + RELAX_WEIGHT * (
        source - operate(padded, weights, diagonal, factor)
    ) / (factor * diagonal)


def restrict(values):
    shaped = values.reshape(
        values.shape[0] // 2, 2, values.shape[1] // 2, 2, values.shape[2] // 2, 2
    )
    return jnp.mean(shaped, axis=(1, 3, 5))


def prolong(values):
    widened = jnp.broadcast_to(
        values[:, None, :, None, :, None],
        (values.shape[0], 2, values.shape[1], 2, values.shape[2], 2),
    )
    return widened.reshape(2 * values.shape[0], 2 * values.shape[1], 2 * values.shape[2])


def spread_flags(layout):
    return (layout == "all", layout != "single", layout != "single")


def mesh_position():
    return (
        (lax.axis_index("grp"), lax.axis_index("gy"), lax.axis_index("gx")),
        (lax.axis_size("grp"), lax.axis_size("gy"), lax.axis_size("gx")),
    )


def take_block(values, source_layout, target_layout, block_shape):
    indices, counts = mesh_position()
    present = spread_flags(source_layout)
    wanted = spread_flags(target_layout)
    offsets = []
    for dimension in range(3):
        if wanted[dimension] and (not present[dimension]):
            offsets.append(indices[dimension] * block_shape[dimension])
        else:
            offsets.append(jnp.int32(0))
    return lax.dynamic_slice(values, offsets, block_shape)


def all_rim(values, loop_width):
    return extended(values, (("grp", 0), ("gy", 1), ("gx", 2)), loop_width)


def on_device(residual, mobility):
    ghost_depth = 1
    single_level = 4
    layouts = (
        ["all"] * 2 + ["group"] * (single_level - 2) + ["single"] * (LEVELS + 1 - single_level)
    )

    def ghost_rim(values, layout, loop_width):
        if layout == "all":
            return all_rim(values, loop_width)
        if layout == "group":
            sides = extended(values, (("gy", 1), ("gx", 2)), loop_width)
            return jnp.pad(sides, ((loop_width, loop_width), (0, 0), (0, 0)))
        return jnp.pad(values, loop_width)

    def join_blocks(stacked):
        counts = (lax.axis_size("gy"), lax.axis_size("gx"))
        grid = stacked.reshape(
            counts[0], counts[1], stacked.shape[1], stacked.shape[2], stacked.shape[3]
        )
        return grid.transpose(2, 0, 3, 1, 4).reshape(
            stacked.shape[1], counts[0] * stacked.shape[2], counts[1] * stacked.shape[3]
        )

    def collect(members, layout):
        if layout == "group":
            return lax.all_gather(members, "grp", axis=0, tiled=True)
        stacked = (
            lax.all_gather(members[0][None], ("gy", "gx"), axis=0, tiled=True),
            lax.all_gather(members[1][None], ("gy", "gx"), axis=0, tiled=True),
        )
        return (join_blocks(stacked[0]), join_blocks(stacked[1]))

    source = residual
    level_mobility = mobility
    leftover = residual
    kept_levels = []
    iterate = residual
    for grid_level in range(LEVELS + 1):
        layout = layouts[grid_level]
        if grid_level > 0:
            source = restrict(leftover)
            level_mobility = restrict(level_mobility)
            if layout != layouts[grid_level - 1]:
                source, level_mobility = collect((source, level_mobility), layout)
        factor = 0.25**grid_level
        if grid_level == LEVELS:
            weights, diagonal = face_coefficients(jnp.pad(level_mobility, 1))
            iterate = RELAX_WEIGHT * source / (factor * diagonal)
            for repeat in range(COARSE - 1):
                iterate = relaxed(jnp.pad(iterate, 1), source, weights, diagonal, factor)
        else:
            loop_width = ghost_depth if layout != "single" else 1
            weights, diagonal = face_coefficients(ghost_rim(level_mobility, layout, loop_width))
            mask_loop = None
            safe_diag = None
            source_loop = None
            iterate = RELAX_WEIGHT * source / (factor * diagonal)
            iterate = relaxed(ghost_rim(iterate, layout, 1), source, weights, diagonal, factor)
            inner_weights = tuple((weight for weight in weights))
            leftover = source - operate(
                ghost_rim(iterate, layout, 1), inner_weights, diagonal, factor
            )
            kept_levels.append(
                (iterate, source, source_loop, weights, diagonal, safe_diag, mask_loop, loop_width)
            )
    for grid_level in range(LEVELS - 1, -1, -1):
        kept_iterate, source, source_loop, weights, diagonal, safe_diag, mask_loop, loop_width = (
            kept_levels[grid_level]
        )
        layout = layouts[grid_level]
        factor = 0.25**grid_level
        coarse_shape = tuple((length // 2 for length in source.shape))
        iterate = kept_iterate + prolong(
            take_block(iterate, layouts[grid_level + 1], layout, coarse_shape)
        )
        for repeat in range(SWEEPS):
            iterate = relaxed(ghost_rim(iterate, layout, 1), source, weights, diagonal, factor)
    return iterate


def solution(mesh):
    in_specs = (P("grp", "gy", "gx"), P("grp", "gy", "gx"))
    out_specs = P("grp", "gy", "gx")
    return jax.shard_map(
        on_device, mesh=mesh, in_specs=in_specs, out_specs=out_specs, check_vma=False
    )
```

profile of v0, /device:TPU:0, one launch (start us, length us, event | category | flops | bytes accessed | tf_op | source)
XLA Modules:
  0.0 448.9 jit_solution(351948599311723068)
XLA Ops:
  0.7 4.9 %collective-permute-start = (f32[1,16,128]{2,1,0:T(8,128)S(1)}, f32[1,16,128]{2,1,0:T(8,128)S(1)}, u32[]{:S(2)}, u32[]{:S(2)}) collective-permute-start(f32[1,16,128]{2,1,0:T(8,128)S(1)} %get-tuple-element.66), channel_id=1, source_target_pairs={{0,8},{8,16},{16,24},{1,9},{9,17},{17,25},{2,10},{10,18},{18,26},{... | collective-permute-start | bytes 24584 | tf_op jit(solution)/shard_map/ppermute | solution.py:22
  7.9 3.3 collective-permute-done.1
  11.2 3.4 collective-permute-start.2
  16.1 10.5 %reshape.154 = f32[8,2,8,2,64,2]{5,4,3,2,1,0:T(8,128)} reshape(f32[16,16,128]{2,1,0:T(8,128)} %param.3) | data formatting | bytes 262144 | tf_op jit(solution)/shard_map/reshape | solution.py:67
  26.6 4.0 reduce_sum.101
  33.5 3.8 collective-permute-done.5
  37.5 3.5 collective-permute-start.6
  42.3 4.5 %collective-permute-start.18 = (f32[1,8,64]{2,1,0:T(8,128)S(1)}, f32[1,8,64]{2,1,0:T(8,128)S(1)}, u32[]{:S(2)}, u32[]{:S(2)}) collective-permute-start(f32[1,8,64]{2,1,0:T(8,128)S(1)} %get-tuple-element.117), channel_id=1, source_target_pairs={{0,8},{8,16},{16,24},{1,9},{9,17},{17,25},{2,10},{10,18},{18,26},{... | collective-permute-start | bytes 6152 | tf_op jit(solution)/shard_map/ppermute | solution.py:22
  49.4 4.5 %collective-permute-start.8 = (f32[18,1,128]{2,1,0:T(1,128)S(1)}, f32[18,1,128]{2,1,0:T(1,128)S(1)}, u32[]{:S(2)}, u32[]{:S(2)}) collective-permute-start(f32[18,1,128]{2,1,0:T(1,128)S(1)} %get-tuple-element.53), channel_id=1, source_target_pairs={{0,4},{1,5},{2,6},{3,7},{8,12},{9,13},{10,14},{11,15},{16,20},{17,... | collective-permute-start | bytes 27656 | tf_op jit(solution)/shard_map/ppermute | solution.py:22
  55.3 14.4 %all_gather.13 = f32[16,4,32]{2,1,0:T(4,128)S(1)} all-gather(f32[4,4,32]{2,1,0:T(4,128)S(1)} %broadcast_multiply_fusion.2), channel_id=1, replica_groups=mesh['grp'=4,'gy'=2,'gx'=4] {'grp'}, dimensions={0}, use_global_device_ids=true | all-gather | bytes 10240 | tf_op jit(solution)/shard_map/all_gather | solution.py:135
  73.3 4.5 %collective-permute-start.36 = (f32[16,1,32]{2,0,1:T(8,128)S(1)}, f32[16,1,32]{2,0,1:T(8,128)S(1)}, u32[]{:S(2)}, u32[]{:S(2)}) collective-permute-start(f32[16,1,32]{2,0,1:T(8,128)S(1)} %get-tuple-element.110), channel_id=1, source_target_pairs={{0,4},{1,5},{2,6},{3,7},{8,12},{9,13},{10,14},{11,15},{16,20},{17,... | collective-permute-start | bytes 6152 | tf_op jit(solution)/shard_map/ppermute | solution.py:22
  83.1 4.5 %collective-permute-start.20 = (f32[10,1,64]{2,1,0:T(1,128)S(1)}, f32[10,1,64]{2,1,0:T(1,128)S(1)}, u32[]{:S(2)}, u32[]{:S(2)}) collective-permute-start(f32[10,1,64]{2,1,0:T(1,128)S(1)} %get-tuple-element.96), channel_id=1, source_target_pairs={{0,4},{1,5},{2,6},{3,7},{8,12},{9,13},{10,14},{11,15},{16,20},{17,... | collective-permute-start | bytes 7688 | tf_op jit(solution)/shard_map/ppermute | solution.py:22
  89.0 4.5 %collective-permute-start.14 = (f32[18,1,128]{2,1,0:T(1,128)S(1)}, f32[18,1,128]{2,1,0:T(1,128)S(1)}, u32[]{:S(2)}, u32[]{:S(2)}) collective-permute-start(f32[18,1,128]{2,1,0:T(1,128)S(1)} %get-tuple-element.51), channel_id=1, source_target_pairs={{0,4},{1,5},{2,6},{3,7},{8,12},{9,13},{10,14},{11,15},{16,20},{17,... | collective-permute-start | bytes 27656 | tf_op jit(solution)/shard_map/ppermute | solution.py:22
  94.9 4.2 collective-permute-done.15
  99.3 3.8 collective-permute-start.16
  104.5 7.1 %collective-permute-start.22 = (f32[10,10,1]{2,1,0:T(8,128)S(1)}, f32[10,10,1]{2,1,0:T(8,128)S(1)}, u32[]{:S(2)}, u32[]{:S(2)}) collective-permute-start(f32[10,10,1]{2,1,0:T(8,128)S(1)} %get-tuple-element.76), channel_id=1, source_target_pairs={{0,1},{1,2},{2,3},{4,5},{5,6},{6,7},{8,9},{9,10},{10,11},{12,13},{... | collective-permute-start | bytes 1208 | tf_op jit(solution)/shard_map/ppermute | solution.py:22
  113.2 9.8 %reshape.153 = f32[8,2,8,2,64,2]{5,4,3,2,1,0:T(8,128)} reshape(f32[16,16,128]{2,1,0:T(8,128)S(1)} %fusion.34) | data formatting | bytes 262144 | tf_op jit(solution)/shard_map/reshape | solution.py:67
  123.0 4.0 reduce_sum.97
  127.1 4.5 %collective-permute-start.24 = (f32[1,8,64]{2,1,0:T(8,128)S(1)}, f32[1,8,64]{2,1,0:T(8,128)S(1)}, u32[]{:S(2)}, u32[]{:S(2)}) collective-permute-start(f32[1,8,64]{2,1,0:T(8,128)S(1)} %get-tuple-element.114), channel_id=1, source_target_pairs={{0,8},{8,16},{16,24},{1,9},{9,17},{17,25},{2,10},{10,18},{18,26},{... | collective-permute-start | bytes 6152 | tf_op jit(solution)/shard_map/ppermute | solution.py:22
  133.0 4.2 collective-permute-done.25
  140.2 4.2 collective-permute-done.27
  147.2 5.9 %collective-permute-done.29 = f32[10,10,1]{2,1,0:T(8,128)S(1)} collective-permute-done((f32[10,10,1]{2,1,0:T(8,128)S(1)}, f32[10,10,1]{2,1,0:T(8,128)S(1)}, u32[]{:S(2)}, u32[]{:S(2)}) %collective-permute-start.29) | collective-permute-done | bytes 432 | tf_op jit(solution)/shard_map/ppermute | solution.py:24
  153.3 3.0 collective-permute-start.30
  157.7 4.2 collective-permute-done.31
  164.9 3.4 collective-permute-start.38
  169.7 4.1 collective-permute-start.34
  175.3 3.0 collective-permute-done.35
  179.6 13.1 %all_gather.12 = f32[16,4,32]{2,1,0:T(4,128)S(1)} all-gather(f32[4,4,32]{2,1,0:T(4,128)S(1)} %broadcast_multiply_fusion.3), channel_id=1, replica_groups=mesh['grp'=4,'gy'=2,'gx'=4] {'grp'}, dimensions={0}, use_global_device_ids=true | all-gather | bytes 10240 | tf_op jit(solution)/shard_map/all_gather | solution.py:135
  192.9 4.5 %collective-permute-start.40 = (f32[16,1,32]{2,0,1:T(8,128)S(1)}, f32[16,1,32]{2,0,1:T(8,128)S(1)}, u32[]{:S(2)}, u32[]{:S(2)}) collective-permute-start(f32[16,1,32]{2,0,1:T(8,128)S(1)} %get-tuple-element.108), channel_id=1, source_target_pairs={{0,4},{1,5},{2,6},{3,7},{8,12},{9,13},{10,14},{11,15},{16,20},{17,... | collective-permute-start | bytes 6152 | tf_op jit(solution)/shard_map/ppermute | solution.py:22
  198.7 4.5 %collective-permute-start.48 = (f32[8,1,16]{2,0,1:T(8,128)S(1)}, f32[8,1,16]{2,0,1:T(8,128)S(1)}, u32[]{:S(2)}, u32[]{:S(2)}) collective-permute-start(f32[8,1,16]{2,0,1:T(8,128)S(1)} %get-tuple-element.140), channel_id=1, source_target_pairs={{0,4},{1,5},{2,6},{3,7},{8,12},{9,13},{10,14},{11,15},{16,20},{17,... | collective-permute-start | bytes 1544 | tf_op jit(solution)/shard_map/ppermute | solution.py:22
  208.8 3.5 collective-permute-done.43
  212.5 4.5 %collective-permute-start.44 = (f32[16,1,32]{2,0,1:T(8,128)S(1)}, f32[16,1,32]{2,0,1:T(8,128)S(1)}, u32[]{:S(2)}, u32[]{:S(2)}) collective-permute-start(f32[16,1,32]{2,0,1:T(8,128)S(1)} %get-tuple-element.106), channel_id=1, source_target_pairs={{0,4},{1,5},{2,6},{3,7},{8,12},{9,13},{10,14},{11,15},{16,20},{17,... | collective-permute-start | bytes 6152 | tf_op jit(solution)/shard_map/ppermute | solution.py:22
  218.4 4.4 collective-permute-start.50
  224.3 3.0 collective-permute-start.46
  232.2 4.5 %collective-permute-start.52 = (f32[8,1,16]{2,0,1:T(8,128)S(1)}, f32[8,1,16]{2,0,1:T(8,128)S(1)}, u32[]{:S(2)}, u32[]{:S(2)}) collective-permute-start(f32[8,1,16]{2,0,1:T(8,128)S(1)} %get-tuple-element.137), channel_id=1, source_target_pairs={{0,4},{1,5},{2,6},{3,7},{8,12},{9,13},{10,14},{11,15},{16,20},{17,... | collective-permute-start | bytes 1544 | tf_op jit(solution)/shard_map/ppermute | solution.py:22
  238.2 10.7 %all-gather.3 = f32[8,4,8]{2,1,0:T(4,128)S(1)} all-gather(f32[1,4,8]{2,1,0:T(4,128)S(1)} %multiply_bitcast_fusion), channel_id=3, replica_groups=mesh['grp'=4,'gy'=2,'gx'=4] {'gy','gx'}, dimensions={0}, use_global_device_ids=true | all-gather | bytes 1152 | tf_op jit(solution)/shard_map/all_gather | solution.py:138
  252.7 3.0 collective-permute-done.55
  259.8 4.2 collective-permute-done.57
  270.9 9.8 %all-gather.2 = f32[8,4,8]{2,1,0:T(4,128)S(1)} all-gather(f32[1,4,8]{2,1,0:T(4,128)S(1)} %multiply_bitcast_fusion.1), channel_id=2, replica_groups=mesh['grp'=4,'gy'=2,'gx'=4] {'gy','gx'}, dimensions={0}, use_global_device_ids=true | all-gather | bytes 1152 | tf_op jit(solution)/shard_map/all_gather | solution.py:137
  285.8 4.2 collective-permute-done.61
  292.7 4.1 collective-permute-done.63
  299.9 4.2 collective-permute-done.65
  304.2 2.9 collective-permute-start.66
  314.8 4.2 collective-permute-done.69
  319.0 2.9 collective-permute-start.70
  329.3 4.2 collective-permute-done.73
  334.9 3.9 collective-permute-start.74
  344.0 4.2 collective-permute-done.77
  351.5 4.2 collective-permute-done.79
  358.4 6.3 %collective-permute-done.81 = f32[10,10,1]{2,1,0:T(8,128)S(1)} collective-permute-done((f32[10,10,1]{2,1,0:T(8,128)S(1)}, f32[10,10,1]{2,1,0:T(8,128)S(1)}, u32[]{:S(2)}, u32[]{:S(2)}) %collective-permute-start.81) | collective-permute-done | bytes 432 | tf_op jit(solution)/shard_map/ppermute | solution.py:24
  364.9 3.0 collective-permute-start.82
  369.3 4.2 collective-permute-done.83
  376.4 4.2 collective-permute-done.85
  384.3 4.1 collective-permute-done.87
  388.5 4.0 broadcast_in_dim.54
  392.4 6.9 %reshape.164 = f32[16,16,128]{2,1,0:T(8,128)S(1)} reshape(f32[8,2,8,2,64,2]{5,4,3,2,1,0:T(8,128)} %broadcast_in_dim.54) | data formatting | bytes 262144 | tf_op jit(solution)/shard_map/reshape | solution.py:78
  399.4 3.7 collective-permute-start.88
  404.4 4.2 collective-permute-done.89
  411.7 4.2 collective-permute-done.91
  419.5 4.4 collective-permute-done.93
  427.4 4.2 collective-permute-done.95
  434.6 4.2 collective-permute-done.97
  439.0 3.4 collective-permute-start.98
  443.7 4.3 collective-permute-done.99
  (316 shorter events, 137.0 us)
Async XLA Ops:
  0.7 6.3 %collective-permute-start = (f32[1,16,128]{2,1,0:T(8,128)S(1)}, f32[1,16,128]{2,1,0:T(8,128)S(1)}, u32[]{:S(2)}, u32[]{:S(2)}) collective-permute-start(f32[1,16,128]{2,1,0:T(8,128)S(1)} %get-tuple-element.66), channel_id=1, source_target_pairs={{0,8},{8,16},{16,24},{1,9},{9,17},{17,25},{2,10},{10,18},{18,26},{... | collective-permute-start | bytes 24584 | tf_op jit(solution)/shard_map/ppermute | solution.py:22
  5.6 5.5 %collective-permute-start.1 = (f32[1,16,128]{2,1,0:T(8,128)S(1)}, f32[1,16,128]{2,1,0:T(8,128)S(1)}, u32[]{:S(2)}, u32[]{:S(2)}) collective-permute-start(f32[1,16,128]{2,1,0:T(8,128)S(1)} %get-tuple-element.65), channel_id=1, source_target_pairs={{8,0},{16,8},{24,16},{9,1},{17,9},{25,17},{10,2},{18,10},{26,18},{... | collective-permute-start | bytes 24584 | tf_op jit(solution)/shard_map/ppermute | solution.py:24
  11.2 19.4 %collective-permute-start.2 = (f32[18,1,128]{2,1,0:T(1,128)S(1)}, f32[18,1,128]{2,1,0:T(1,128)S(1)}, u32[]{:S(2)}, u32[]{:S(2)}) collective-permute-start(f32[18,1,128]{2,1,0:T(1,128)S(1)} %get-tuple-element.56), channel_id=1, source_target_pairs={{0,4},{1,5},{2,6},{3,7},{8,12},{9,13},{10,14},{11,15},{16,20},{17,... | collective-permute-start | bytes 27656 | tf_op jit(solution)/shard_map/ppermute | solution.py:22
  14.7 16.0 %collective-permute-start.3 = (f32[18,1,128]{2,1,0:T(1,128)S(1)}, f32[18,1,128]{2,1,0:T(1,128)S(1)}, u32[]{:S(2)}, u32[]{:S(2)}) collective-permute-start(f32[18,1,128]{2,1,0:T(1,128)S(1)} %get-tuple-element.55), channel_id=1, source_target_pairs={{4,0},{5,1},{6,2},{7,3},{12,8},{13,9},{14,10},{15,11},{20,16},{21,... | collective-permute-start | bytes 27656 | tf_op jit(solution)/shard_map/ppermute | solution.py:24
  37.5 11.9 %collective-permute-start.6 = (f32[1,16,128]{2,1,0:T(8,128)S(1)}, f32[1,16,128]{2,1,0:T(8,128)S(1)}, u32[]{:S(2)}, u32[]{:S(2)}) collective-permute-start(f32[1,16,128]{2,1,0:T(8,128)S(1)} %get-tuple-element.63), channel_id=1, source_target_pairs={{0,8},{8,16},{16,24},{1,9},{9,17},{17,25},{2,10},{10,18},{18,26},{... | collective-permute-start | bytes 24584 | tf_op jit(solution)/shard_map/ppermute | solution.py:22
  41.0 8.4 %collective-permute-start.7 = (f32[1,16,128]{2,1,0:T(8,128)S(1)}, f32[1,16,128]{2,1,0:T(8,128)S(1)}, u32[]{:S(2)}, u32[]{:S(2)}) collective-permute-start(f32[1,16,128]{2,1,0:T(8,128)S(1)} %get-tuple-element.64), channel_id=1, source_target_pairs={{8,0},{16,8},{24,16},{9,1},{17,9},{25,17},{10,2},{18,10},{26,18},{... | collective-permute-start | bytes 24584 | tf_op jit(solution)/shard_map/ppermute | solution.py:24
  42.3 39.4 %collective-permute-start.18 = (f32[1,8,64]{2,1,0:T(8,128)S(1)}, f32[1,8,64]{2,1,0:T(8,128)S(1)}, u32[]{:S(2)}, u32[]{:S(2)}) collective-permute-start(f32[1,8,64]{2,1,0:T(8,128)S(1)} %get-tuple-element.117), channel_id=1, source_target_pairs={{0,8},{8,16},{16,24},{1,9},{9,17},{17,25},{2,10},{10,18},{18,26},{... | collective-permute-start | bytes 6152 | tf_op jit(solution)/shard_map/ppermute | solution.py:22
  46.9 36.2 %collective-permute-start.19 = (f32[1,8,64]{2,1,0:T(8,128)S(1)}, f32[1,8,64]{2,1,0:T(8,128)S(1)}, u32[]{:S(2)}, u32[]{:S(2)}) collective-permute-start(f32[1,8,64]{2,1,0:T(8,128)S(1)} %get-tuple-element.116), channel_id=1, source_target_pairs={{8,0},{16,8},{24,16},{9,1},{17,9},{25,17},{10,2},{18,10},{26,18},{... | collective-permute-start | bytes 6152 | tf_op jit(solution)/shard_map/ppermute | solution.py:24
  49.4 20.3 %collective-permute-start.8 = (f32[18,1,128]{2,1,0:T(1,128)S(1)}, f32[18,1,128]{2,1,0:T(1,128)S(1)}, u32[]{:S(2)}, u32[]{:S(2)}) collective-permute-start(f32[18,1,128]{2,1,0:T(1,128)S(1)} %get-tuple-element.53), channel_id=1, source_target_pairs={{0,4},{1,5},{2,6},{3,7},{8,12},{9,13},{10,14},{11,15},{16,20},{17,... | collective-permute-start | bytes 27656 | tf_op jit(solution)/shard_map/ppermute | solution.py:22
  54.0 15.8 %collective-permute-start.9 = (f32[18,1,128]{2,1,0:T(1,128)S(1)}, f32[18,1,128]{2,1,0:T(1,128)S(1)}, u32[]{:S(2)}, u32[]{:S(2)}) collective-permute-start(f32[18,1,128]{2,1,0:T(1,128)S(1)} %get-tuple-element.54), channel_id=1, source_target_pairs={{4,0},{5,1},{6,2},{7,3},{12,8},{13,9},{14,10},{15,11},{20,16},{21,... | collective-permute-start | bytes 27656 | tf_op jit(solution)/shard_map/ppermute | solution.py:24
  69.9 8.3 %collective-permute-start.10 = (f32[18,18,1]{2,1,0:T(8,128)S(1)}, f32[18,18,1]{2,1,0:T(8,128)S(1)}, u32[]{:S(2)}, u32[]{:S(2)}) collective-permute-start(f32[18,18,1]{2,1,0:T(8,128)S(1)} %get-tuple-element.43), channel_id=1, source_target_pairs={{0,1},{1,2},{2,3},{4,5},{5,6},{6,7},{8,9},{9,10},{10,11},{12,13},{... | collective-permute-start | bytes 3896 | tf_op jit(solution)/shard_map/ppermute | solution.py:22
  71.9 7.6 %collective-permute-start.11 = (f32[18,18,1]{2,1,0:T(8,128)S(1)}, f32[18,18,1]{2,1,0:T(8,128)S(1)}, u32[]{:S(2)}, u32[]{:S(2)}) collective-permute-start(f32[18,18,1]{2,1,0:T(8,128)S(1)} %get-tuple-element.44), channel_id=1, source_target_pairs={{1,0},{2,1},{3,2},{5,4},{6,5},{7,6},{9,8},{10,9},{11,10},{13,12},{... | collective-permute-start | bytes 3896 | tf_op jit(solution)/shard_map/ppermute | solution.py:24
  73.3 66.9 %collective-permute-start.36 = (f32[16,1,32]{2,0,1:T(8,128)S(1)}, f32[16,1,32]{2,0,1:T(8,128)S(1)}, u32[]{:S(2)}, u32[]{:S(2)}) collective-permute-start(f32[16,1,32]{2,0,1:T(8,128)S(1)} %get-tuple-element.110), channel_id=1, source_target_pairs={{0,4},{1,5},{2,6},{3,7},{8,12},{9,13},{10,14},{11,15},{16,20},{17,... | collective-permute-start | bytes 6152 | tf_op jit(solution)/shard_map/ppermute | solution.py:22
  78.2 79.4 %collective-permute-start.37 = (f32[16,1,32]{2,0,1:T(8,128)S(1)}, f32[16,1,32]{2,0,1:T(8,128)S(1)}, u32[]{:S(2)}, u32[]{:S(2)}) collective-permute-start(f32[16,1,32]{2,0,1:T(8,128)S(1)} %get-tuple-element.111), channel_id=1, source_target_pairs={{4,0},{5,1},{6,2},{7,3},{12,8},{13,9},{14,10},{15,11},{20,16},{21,... | collective-permute-start | bytes 6152 | tf_op jit(solution)/shard_map/ppermute | solution.py:24
  79.8 7.8 %collective-permute-start.12 = (f32[1,16,128]{2,1,0:T(8,128)S(1)}, f32[1,16,128]{2,1,0:T(8,128)S(1)}, u32[]{:S(2)}, u32[]{:S(2)}) collective-permute-start(f32[1,16,128]{2,1,0:T(8,128)S(1)} %get-tuple-element.61), channel_id=1, source_target_pairs={{0,8},{8,16},{16,24},{1,9},{9,17},{17,25},{2,10},{10,18},{18,26},{... | collective-permute-start | bytes 24584 | tf_op jit(solution)/shard_map/ppermute | solution.py:22
  81.8 7.2 %collective-permute-start.13 = (f32[1,16,128]{2,1,0:T(8,128)S(1)}, f32[1,16,128]{2,1,0:T(8,128)S(1)}, u32[]{:S(2)}, u32[]{:S(2)}) collective-permute-start(f32[1,16,128]{2,1,0:T(8,128)S(1)} %get-tuple-element.62), channel_id=1, source_target_pairs={{8,0},{16,8},{24,16},{9,1},{17,9},{25,17},{10,2},{18,10},{26,18},{... | collective-permute-start | bytes 24584 | tf_op jit(solution)/shard_map/ppermute | solution.py:24
  83.1 10.4 %collective-permute-start.20 = (f32[10,1,64]{2,1,0:T(1,128)S(1)}, f32[10,1,64]{2,1,0:T(1,128)S(1)}, u32[]{:S(2)}, u32[]{:S(2)}) collective-permute-start(f32[10,1,64]{2,1,0:T(1,128)S(1)} %get-tuple-element.96), channel_id=1, source_target_pairs={{0,4},{1,5},{2,6},{3,7},{8,12},{9,13},{10,14},{11,15},{16,20},{17,... | collective-permute-start | bytes 7688 | tf_op jit(solution)/shard_map/ppermute | solution.py:22
  87.6 7.2 %collective-permute-start.21 = (f32[10,1,64]{2,1,0:T(1,128)S(1)}, f32[10,1,64]{2,1,0:T(1,128)S(1)}, u32[]{:S(2)}, u32[]{:S(2)}) collective-permute-start(f32[10,1,64]{2,1,0:T(1,128)S(1)} %get-tuple-element.95), channel_id=1, source_target_pairs={{4,0},{5,1},{6,2},{7,3},{12,8},{13,9},{14,10},{15,11},{20,16},{21,... | collective-permute-start | bytes 7688 | tf_op jit(solution)/shard_map/ppermute | solution.py:24
  89.0 5.9 %collective-permute-start.14 = (f32[18,1,128]{2,1,0:T(1,128)S(1)}, f32[18,1,128]{2,1,0:T(1,128)S(1)}, u32[]{:S(2)}, u32[]{:S(2)}) collective-permute-start(f32[18,1,128]{2,1,0:T(1,128)S(1)} %get-tuple-element.51), channel_id=1, source_target_pairs={{0,4},{1,5},{2,6},{3,7},{8,12},{9,13},{10,14},{11,15},{16,20},{17,... | collective-permute-start | bytes 27656 | tf_op jit(solution)/shard_map/ppermute | solution.py:22
  93.5 5.6 %collective-permute-start.15 = (f32[18,1,128]{2,1,0:T(1,128)S(1)}, f32[18,1,128]{2,1,0:T(1,128)S(1)}, u32[]{:S(2)}, u32[]{:S(2)}) collective-permute-start(f32[18,1,128]{2,1,0:T(1,128)S(1)} %get-tuple-element.52), channel_id=1, source_target_pairs={{4,0},{5,1},{6,2},{7,3},{12,8},{13,9},{14,10},{15,11},{20,16},{21,... | collective-permute-start | bytes 27656 | tf_op jit(solution)/shard_map/ppermute | solution.py:24
  99.3 12.3 %collective-permute-start.16 = (f32[18,18,1]{2,1,0:T(8,128)S(1)}, f32[18,18,1]{2,1,0:T(8,128)S(1)}, u32[]{:S(2)}, u32[]{:S(2)}) collective-permute-start(f32[18,18,1]{2,1,0:T(8,128)S(1)} %get-tuple-element.41), channel_id=1, source_target_pairs={{0,1},{1,2},{2,3},{4,5},{5,6},{6,7},{8,9},{9,10},{10,11},{12,13},{... | collective-permute-start | bytes 3896 | tf_op jit(solution)/shard_map/ppermute | solution.py:22
  103.1 9.8 %collective-permute-start.17 = (f32[18,18,1]{2,1,0:T(8,128)S(1)}, f32[18,18,1]{2,1,0:T(8,128)S(1)}, u32[]{:S(2)}, u32[]{:S(2)}) collective-permute-start(f32[18,18,1]{2,1,0:T(8,128)S(1)} %get-tuple-element.42), channel_id=1, source_target_pairs={{1,0},{2,1},{3,2},{5,4},{6,5},{7,6},{9,8},{10,9},{11,10},{13,12},{... | collective-permute-start | bytes 3896 | tf_op jit(solution)/shard_map/ppermute | solution.py:24
  104.5 22.5 %collective-permute-start.22 = (f32[10,10,1]{2,1,0:T(8,128)S(1)}, f32[10,10,1]{2,1,0:T(8,128)S(1)}, u32[]{:S(2)}, u32[]{:S(2)}) collective-permute-start(f32[10,10,1]{2,1,0:T(8,128)S(1)} %get-tuple-element.76), channel_id=1, source_target_pairs={{0,1},{1,2},{2,3},{4,5},{5,6},{6,7},{8,9},{9,10},{10,11},{12,13},{... | collective-permute-start | bytes 1208 | tf_op jit(solution)/shard_map/ppermute | solution.py:22
  111.6 15.4 %collective-permute-start.23 = (f32[10,10,1]{2,1,0:T(8,128)S(1)}, f32[10,10,1]{2,1,0:T(8,128)S(1)}, u32[]{:S(2)}, u32[]{:S(2)}) collective-permute-start(f32[10,10,1]{2,1,0:T(8,128)S(1)} %get-tuple-element.75), channel_id=1, source_target_pairs={{1,0},{2,1},{3,2},{5,4},{6,5},{7,6},{9,8},{10,9},{11,10},{13,12},{... | collective-permute-start | bytes 1208 | tf_op jit(solution)/shard_map/ppermute | solution.py:24
  127.1 5.9 %collective-permute-start.24 = (f32[1,8,64]{2,1,0:T(8,128)S(1)}, f32[1,8,64]{2,1,0:T(8,128)S(1)}, u32[]{:S(2)}, u32[]{:S(2)}) collective-permute-start(f32[1,8,64]{2,1,0:T(8,128)S(1)} %get-tuple-element.114), channel_id=1, source_target_pairs={{0,8},{8,16},{16,24},{1,9},{9,17},{17,25},{2,10},{10,18},{18,26},{... | collective-permute-start | bytes 6152 | tf_op jit(solution)/shard_map/ppermute | solution.py:22
  131.7 5.5 %collective-permute-start.25 = (f32[1,8,64]{2,1,0:T(8,128)S(1)}, f32[1,8,64]{2,1,0:T(8,128)S(1)}, u32[]{:S(2)}, u32[]{:S(2)}) collective-permute-start(f32[1,8,64]{2,1,0:T(8,128)S(1)} %get-tuple-element.115), channel_id=1, source_target_pairs={{8,0},{16,8},{24,16},{9,1},{17,9},{25,17},{10,2},{18,10},{26,18},{... | collective-permute-start | bytes 6152 | tf_op jit(solution)/shard_map/ppermute | solution.py:24
  138.9 5.5 %collective-permute-start.27 = (f32[10,1,64]{2,1,0:T(1,128)S(1)}, f32[10,1,64]{2,1,0:T(1,128)S(1)}, u32[]{:S(2)}, u32[]{:S(2)}) collective-permute-start(f32[10,1,64]{2,1,0:T(1,128)S(1)} %get-tuple-element.94), channel_id=1, source_target_pairs={{4,0},{5,1},{6,2},{7,3},{12,8},{13,9},{14,10},{15,11},{20,16},{21,... | collective-permute-start | bytes 7688 | tf_op jit(solution)/shard_map/ppermute | solution.py:24
  145.9 7.3 %collective-permute-start.29 = (f32[10,10,1]{2,1,0:T(8,128)S(1)}, f32[10,10,1]{2,1,0:T(8,128)S(1)}, u32[]{:S(2)}, u32[]{:S(2)}) collective-permute-start(f32[10,10,1]{2,1,0:T(8,128)S(1)} %get-tuple-element.74), channel_id=1, source_target_pairs={{1,0},{2,1},{3,2},{5,4},{6,5},{7,6},{9,8},{10,9},{11,10},{13,12},{... | collective-permute-start | bytes 1208 | tf_op jit(solution)/shard_map/ppermute | solution.py:24
  156.3 5.5 %collective-permute-start.31 = (f32[1,8,64]{2,1,0:T(8,128)S(1)}, f32[1,8,64]{2,1,0:T(8,128)S(1)}, u32[]{:S(2)}, u32[]{:S(2)}) collective-permute-start(f32[1,8,64]{2,1,0:T(8,128)S(1)} %get-tuple-element.113), channel_id=1, source_target_pairs={{8,0},{16,8},{24,16},{9,1},{17,9},{25,17},{10,2},{18,10},{26,18},{... | collective-permute-start | bytes 6152 | tf_op jit(solution)/shard_map/ppermute | solution.py:24
  161.9 7.7 %collective-permute-start.32 = (f32[10,1,64]{2,1,0:T(1,128)S(1)}, f32[10,1,64]{2,1,0:T(1,128)S(1)}, u32[]{:S(2)}, u32[]{:S(2)}) collective-permute-start(f32[10,1,64]{2,1,0:T(1,128)S(1)} %get-tuple-element.91), channel_id=1, source_target_pairs={{0,4},{1,5},{2,6},{3,7},{8,12},{9,13},{10,14},{11,15},{16,20},{17,... | collective-permute-start | bytes 7688 | tf_op jit(solution)/shard_map/ppermute | solution.py:22
  163.5 6.0 %collective-permute-start.33 = (f32[10,1,64]{2,1,0:T(1,128)S(1)}, f32[10,1,64]{2,1,0:T(1,128)S(1)}, u32[]{:S(2)}, u32[]{:S(2)}) collective-permute-start(f32[10,1,64]{2,1,0:T(1,128)S(1)} %get-tuple-element.92), channel_id=1, source_target_pairs={{4,0},{5,1},{6,2},{7,3},{12,8},{13,9},{14,10},{15,11},{20,16},{21,... | collective-permute-start | bytes 7688 | tf_op jit(solution)/shard_map/ppermute | solution.py:24
  164.9 10.2 %collective-permute-start.38 = (f32[16,6,1]{2,0,1:T(8,128)S(1)}, f32[16,6,1]{2,0,1:T(8,128)S(1)}, u32[]{:S(2)}, u32[]{:S(2)}) collective-permute-start(f32[16,6,1]{2,0,1:T(8,128)S(1)} %get-tuple-element.85), channel_id=1, source_target_pairs={{0,1},{1,2},{2,3},{4,5},{5,6},{6,7},{8,9},{9,10},{10,11},{12,13},{... | collective-permute-start | bytes 1160 | tf_op jit(solution)/shard_map/ppermute | solution.py:22
  168.3 6.9 %collective-permute-start.39 = (f32[16,6,1]{2,0,1:T(8,128)S(1)}, f32[16,6,1]{2,0,1:T(8,128)S(1)}, u32[]{:S(2)}, u32[]{:S(2)}) collective-permute-start(f32[16,6,1]{2,0,1:T(8,128)S(1)} %get-tuple-element.86), channel_id=1, source_target_pairs={{1,0},{2,1},{3,2},{5,4},{6,5},{7,6},{9,8},{10,9},{11,10},{13,12},{... | collective-permute-start | bytes 1160 | tf_op jit(solution)/shard_map/ppermute | solution.py:24
  169.7 5.6 %collective-permute-start.34 = (f32[10,10,1]{2,1,0:T(8,128)S(1)}, f32[10,10,1]{2,1,0:T(8,128)S(1)}, u32[]{:S(2)}, u32[]{:S(2)}) collective-permute-start(f32[10,10,1]{2,1,0:T(8,128)S(1)} %get-tuple-element.71), channel_id=1, source_target_pairs={{0,1},{1,2},{2,3},{4,5},{5,6},{6,7},{8,9},{9,10},{10,11},{12,13},{... | collective-permute-start | bytes 1208 | tf_op jit(solution)/shard_map/ppermute | solution.py:22
  192.9 11.7 %collective-permute-start.40 = (f32[16,1,32]{2,0,1:T(8,128)S(1)}, f32[16,1,32]{2,0,1:T(8,128)S(1)}, u32[]{:S(2)}, u32[]{:S(2)}) collective-permute-start(f32[16,1,32]{2,0,1:T(8,128)S(1)} %get-tuple-element.108), channel_id=1, source_target_pairs={{0,4},{1,5},{2,6},{3,7},{8,12},{9,13},{10,14},{11,15},{16,20},{17,... | collective-permute-start | bytes 6152 | tf_op jit(solution)/shard_map/ppermute | solution.py:22
  197.4 7.2 %collective-permute-start.41 = (f32[16,1,32]{2,0,1:T(8,128)S(1)}, f32[16,1,32]{2,0,1:T(8,128)S(1)}, u32[]{:S(2)}, u32[]{:S(2)}) collective-permute-start(f32[16,1,32]{2,0,1:T(8,128)S(1)} %get-tuple-element.109), channel_id=1, source_target_pairs={{4,0},{5,1},{6,2},{7,3},{12,8},{13,9},{14,10},{15,11},{20,16},{21,... | collective-permute-start | bytes 6152 | tf_op jit(solution)/shard_map/ppermute | solution.py:24
  198.7 8.6 %collective-permute-start.48 = (f32[8,1,16]{2,0,1:T(8,128)S(1)}, f32[8,1,16]{2,0,1:T(8,128)S(1)}, u32[]{:S(2)}, u32[]{:S(2)}) collective-permute-start(f32[8,1,16]{2,0,1:T(8,128)S(1)} %get-tuple-element.140), channel_id=1, source_target_pairs={{0,4},{1,5},{2,6},{3,7},{8,12},{9,13},{10,14},{11,15},{16,20},{17,... | collective-permute-start | bytes 1544 | tf_op jit(solution)/shard_map/ppermute | solution.py:22
  203.3 5.5 %collective-permute-start.49 = (f32[8,1,16]{2,0,1:T(8,128)S(1)}, f32[8,1,16]{2,0,1:T(8,128)S(1)}, u32[]{:S(2)}, u32[]{:S(2)}) collective-permute-start(f32[8,1,16]{2,0,1:T(8,128)S(1)} %get-tuple-element.139), channel_id=1, source_target_pairs={{4,0},{5,1},{6,2},{7,3},{12,8},{13,9},{14,10},{15,11},{20,16},{21,... | collective-permute-start | bytes 1544 | tf_op jit(solution)/shard_map/ppermute | solution.py:24
  206.0 6.3 %collective-permute-start.43 = (f32[16,6,1]{2,0,1:T(8,128)S(1)}, f32[16,6,1]{2,0,1:T(8,128)S(1)}, u32[]{:S(2)}, u32[]{:S(2)}) collective-permute-start(f32[16,6,1]{2,0,1:T(8,128)S(1)} %get-tuple-element.84), channel_id=1, source_target_pairs={{1,0},{2,1},{3,2},{5,4},{6,5},{7,6},{9,8},{10,9},{11,10},{13,12},{... | collective-permute-start | bytes 1160 | tf_op jit(solution)/shard_map/ppermute | solution.py:24
  212.5 11.6 %collective-permute-start.44 = (f32[16,1,32]{2,0,1:T(8,128)S(1)}, f32[16,1,32]{2,0,1:T(8,128)S(1)}, u32[]{:S(2)}, u32[]{:S(2)}) collective-permute-start(f32[16,1,32]{2,0,1:T(8,128)S(1)} %get-tuple-element.106), channel_id=1, source_target_pairs={{0,4},{1,5},{2,6},{3,7},{8,12},{9,13},{10,14},{11,15},{16,20},{17,... | collective-permute-start | bytes 6152 | tf_op jit(solution)/shard_map/ppermute | solution.py:22
  217.1 7.1 %collective-permute-start.45 = (f32[16,1,32]{2,0,1:T(8,128)S(1)}, f32[16,1,32]{2,0,1:T(8,128)S(1)}, u32[]{:S(2)}, u32[]{:S(2)}) collective-permute-start(f32[16,1,32]{2,0,1:T(8,128)S(1)} %get-tuple-element.107), channel_id=1, source_target_pairs={{4,0},{5,1},{6,2},{7,3},{12,8},{13,9},{14,10},{15,11},{20,16},{21,... | collective-permute-start | bytes 6152 | tf_op jit(solution)/shard_map/ppermute | solution.py:24
  218.4 10.3 %collective-permute-start.50 = (f32[8,4,1]{2,0,1:T(8,128)S(1)}, f32[8,4,1]{2,0,1:T(8,128)S(1)}, u32[]{:S(2)}, u32[]{:S(2)}) collective-permute-start(f32[8,4,1]{2,0,1:T(8,128)S(1)} %get-tuple-element.126), channel_id=1, source_target_pairs={{0,1},{1,2},{2,3},{4,5},{5,6},{6,7},{8,9},{9,10},{10,11},{12,13},{... | collective-permute-start | bytes 392 | tf_op jit(solution)/shard_map/ppermute | solution.py:22
  222.8 5.9 %collective-permute-start.51 = (f32[8,4,1]{2,0,1:T(8,128)S(1)}, f32[8,4,1]{2,0,1:T(8,128)S(1)}, u32[]{:S(2)}, u32[]{:S(2)}) collective-permute-start(f32[8,4,1]{2,0,1:T(8,128)S(1)} %get-tuple-element.127), channel_id=1, source_target_pairs={{1,0},{2,1},{3,2},{5,4},{6,5},{7,6},{9,8},{10,9},{11,10},{13,12},{... | collective-permute-start | bytes 392 | tf_op jit(solution)/shard_map/ppermute | solution.py:24
  232.2 16.8 %collective-permute-start.52 = (f32[8,1,16]{2,0,1:T(8,128)S(1)}, f32[8,1,16]{2,0,1:T(8,128)S(1)}, u32[]{:S(2)}, u32[]{:S(2)}) collective-permute-start(f32[8,1,16]{2,0,1:T(8,128)S(1)} %get-tuple-element.137), channel_id=1, source_target_pairs={{0,4},{1,5},{2,6},{3,7},{8,12},{9,13},{10,14},{11,15},{16,20},{17,... | collective-permute-start | bytes 1544 | tf_op jit(solution)/shard_map/ppermute | solution.py:22
  236.7 12.3 %collective-permute-start.53 = (f32[8,1,16]{2,0,1:T(8,128)S(1)}, f32[8,1,16]{2,0,1:T(8,128)S(1)}, u32[]{:S(2)}, u32[]{:S(2)}) collective-permute-start(f32[8,1,16]{2,0,1:T(8,128)S(1)} %get-tuple-element.138), channel_id=1, source_target_pairs={{4,0},{5,1},{6,2},{7,3},{12,8},{13,9},{14,10},{15,11},{20,16},{21,... | collective-permute-start | bytes 1544 | tf_op jit(solution)/shard_map/ppermute | solution.py:24
  258.5 5.5 %collective-permute-start.57 = (f32[8,1,16]{2,0,1:T(8,128)S(1)}, f32[8,1,16]{2,0,1:T(8,128)S(1)}, u32[]{:S(2)}, u32[]{:S(2)}) collective-permute-start(f32[8,1,16]{2,0,1:T(8,128)S(1)} %get-tuple-element.136), channel_id=1, source_target_pairs={{4,0},{5,1},{6,2},{7,3},{12,8},{13,9},{14,10},{15,11},{20,16},{21,... | collective-permute-start | bytes 1544 | tf_op jit(solution)/shard_map/ppermute | solution.py:24
  284.5 5.5 %collective-permute-start.61 = (f32[8,1,16]{2,0,1:T(8,128)S(1)}, f32[8,1,16]{2,0,1:T(8,128)S(1)}, u32[]{:S(2)}, u32[]{:S(2)}) collective-permute-start(f32[8,1,16]{2,0,1:T(8,128)S(1)} %get-tuple-element.131), channel_id=1, source_target_pairs={{4,0},{5,1},{6,2},{7,3},{12,8},{13,9},{14,10},{15,11},{20,16},{21,... | collective-permute-start | bytes 1544 | tf_op jit(solution)/shard_map/ppermute | solution.py:24
  291.4 5.4 %collective-permute-start.63 = (f32[8,4,1]{2,0,1:T(8,128)S(1)}, f32[8,4,1]{2,0,1:T(8,128)S(1)}, u32[]{:S(2)}, u32[]{:S(2)}) collective-permute-start(f32[8,4,1]{2,0,1:T(8,128)S(1)} %get-tuple-element.121), channel_id=1, source_target_pairs={{1,0},{2,1},{3,2},{5,4},{6,5},{7,6},{9,8},{10,9},{11,10},{13,12},{... | collective-permute-start | bytes 392 | tf_op jit(solution)/shard_map/ppermute | solution.py:24
  298.6 5.5 %collective-permute-start.65 = (f32[8,1,16]{2,0,1:T(8,128)S(1)}, f32[8,1,16]{2,0,1:T(8,128)S(1)}, u32[]{:S(2)}, u32[]{:S(2)}) collective-permute-start(f32[8,1,16]{2,0,1:T(8,128)S(1)} %get-tuple-element.129), channel_id=1, source_target_pairs={{4,0},{5,1},{6,2},{7,3},{12,8},{13,9},{14,10},{15,11},{20,16},{21,... | collective-permute-start | bytes 1544 | tf_op jit(solution)/shard_map/ppermute | solution.py:24
  313.4 5.5 %collective-permute-start.69 = (f32[16,1,32]{2,0,1:T(8,128)S(1)}, f32[16,1,32]{2,0,1:T(8,128)S(1)}, u32[]{:S(2)}, u32[]{:S(2)}) collective-permute-start(f32[16,1,32]{2,0,1:T(8,128)S(1)} %get-tuple-element.105), channel_id=1, source_target_pairs={{4,0},{5,1},{6,2},{7,3},{12,8},{13,9},{14,10},{15,11},{20,16},{21,... | collective-permute-start | bytes 6152 | tf_op jit(solution)/shard_map/ppermute | solution.py:24
  328.0 5.5 %collective-permute-start.73 = (f32[16,1,32]{2,0,1:T(8,128)S(1)}, f32[16,1,32]{2,0,1:T(8,128)S(1)}, u32[]{:S(2)}, u32[]{:S(2)}) collective-permute-start(f32[16,1,32]{2,0,1:T(8,128)S(1)} %get-tuple-element.102), channel_id=1, source_target_pairs={{4,0},{5,1},{6,2},{7,3},{12,8},{13,9},{14,10},{15,11},{20,16},{21,... | collective-permute-start | bytes 6152 | tf_op jit(solution)/shard_map/ppermute | solution.py:24
  333.6 5.2 %collective-permute-start.75 = (f32[16,6,1]{2,0,1:T(8,128)S(1)}, f32[16,6,1]{2,0,1:T(8,128)S(1)}, u32[]{:S(2)}, u32[]{:S(2)}) collective-permute-start(f32[16,6,1]{2,0,1:T(8,128)S(1)} %get-tuple-element.78), channel_id=1, source_target_pairs={{1,0},{2,1},{3,2},{5,4},{6,5},{7,6},{9,8},{10,9},{11,10},{13,12},{... | collective-permute-start | bytes 1160 | tf_op jit(solution)/shard_map/ppermute | solution.py:24
  342.7 5.5 %collective-permute-start.77 = (f32[1,8,64]{2,1,0:T(8,128)S(1)}, f32[1,8,64]{2,1,0:T(8,128)S(1)}, u32[]{:S(2)}, u32[]{:S(2)}) collective-permute-start(f32[1,8,64]{2,1,0:T(8,128)S(1)} %get-tuple-element.100), channel_id=1, source_target_pairs={{8,0},{16,8},{24,16},{9,1},{17,9},{25,17},{10,2},{18,10},{26,18},{... | collective-permute-start | bytes 6152 | tf_op jit(solution)/shard_map/ppermute | solution.py:24
  350.2 5.5 %collective-permute-start.79 = (f32[10,1,64]{2,1,0:T(1,128)S(1)}, f32[10,1,64]{2,1,0:T(1,128)S(1)}, u32[]{:S(2)}, u32[]{:S(2)}) collective-permute-start(f32[10,1,64]{2,1,0:T(1,128)S(1)} %get-tuple-element.90), channel_id=1, source_target_pairs={{4,0},{5,1},{6,2},{7,3},{12,8},{13,9},{14,10},{15,11},{20,16},{21,... | collective-permute-start | bytes 7688 | tf_op jit(solution)/shard_map/ppermute | solution.py:24
  357.1 7.7 %collective-permute-start.81 = (f32[10,10,1]{2,1,0:T(8,128)S(1)}, f32[10,10,1]{2,1,0:T(8,128)S(1)}, u32[]{:S(2)}, u32[]{:S(2)}) collective-permute-start(f32[10,10,1]{2,1,0:T(8,128)S(1)} %get-tuple-element.70), channel_id=1, source_target_pairs={{1,0},{2,1},{3,2},{5,4},{6,5},{7,6},{9,8},{10,9},{11,10},{13,12},{... | collective-permute-start | bytes 1208 | tf_op jit(solution)/shard_map/ppermute | solution.py:24
  367.9 5.5 %collective-permute-start.83 = (f32[1,8,64]{2,1,0:T(8,128)S(1)}, f32[1,8,64]{2,1,0:T(8,128)S(1)}, u32[]{:S(2)}, u32[]{:S(2)}) collective-permute-start(f32[1,8,64]{2,1,0:T(8,128)S(1)} %get-tuple-element.98), channel_id=1, source_target_pairs={{8,0},{16,8},{24,16},{9,1},{17,9},{25,17},{10,2},{18,10},{26,18},{... | collective-permute-start | bytes 6152 | tf_op jit(solution)/shard_map/ppermute | solution.py:24
  375.1 5.5 %collective-permute-start.85 = (f32[10,1,64]{2,1,0:T(1,128)S(1)}, f32[10,1,64]{2,1,0:T(1,128)S(1)}, u32[]{:S(2)}, u32[]{:S(2)}) collective-permute-start(f32[10,1,64]{2,1,0:T(1,128)S(1)} %get-tuple-element.88), channel_id=1, source_target_pairs={{4,0},{5,1},{6,2},{7,3},{12,8},{13,9},{14,10},{15,11},{20,16},{21,... | collective-permute-start | bytes 7688 | tf_op jit(solution)/shard_map/ppermute | solution.py:24
  383.0 5.4 %collective-permute-start.87 = (f32[10,10,1]{2,1,0:T(8,128)S(1)}, f32[10,10,1]{2,1,0:T(8,128)S(1)}, u32[]{:S(2)}, u32[]{:S(2)}) collective-permute-start(f32[10,10,1]{2,1,0:T(8,128)S(1)} %get-tuple-element.68), channel_id=1, source_target_pairs={{1,0},{2,1},{3,2},{5,4},{6,5},{7,6},{9,8},{10,9},{11,10},{13,12},{... | collective-permute-start | bytes 1208 | tf_op jit(solution)/shard_map/ppermute | solution.py:24
  403.1 5.5 %collective-permute-start.89 = (f32[1,16,128]{2,1,0:T(8,128)S(1)}, f32[1,16,128]{2,1,0:T(8,128)S(1)}, u32[]{:S(2)}, u32[]{:S(2)}) collective-permute-start(f32[1,16,128]{2,1,0:T(8,128)S(1)} %get-tuple-element.60), channel_id=1, source_target_pairs={{8,0},{16,8},{24,16},{9,1},{17,9},{25,17},{10,2},{18,10},{26,18},{... | collective-permute-start | bytes 24584 | tf_op jit(solution)/shard_map/ppermute | solution.py:24
  410.3 5.6 %collective-permute-start.91 = (f32[18,1,128]{2,1,0:T(1,128)S(1)}, f32[18,1,128]{2,1,0:T(1,128)S(1)}, u32[]{:S(2)}, u32[]{:S(2)}) collective-permute-start(f32[18,1,128]{2,1,0:T(1,128)S(1)} %get-tuple-element.50), channel_id=1, source_target_pairs={{4,0},{5,1},{6,2},{7,3},{12,8},{13,9},{14,10},{15,11},{20,16},{21,... | collective-permute-start | bytes 27656 | tf_op jit(solution)/shard_map/ppermute | solution.py:24
  418.2 5.7 %collective-permute-start.93 = (f32[18,18,1]{2,1,0:T(8,128)S(1)}, f32[18,18,1]{2,1,0:T(8,128)S(1)}, u32[]{:S(2)}, u32[]{:S(2)}) collective-permute-start(f32[18,18,1]{2,1,0:T(8,128)S(1)} %get-tuple-element.40), channel_id=1, source_target_pairs={{1,0},{2,1},{3,2},{5,4},{6,5},{7,6},{9,8},{10,9},{11,10},{13,12},{... | collective-permute-start | bytes 3896 | tf_op jit(solution)/shard_map/ppermute | solution.py:24
  426.0 5.5 %collective-permute-start.95 = (f32[1,16,128]{2,1,0:T(8,128)S(1)}, f32[1,16,128]{2,1,0:T(8,128)S(1)}, u32[]{:S(2)}, u32[]{:S(2)}) collective-permute-start(f32[1,16,128]{2,1,0:T(8,128)S(1)} %get-tuple-element.58), channel_id=1, source_target_pairs={{8,0},{16,8},{24,16},{9,1},{17,9},{25,17},{10,2},{18,10},{26,18},{... | collective-permute-start | bytes 24584 | tf_op jit(solution)/shard_map/ppermute | solution.py:24
  433.3 5.6 %collective-permute-start.97 = (f32[18,1,128]{2,1,0:T(1,128)S(1)}, f32[18,1,128]{2,1,0:T(1,128)S(1)}, u32[]{:S(2)}, u32[]{:S(2)}) collective-permute-start(f32[18,1,128]{2,1,0:T(1,128)S(1)} %get-tuple-element.48), channel_id=1, source_target_pairs={{4,0},{5,1},{6,2},{7,3},{12,8},{13,9},{14,10},{15,11},{20,16},{21,... | collective-permute-start | bytes 27656 | tf_op jit(solution)/shard_map/ppermute | solution.py:24
  442.4 5.6 %collective-permute-start.99 = (f32[18,18,1]{2,1,0:T(8,128)S(1)}, f32[18,18,1]{2,1,0:T(8,128)S(1)}, u32[]{:S(2)}, u32[]{:S(2)}) collective-permute-start(f32[18,18,1]{2,1,0:T(8,128)S(1)} %get-tuple-element.38), channel_id=1, source_target_pairs={{1,0},{2,1},{3,2},{5,4},{6,5},{7,6},{9,8},{10,9},{11,10},{13,12},{... | collective-permute-start | bytes 3896 | tf_op jit(solution)/shard_map/ppermute | solution.py:24
  (38 other events, 178.8 us)
where the time goes:
time: 456 us; the launch traced here: 449 us
  starting transfers between devices  214 us (47%)
  waiting for transfers between devices  130 us (29%)
  blocking collectives  48.1 us (11%)
  local copies, waits for them, and re-layouts  39.4 us (9%)
  other arithmetic  15.4 us (3%)
    ppermute x50, starting transfers between devices, extended(): lax.ppermute(tail, axis, [(i, (i + 1) % count) for i in range(ends)])  149 us
    ppermute x50, waiting for transfers between devices, extended(): lax.ppermute(head, axis, [((i + 1) % count, i) for i in range(ends)])  129 us
    ppermute x50, starting transfers between devices, extended(): lax.ppermute(head, axis, [((i + 1) % count, i) for i in range(ends)])  64.9 us
    all_gather x2, blocking collectives, collect(): return lax.all_gather(members, 'grp', axis=0, tiled=True)  27.6 us
    reshape x5, local copies, waits for them, and re-layouts, restrict(): values.reshape(values.shape[0] // 2, 2, values.shape[1] // 2, 2, values.s...  22 us
    all_gather x1, blocking collectives, collect(): lax.all_gather(members[1][None], ('gy', 'gx'), axis=0, tiled=True)  10.7 us
    all_gather x1, blocking collectives, collect(): lax.all_gather(members[0][None], ('gy', 'gx'), axis=0, tiled=True)  9.83 us
    reduce_sum x13, other arithmetic, restrict(): return jnp.mean(shaped, axis=(1, 3, 5))  9.14 us
  transfers between devices with their start and end apart: 100, of which 36 were waited for; matrix products, arithmetic and copies ran while one was open for 7% of the time, Pallas kernels for 0%

commit v1 on v0

v1 whole, which is shorter than its diff:
```python
import jax
import jax.numpy as jnp
import numpy as np
from jax import lax
from jax.experimental import pallas as pl
from jax.experimental.pallas import tpu as pltpu
from jax.sharding import PartitionSpec as P

LEVELS = 5
COARSE = 8
AXES = ("grp", "gy", "gx")
F32 = jnp.float32

HALO = 3
ZW = 4 + 2 * HALO
XW = 32 + 2 * HALO
LW = 384
EDGE = 4 * HALO
M_DEEP, M_FAR, R_DEEP, R_FAR = 11, 4, 10, 3
M_EDGE, R_EDGE = 11, 10


def lane_iota(rows=8):
    return lax.broadcasted_iota(jnp.int32, (rows, 128), 1)


def gather(source, index):
    return jnp.take_along_axis(source, index, axis=1, mode="promise_in_bounds")


def spread(source, offset, px):
    rows = source.shape[0]
    return gather(source, (4 * lane_iota(rows) + (px - 4 * offset)) & 127)


def between(low, high, rows=8):
    lane = lane_iota(rows)
    return (lane >= low) & (lane < high)


def table(rows):
    return jnp.asarray(np.repeat(np.stack(rows)[:, None, :], 8, axis=1).astype(np.int32))


def edge_send_rows():
    row = np.zeros(128, np.int64)
    base = 0
    for a, width in ((1, M_EDGE), (0, R_EDGE)):
        for side in (0, 1):
            first = EDGE - width if side == 0 else 0
            for z in range(HALO):
                for k in range(width):
                    row[base] = a * 48 + z * 12 + first + k + (1000 if side else 0)
                    base += 1
    return [row]


def edge_own_rows():
    rows = []
    for side, tiles in ((0, (0, 1)), (1, (1, 2))):
        for tile in tiles:
            row = np.full(128, -1, np.int64)
            for lane in range(128):
                z, x = divmod(128 * tile + lane, XW)
                x = x if side == 0 else x - (XW - HALO)
                if HALO <= z < HALO + 4 and 0 <= x < HALO:
                    row[lane] = (z - HALO) * 12 + 4 * x
            rows.append(row)
    return rows


def edge_far_rows():
    rows = []
    base_of = {(1, 0): 0, (1, 1): 33, (0, 0): 66, (0, 1): 96}
    for tile, first in ((0, 0), (2, HALO + 4)):
        for a, width in ((0, R_EDGE), (1, M_EDGE)):
            row = np.full(128, -1000, np.int64)
            for lane in range(128):
                z, x = divmod(128 * tile + lane, XW)
                if not first <= z < first + HALO:
                    continue
                for side in (0, 1):
                    k = 4 * x if side == 0 else 4 * (x - (XW - HALO))
                    if 0 <= k < EDGE:
                        start = base_of[a, side] + (z - first) * width
                        row[lane] = start + k - (EDGE - width if side == 0 else 0)
            rows.append(row)
    return rows


def coordinate_rows(rows):
    cells = np.arange(LW)
    z, x = cells // XW, cells % XW
    z = np.where(cells < ZW * XW, z, -1000000)
    both = np.stack([z, x])[:, None, :]
    return jnp.asarray(np.repeat(both, rows, axis=1).astype(np.int32))


class Plan:
    def __init__(self, mesh):
        self.counts = tuple(mesh.shape[axis] for axis in AXES)
        self.near = 1 if self.counts[1] == 2 else 2
        self.rows = 16 * (1 + self.near)
        self.cells = self.rows // 4
        self.tile = -(-self.cells // 8) * 8
        self.z_rows = 16 + 8 * self.near
        sizes = [
            M_DEEP * self.z_rows,
            M_FAR * 8 * self.near,
            R_DEEP * self.z_rows,
            R_FAR * 8 * self.near,
            4 * self.rows,
        ]
        self.starts = [sum(sizes[:i]) for i in range(len(sizes))]
        self.payload = sum(sizes)
        self.devices = self.counts[0] * self.counts[1] * self.counts[2]
        self.coarse = (4 * self.counts[0], 4 * self.counts[1], 32 * self.counts[2])

    def pairs(self, swaps):
        out = []
        for index in np.ndindex(*self.counts):
            there = []
            for axis, swap in enumerate(swaps):
                i, n = index[axis], self.counts[axis]
                j = i if swap is None else (i + 1 if i % 2 == swap else i - 1)
                if axis == 2:
                    j = j % n
                there.append(j)
            if all(0 <= j < n for j, n in zip(there, self.counts)):
                out.append(
                    (
                        int(np.ravel_multi_index(index, self.counts)),
                        int(np.ravel_multi_index(there, self.counts)),
                    )
                )
        return out

    def y_places(self):
        iy = lax.axis_index("gy")
        if self.near == 1:
            return 16 * iy, [(1 - iy, 16 * (1 - iy))]
        odd = lax.rem(iy, 2)
        return 16, [(1 - odd, 32 * (1 - odd)), (odd, 32 * odd)]


def is_even(axis):
    return lax.rem(lax.axis_index(axis), 2) == 0


def at(start, size):
    if isinstance(start, int):
        return pl.ds(start, size)
    return pl.ds(pl.multiple_of(start, 8), size)


def edges_kernel(r_ref, m_ref, even_ref, odd_ref):
    even = is_even("gx")
    for pz in range(4):
        for half in range(2):
            to_right = jnp.zeros((8, 128), F32)
            to_left = jnp.zeros((8, 128), F32)
            for a, ref in enumerate((r_ref, m_ref)):
                for z in range(4):
                    cells = ref[4 * z + pz, 8 * half : 8 * half + 8, :]
                    base = a * 48 + z * 12
                    here = between(base, base + EDGE)
                    shift = (base - (128 - EDGE)) % 128
                    to_right = jnp.where(here, pltpu.roll(cells, shift, 1), to_right)
                    to_left = jnp.where(here, pltpu.roll(cells, base, 1), to_left)
            rows = slice(8 * half, 8 * half + 8)
            even_ref[pz, rows, :] = jnp.where(even, to_right, to_left)
            odd_ref[pz, rows, :] = jnp.where(even, to_left, to_right)


def z_pack_kernel(plan, *refs):
    near = plan.near
    tab_ref, r_ref, m_ref = refs[:3]
    beside = [refs[3 + 2 * i : 5 + 2 * i] for i in range(near)]
    edges = [refs[3 + 2 * near + 2 * i : 5 + 2 * near + 2 * i] for i in range(1 + near)]
    outs = refs[-2:]
    own_row, places = plan.y_places()
    x_even = is_even("gx")
    z_even = is_even("grp")
    index = tab_ref[0]
    for swap, out in enumerate(outs):
        top = z_even if swap == 0 else jnp.logical_not(z_even)
        for a, ref, deep, far, start, far_start in (
            (1, m_ref, M_DEEP, M_FAR, plan.starts[0], plan.starts[1]),
            (0, r_ref, R_DEEP, R_FAR, plan.starts[2], plan.starts[3]),
        ):
            for d in range(1, deep + 1):
                plane = jnp.where(top, 16 - d, d - 1)
                row = start + (d - 1) * plan.z_rows
                out[row : row + 16, :] = ref[plane]
                for i, (side, _) in enumerate(places):
                    to = row + 16 + 8 * i
                    out[to : to + 8, :] = beside[i][a][plane, at(8 * (1 - side), 8), :]
                    if d <= far:
                        to = far_start + ((d - 1) * near + i) * 8
                        out[to : to + 8, :] = beside[i][a][plane, at(8 * side, 8), :]
        first = jnp.where(top, 12, 0)
        use_right = index >= 1000
        lanes = jnp.where(use_right, index - 1000, index) + first
        for i in range(1 + near):
            base = own_row if i == 0 else places[i - 1][1]
            even_ref, odd_ref = edges[i]
            for pz in range(4):
                for half in range(2):
                    rows = slice(8 * half, 8 * half + 8)
                    even, odd = even_ref[pz, rows, :], odd_ref[pz, rows, :]
                    left = gather(jnp.where(x_even, odd, even), lanes)
                    right = gather(jnp.where(x_even, even, odd), lanes)
                    to = at(plan.starts[4] + pz * plan.rows + base + 8 * half, 8)
                    out[to, :] = jnp.where(use_right, right, left)


def padded_rows(plan, cells):
    if plan.cells == plan.tile:
        return cells
    return jnp.concatenate(
        [cells, jnp.zeros((plan.tile - plan.cells, cells.shape[1]), F32)], axis=0
    )


def every_fourth(plan, ref, lead, py):
    return padded_rows(plan, ref[(*lead, pl.ds(py, plan.cells, 4), slice(None))])


def own_kernel(plan, *refs):
    near = plan.near
    tab_ref, r_ref, m_ref = refs[:3]
    beside = [refs[3 + 2 * i : 5 + 2 * i] for i in range(near)]
    edges = [refs[3 + 2 * near + 2 * i : 5 + 2 * near + 2 * i] for i in range(1 + near)]
    out, planes, sides = refs[-3:]
    tile = plan.tile
    own_row, places = plan.y_places()
    x_even = is_even("gx")
    blocks = [(own_row, (r_ref, m_ref))] + [(place[1], b) for place, b in zip(places, beside)]
    for i, (base, pair) in enumerate(blocks):
        for a in range(2):
            planes[a, :, at(base, 16), :] = pair[a][...]
        even, odd = edges[i][0][...], edges[i][1][...]
        sides[0, :, at(base, 16), :] = jnp.where(x_even, odd, even)
        sides[1, :, at(base, 16), :] = jnp.where(x_even, even, odd)

    def body(pz, carry):
        for a in range(2):
            for py in range(4):
                cells = [every_fourth(plan, planes, (a, 4 * z + pz), py) for z in range(4)]
                side = [every_fourth(plan, sides, (s, pz), py) for s in range(2)]
                for px in range(4):
                    for t in range(3):
                        value = jnp.zeros((tile, 128), F32)
                        for z in range(4):
                            offset = (z + HALO) * XW + HALO - 128 * t
                            low, high = max(offset, 0), min(offset + 32, 128)
                            if low < high:
                                value = jnp.where(
                                    between(low, high, tile),
                                    spread(cells[z], offset % 32, px),
                                    value,
                                )
                        for s in range(2):
                            if t - s in (0, 1):
                                index = tab_ref[2 * s + t - s]
                                index = jnp.concatenate([index] * (tile // 8), axis=0)
                                lanes = jnp.maximum(index, 0) + (48 * a + px)
                                value = jnp.where(index >= 0, gather(side[s], lanes), value)
                        out[a, pz, py, px, :, 128 * t : 128 * t + 128] = value
        return carry

    lax.fori_loop(0, 4, body, 0)


def inside_mask(plan, coord_ref):
    tile = plan.tile
    z = coord_ref[0] + (4 * lax.axis_index("grp") - HALO)
    x = coord_ref[1] + (32 * lax.axis_index("gx") - HALO)
    mask = (z >= 0) & (z < plan.coarse[0]) & (x >= 0) & (x < plan.coarse[2])
    if plan.near == 2:
        row = lax.broadcasted_iota(jnp.int32, (tile, LW), 0)
        y = row + (4 * lax.axis_index("gy") - 4)
        mask = mask & (row < plan.cells) & (y >= 0) & (y < plan.coarse[1])
    return mask


def roll_lanes(value, shift):
    return pltpu.roll(value, shift % LW, 1)


def fill_rim(plan, ref, n):
    tile = plan.tile
    row = lax.broadcasted_iota(jnp.int32, (tile, LW), 0)

    def body(i, carry):
        for j in range(n):
            ref[0, i + 1, j + 1] = roll_lanes(ref[n, i + 1, j + 1], XW)
            ref[n + 1, i + 1, j + 1] = roll_lanes(ref[1, i + 1, j + 1], -XW)
            up = pltpu.roll(ref[i + 1, n, j + 1], 1, 0)
            down = pltpu.roll(ref[i + 1, 1, j + 1], tile - 1, 0)
            ref[i + 1, 0, j + 1] = jnp.where(row == 0, 0.0, up)
            ref[i + 1, n + 1, j + 1] = jnp.where(row == tile - 1, 0.0, down)
            ref[i + 1, j + 1, 0] = roll_lanes(ref[i + 1, j + 1, n], 1)
            ref[i + 1, j + 1, n + 1] = roll_lanes(ref[i + 1, j + 1, 1], -1)
        return carry

    lax.fori_loop(0, n, body, 0)


def around(ref, a, b, c):
    return (
        ref[a, b + 1, c + 1],
        ref[a + 2, b + 1, c + 1],
        ref[a + 1, b, c + 1],
        ref[a + 1, b + 2, c + 1],
        ref[a + 1, b + 1, c],
        ref[a + 1, b + 1, c + 2],
    )


def pull(m_ref, v_ref, h_ref, a, b, c):
    cells = around(v_ref, a, b, c)
    mobility = around(m_ref, a, b, c)
    total = ((cells[0] + cells[1]) + (cells[2] + cells[3])) + (cells[4] + cells[5])
    products = [m * v for m, v in zip(mobility, cells)]
    other = ((products[0] + products[1]) + (products[2] + products[3])) + (
        products[4] + products[5]
    )
    return h_ref[a, b, c] * (m_ref[a + 1, b + 1, c + 1] * total + other)


def over_pairs(n, step):
    def body(i, carry):
        step(lax.div(i, n), lax.rem(i, n))
        return carry

    lax.fori_loop(0, n * n, body, 0)


def descend(plan, n, factor, inside, m_ref, r_ref, v_ref, w_ref, d_ref, h_ref, e_ref, k_ref):
    fill_rim(plan, m_ref, n)

    def first(a, b):
        for c in range(n):
            s = around(m_ref, a, b, c)
            d = 3.0 * m_ref[a + 1, b + 1, c + 1] + 0.5 * (
                ((s[0] + s[1]) + (s[2] + s[3])) + (s[4] + s[5])
            )
            h = jnp.where(inside, 0.4 / d, 0.0)
            e = (2.0 / factor) * h * r_ref[a, b, c]
            d_ref[a, b, c] = d
            h_ref[a, b, c] = h
            e_ref[a, b, c] = e
            v_ref[a + 1, b + 1, c + 1] = e

    over_pairs(n, first)
    fill_rim(plan, v_ref, n)

    def second(a, b):
        for c in range(n):
            value = 1.2 * e_ref[a, b, c] + pull(m_ref, v_ref, h_ref, a, b, c)
            w_ref[a + 1, b + 1, c + 1] = value
            k_ref[a, b, c] = value

    over_pairs(n, second)
    fill_rim(plan, w_ref, n)


def leftover(factor, m_ref, r_ref, w_ref, d_ref, h_ref, a, b, c):
    away = w_ref[a + 1, b + 1, c + 1] - 1.25 * pull(m_ref, w_ref, h_ref, a, b, c)
    return r_ref[a, b, c] - factor * (d_ref[a, b, c] * away)


def down_kernel(plan, *refs):
    (tab_ref, coord_ref, own_ref, even_ref, odd_ref) = refs[:5]
    chunk, m0_out, h0, e0, k0, m1_out, h1, e1, k1 = refs[5:14]
    m0, r0, v0, w0, d0, m1, r1, v1, w1, d1, planes, sides = refs[14:]
    near, tile = plan.near, plan.tile
    own_row, places = plan.y_places()
    z_even = is_even("grp")
    inside = inside_mask(plan, coord_ref)

    for side in range(2):
        use_even = jnp.logical_not(z_even) if side == 0 else z_even

        def read(rows):
            return jnp.where(use_even, even_ref[rows, :], odd_ref[rows, :])

        for a, deep, far, start, far_start in (
            (1, M_DEEP, M_FAR, plan.starts[0], plan.starts[1]),
            (0, R_DEEP, R_FAR, plan.starts[2], plan.starts[3]),
        ):
            for d in range(1, EDGE + 1):
                plane = EDGE - d if side == 0 else d - 1
                if d > far:
                    planes[side, a, plane] = jnp.zeros((plan.rows, 128), F32)
                if d > deep:
                    continue
                row = start + (d - 1) * plan.z_rows
                planes[side, a, plane, at(own_row, 16), :] = read(slice(row, row + 16))
                for i, (y_side, base) in enumerate(places):
                    row_i = row + 16 + 8 * i
                    planes[side, a, plane, at(base + 8 * (1 - y_side), 8), :] = read(
                        slice(row_i, row_i + 8)
                    )
                    if d <= far:
                        row_i = far_start + ((d - 1) * near + i) * 8
                        planes[side, a, plane, at(base + 8 * y_side, 8), :] = read(
                            slice(row_i, row_i + 8)
                        )
        for pz in range(4):
            row = plan.starts[4] + pz * plan.rows
            sides[side, pz] = read(slice(row, row + plan.rows))

    def place(pz, carry):
        for a in range(2):
            for py in range(4):
                for side, t in ((0, 0), (1, 2)):
                    cells = [
                        every_fourth(plan, planes, (side, a, 4 * z + pz), py)
                        for z in range(HALO)
                    ]
                    edge = every_fourth(plan, sides, (side, pz), py)
                    index = tab_ref[2 * side + a]
                    index = jnp.concatenate([index] * (tile // 8), axis=0)
                    lanes = slice(128 * t, 128 * t + 128)
                    for px in range(4):
                        value = own_ref[a, pz, py, px, :, lanes]
                        for z in range(HALO):
                            offset = (z if side == 0 else z + HALO + 4) * XW + HALO - 128 * t
                            value = jnp.where(
                                between(offset, offset + 32, tile),
                                spread(cells[z], offset % 32, px),
                                value,
                            )
                        from_edge = jnp.clip(index + px, 0, 127)
                        value = jnp.where(index > -100, gather(edge, from_edge), value)
                        value = jnp.where(inside[:, lanes], value, 0.0)
                        if a == 1:
                            m0[pz + 1, py + 1, px + 1, :, lanes] = value
                            m0_out[pz, py, px, :, lanes] = value
                        else:
                            r0[pz, py, px, :, lanes] = value
                for px in range(4):
                    lanes = slice(128, 256)
                    value = jnp.where(inside[:, lanes], own_ref[a, pz, py, px, :, lanes], 0.0)
                    if a == 1:
                        m0[pz + 1, py + 1, px + 1, :, lanes] = value
                        m0_out[pz, py, px, :, lanes] = value
                    else:
                        r0[pz, py, px, :, lanes] = value
        return carry

    lax.fori_loop(0, 4, place, 0)

    descend(plan, 4, 1.0, inside, m0, r0, v0, w0, d0, h0, e0, k0)

    def restrict(a, b):
        for c in range(2):
            rest = jnp.zeros((tile, LW), F32)
            mobility = jnp.zeros((tile, LW), F32)
            for da in range(2):
                for db in range(2):
                    for dc in range(2):
                        i, j, k = 2 * a + da, 2 * b + db, 2 * c + dc
                        rest = rest + leftover(1.0, m0, r0, w0, d0, h0, i, j, k)
                        mobility = mobility + m0[i + 1, j + 1, k + 1]
            r1[a, b, c] = 0.125 * rest
            m1[a + 1, b + 1, c + 1] = 0.125 * mobility
            m1_out[a, b, c] = 0.125 * mobility

    over_pairs(2, restrict)
    descend(plan, 2, 0.25, inside, m1, r1, v1, w1, d1, h1, e1, k1)
    rest = jnp.zeros((tile, LW), F32)
    mobility = jnp.zeros((tile, LW), F32)
    for a in range(2):
        for b in range(2):
            for c in range(2):
                rest = rest + leftover(0.25, m1, r1, w1, d1, h1, a, b, c)
                mobility = mobility + m1[a + 1, b + 1, c + 1]
    both = []
    for total in (rest, mobility):
        packed = jnp.zeros((tile, 128), F32)
        for t in range(3):
            part = 0.125 * total[:, 128 * t : 128 * t + 128]
            for z in range(4):
                offset = (z + HALO) * XW + HALO - 128 * t
                low, high = max(offset, 0), min(offset + 32, 128)
                if low < high:
                    move = 32 * z - offset
                    packed = jnp.where(
                        between(low + move, high + move, tile),
                        pltpu.roll(part, move % 128, 1),
                        packed,
                    )
        both.append(own_rows(plan, packed))
    block = jnp.concatenate(both, axis=0)

    def put(i, carry):
        chunk[i] = block
        return carry

    lax.fori_loop(0, plan.devices, put, 0, unroll=8)


def own_rows(plan, cells):
    if plan.near == 1:
        return jnp.where(lax.axis_index("gy") == 0, cells[0:4], cells[4:8])
    return cells[4:8]


class Level:
    def __init__(self, plan, level):
        self.size = tuple(n >> (level - 2) for n in plan.coarse)
        self.tile = max(8, self.size[1])
        self.shape = (self.size[0], self.tile, 128)
        self.factor = 0.25**level

    def shifts(self, v):
        z, y, x = self.size
        if z > 1:
            none = jnp.zeros((1, self.tile, 128), F32)
            yield jnp.concatenate([none, v[:-1]], axis=0)
            yield jnp.concatenate([v[1:], none], axis=0)
        else:
            yield jnp.zeros_like(v)
            yield jnp.zeros_like(v)
        row = lax.broadcasted_iota(jnp.int32, self.shape, 1)
        lane = lax.broadcasted_iota(jnp.int32, self.shape, 2)
        up, down = pltpu.roll(v, 1, 1), pltpu.roll(v, self.tile - 1, 1)
        if y == self.tile:
            up = jnp.where(row == 0, 0.0, up)
            down = jnp.where(row == self.tile - 1, 0.0, down)
        yield up
        yield down
        left, right = pltpu.roll(v, 1, 2), pltpu.roll(v, 127, 2)
        if x == 128:
            left = jnp.where(lane == 0, 0.0, left)
            right = jnp.where(lane == 127, 0.0, right)
        yield left
        yield right

    def prepare(self, mobility, source):
        z, y, x = self.size
        row = lax.broadcasted_iota(jnp.int32, self.shape, 1)
        lane = lax.broadcasted_iota(jnp.int32, self.shape, 2)
        inside = (row < y) & (lane < x)
        sums = [mobility + near for near in self.shifts(mobility)]
        self.diagonal = 0.5 * (
            ((sums[0] + sums[1]) + (sums[2] + sums[3])) + (sums[4] + sums[5])
        )
        h = jnp.where(inside, 0.4 / self.diagonal, 0.0)
        self.weights = [h * s for s in sums]
        self.first = (2.0 / self.factor) * h * source
        self.source = source

    def pull(self, v):
        t = [w * near for w, near in zip(self.weights, self.shifts(v))]
        return ((t[0] + t[1]) + (t[2] + t[3])) + (t[4] + t[5])

    def relax(self, v):
        return 0.2 * v + self.first + self.pull(v)

    def leftover(self, v):
        return self.source - self.factor * (self.diagonal * (v - 1.25 * self.pull(v)))


def lanes_2d(values, index):
    flat = values.reshape(-1, 128)
    rows = flat.shape[0]
    lane = lax.broadcasted_iota(jnp.int32, (rows, 128), 1)
    return gather(flat, index(lane)).reshape(values.shape)


def coarsen(values, fine, coarse, fine_ref, coarse_ref):
    z, y, x = coarse.size
    tile = fine.tile
    pairs = values.reshape(z, 2, tile, 128)
    fine_ref[0:z] = pairs[:, 0] + pairs[:, 1]
    rows = fine_ref[0:z, pl.ds(0, y, 2), :] + fine_ref[0:z, pl.ds(1, y, 2), :]
    coarse_ref[0:z, 0:y, :] = rows
    full = coarse_ref[0:z]
    full = full + pltpu.roll(full, 127, 2)
    full = lanes_2d(full, lambda lane: (2 * lane) & 127)
    lane = lax.broadcasted_iota(jnp.int32, full.shape, 2)
    return jnp.where(lane < x, 0.125 * full, 0.0)


def refine(values, fine, coarse, fine_ref):
    z, y, x = coarse.size
    wide = lanes_2d(values, lambda lane: lax.shift_right_logical(lane, 1))
    fine_ref[0:z, pl.ds(0, y, 2), :] = wide[:, 0:y]
    fine_ref[0:z, pl.ds(1, y, 2), :] = wide[:, 0:y]
    rows = fine_ref[0:z]
    return jnp.broadcast_to(rows[:, None], (z, 2, fine.tile, 128)).reshape(fine.shape)


def ascend(plan, n, m_ref, h_ref, e_ref, k_ref, below, v_ref, w_ref, emit):
    def start(a, b):
        for c in range(n):
            v_ref[a + 1, b + 1, c + 1] = k_ref[a, b, c] + below(a, b, c)

    over_pairs(n, start)
    fill_rim(plan, v_ref, n)

    def middle(a, b):
        for c in range(n):
            w_ref[a + 1, b + 1, c + 1] = (
                0.2 * v_ref[a + 1, b + 1, c + 1]
                + e_ref[a, b, c]
                + pull(m_ref, v_ref, h_ref, a, b, c)
            )

    over_pairs(n, middle)
    fill_rim(plan, w_ref, n)

    def last(a, b):
        for c in range(n):
            emit(
                a,
                b,
                c,
                0.2 * w_ref[a + 1, b + 1, c + 1]
                + e_ref[a, b, c]
                + pull(m_ref, w_ref, h_ref, a, b, c),
            )

    over_pairs(n, last)


def up_kernel(plan, *refs):
    coord_ref, joined, m0_in, h0, e0, k0, m1_in, h1, e1, k1, out = refs[:11]
    m0, v0, w0, m1, v1, w1, window = refs[11:18]
    r2, m2, v2 = refs[18:21]
    fine_refs = refs[21:24]
    coarse_refs = refs[24:27]
    tile = plan.tile
    gz, gy, gx = plan.counts
    iz, iy, ix = (lax.axis_index(axis) for axis in AXES)
    inside = inside_mask(plan, coord_ref)

    def unpack(z_block, carry):
        for z in range(4):
            for y_block in range(gy):
                value = jnp.zeros((8, 128), F32)
                for x_block in range(gx):
                    part = joined[(z_block * gy + y_block) * gx + x_block]
                    value = jnp.where(
                        between(32 * x_block, 32 * x_block + 32),
                        pltpu.roll(part, (32 * (x_block - z)) % 128, 1),
                        value,
                    )
                rows = slice(4 * y_block, 4 * y_block + 4)
                r2[4 * z_block + z, rows, :] = value[0:4]
                m2[4 * z_block + z, rows, :] = value[4:8]
        return carry

    lax.fori_loop(0, gz, unpack, 0)
    for ref in (*fine_refs, *coarse_refs):
        ref[...] = jnp.zeros(ref.shape, F32)

    levels = [Level(plan, level) for level in range(2, LEVELS + 1)]
    mobility, source = m2[...], r2[...]
    kept = []
    for i, level in enumerate(levels):
        level.prepare(mobility, source)
        if i < len(levels) - 1:
            e = level.first + level.first * 0.2 + level.pull(level.first)
            kept.append(e)
            args = (level, levels[i + 1], fine_refs[i], coarse_refs[i])
            mobility = coarsen(mobility, *args)
            source = coarsen(level.leftover(e), *args)
    level = levels[-1]
    v = level.first
    for repeat in range(COARSE - 1):
        v = level.relax(v)
    for i in range(len(levels) - 2, -1, -1):
        v = kept[i] + refine(v, levels[i], levels[i + 1], fine_refs[i])
        v = levels[i].relax(levels[i].relax(v))

    v2[...] = jnp.zeros(v2.shape, F32)
    margin = 0 if plan.near == 1 else 8
    v2[pl.ds(HALO, plan.coarse[0]), pl.ds(margin, plan.coarse[1]), :] = v
    planes = []
    for z in range(ZW):
        if plan.near == 1:
            planes.append(v2[4 * iz + z])
        else:
            planes.append(v2[4 * iz + z, pl.ds(4 * iy + 4, tile), :])
    for t in range(3):
        value = jnp.zeros((tile, 128), F32)
        for z in range(ZW):
            offset = z * XW - 128 * t
            low, high = max(offset, 0), min(offset + XW, 128)
            if low < high:
                shift = lax.rem(offset % 128 + HALO - 32 * ix + 256, 128)
                value = jnp.where(
                    between(low, high, tile), pltpu.roll(planes[z], shift, 1), value
                )
        lanes = slice(128 * t, 128 * t + 128)
        window[:, lanes] = jnp.where(inside[:, lanes], value, 0.0)

    def widen(n, source_ref, ref):
        def step(a, b):
            for c in range(n):
                ref[a + 1, b + 1, c + 1] = source_ref[a, b, c]

        over_pairs(n, step)
        fill_rim(plan, ref, n)

    widen(2, m1_in, m1)
    widen(4, m0_in, m0)
    below = window[...]

    def keep(a, b, c, value):
        v1[a + 1, b + 1, c + 1] = value

    ascend(plan, 2, m1, h1, e1, k1, lambda a, b, c: below, v1, w1, keep)

    def from_half(a, b, c):
        return v1[lax.div(a, 2) + 1, lax.div(b, 2) + 1, c // 2 + 1]

    def finish(a, b, c, value):
        v0[a + 1, b + 1, c + 1] = value

    ascend(plan, 4, m0, h0, e0, k0, from_half, v0, w0, finish)

    def store(pz, carry):
        for py in range(4):
            for z in range(4):
                base = (z + HALO) * XW + HALO
                value = jnp.zeros((tile, 128), F32)
                lane = lane_iota(tile)
                for px in range(4):
                    for t in range(3):
                        offset = base - 128 * t
                        low, high = max(offset, 0), min(offset + 32, 128)
                        if low < high:
                            index = (lax.shift_right_logical(lane, 2) + offset) & 127
                            here = (
                                ((lane & 3) == px)
                                & (lane >= 4 * (low - offset))
                                & (lane < 4 * (high - offset))
                            )
                            part = v0[pz + 1, py + 1, px + 1, :, 128 * t : 128 * t + 128]
                            value = jnp.where(here, gather(part, index), value)
                out[4 * z + pz, pl.ds(py, 4, 4), :] = own_rows(plan, value)
        return carry

    lax.fori_loop(0, 4, store, 0)


def call(kernel, outs, scratch, *args):
    return pl.pallas_call(
        kernel,
        out_shape=[jax.ShapeDtypeStruct(shape, F32) for shape in outs],
        scratch_shapes=[pltpu.VMEM(shape, F32) for shape in scratch],
        compiler_params=pltpu.CompilerParams(vmem_limit_bytes=48 * 1024 * 1024),
    )(*args)


def solution(mesh):
    plan = Plan(mesh)
    near, tile = plan.near, plan.tile
    z2, y2, x2 = plan.coarse
    full = (4, 4, 4, tile, LW)
    half = (2, 2, 2, tile, LW)
    full_rim = (6, 6, 6, tile, LW)
    half_rim = (4, 4, 4, tile, LW)
    y_swaps = list(range(near))

    def swap(values, *swaps):
        return lax.ppermute(values, AXES, plan.pairs(swaps))

    def on_device(residual, mobility):
        assert residual.shape == (16, 16, 128)
        beside = []
        for y in y_swaps:
            beside += [swap(residual, None, y, None), swap(mobility, None, y, None)]
        even, odd = call(edges_kernel, [(4, 16, 128)] * 2, [], residual, mobility)
        edges = [swap(even, None, None, 0), swap(odd, None, None, 1)]
        for y in y_swaps:
            edges += [swap(even, None, y, 0), swap(odd, None, y, 1)]
        pieces = (residual, mobility, *beside, *edges)
        sends = call(
            lambda *refs: z_pack_kernel(plan, *refs),
            [(plan.payload, 128)] * 2,
            [],
            table(edge_send_rows()),
            *pieces,
        )
        arrived = [swap(sends[0], 0, None, None), swap(sends[1], 1, None, None)]
        (own,) = call(
            lambda *refs: own_kernel(plan, *refs),
            [(2, *full)],
            [(2, 16, plan.rows, 128), (2, 4, plan.rows, 128)],
            table(edge_own_rows()),
            *pieces,
        )
        coordinates = coordinate_rows(tile)
        chunk, *state = call(
            lambda *refs: down_kernel(plan, *refs),
            [(plan.devices, 8, 128)] + [full] * 4 + [half] * 4,
            [full_rim, full, full_rim, full_rim, full]
            + [half_rim, half, half_rim, half_rim, half]
            + [(2, 2, EDGE, plan.rows, 128), (2, 4, plan.rows, 128)],
            table(edge_far_rows()),
            coordinates,
            own,
            *arrived,
        )
        joined = lax.all_to_all(chunk, AXES, 0, 0, tiled=True)
        levels = [Level(plan, level) for level in range(2, LEVELS + 1)]
        margin = 0 if near == 1 else 16
        (out,) = call(
            lambda *refs: up_kernel(plan, *refs),
            [(16, 16, 128)],
            [full_rim] * 3
            + [half_rim] * 3
            + [(tile, LW)]
            + [(z2, y2, 128)] * 2
            + [(z2 + 2 * HALO, y2 + margin, 128)]
            + [level.shape for level in levels[:-1]]
            + [level.shape for level in levels[1:]],
            coordinates,
            joined,
            *state,
        )
        return out

    spec = P(*AXES)
    return jax.shard_map(
        on_device, mesh=mesh, in_specs=(spec, spec), out_specs=spec, check_vma=False
    )
```

time: 456 us -> 71.2 us (0.16); the launches traced: 449 us -> 70.9 us
  starting transfers between devices: 214 us -> 9.48 us
  waiting for transfers between devices: 130 us -> 8.73 us
  local copies, waits for them, and re-layouts: 39.4 us -> 3.21 us
  Pallas kernels: 0 us -> 33.7 us
  blocking collectives: 48.1 us -> 15.8 us
  other arithmetic: 15.4 us -> 0 us
    ppermute x100 -> x8, starting transfers between devices: 214 us -> 9.48 us  [swap(): return lax.ppermute(values, AXES, plan.pairs(swaps))]
    ppermute x100 -> x8, waiting for transfers between devices: 130 us -> 8.73 us  [swap(): return lax.ppermute(values, AXES, plan.pairs(swaps))]
    all_gather x4 -> x0, blocking collectives: 48.1 us -> none  [the longest x2 27.6 us: collect(): return lax.all_gather(members, 'grp', axis=0, tiled=True)]
    pallas_call x0 -> x5, Pallas kernels: none -> 33.7 us  [call(): pl.pallas_call(kernel, out_shape=[jax.ShapeDtypeStruct(shape, F32) for sh...]
    reshape x10 -> x0, local copies, waits for them, and re-layouts: 29.9 us -> none  [the longest x5 22 us: restrict(): values.reshape(values.shape[0] // 2, 2, values.shape[1] // 2, 2, values.s...]
    all_to_all x0 -> x1, blocking collectives: none -> 15.8 us  [on_device(): joined = lax.all_to_all(chunk, AXES, 0, 0, tiled=True)]
    reduce_sum x13 -> x0, other arithmetic: 9.14 us -> none  [restrict(): return jnp.mean(shaped, axis=(1, 3, 5))]
    broadcast_in_dim x7 -> x0, local copies, waits for them, and re-layouts: 4.56 us -> none  [prolong(): jnp.broadcast_to(values[:, None, :, None, :, None], (values.shape[0], 2,...]
  transfers between devices with their start and end apart: 100 -> 8, of which waited for: 36 -> 4; matrix products, arithmetic and copies ran while one was open for 7% -> 0% of each run, Pallas kernels for 0% -> 5%
where the time goes in v1:
time: 71.2 us; the launch traced here: 70.9 us
  Pallas kernels  33.7 us (47%)
  blocking collectives  15.8 us (22%)
  starting transfers between devices  9.48 us (13%)
  waiting for transfers between devices  8.73 us (12%)
  local copies, waits for them, and re-layouts  3.21 us (5%)
    pallas_call x5, Pallas kernels, call(): pl.pallas_call(kernel, out_shape=[jax.ShapeDtypeStruct(shape, F32) for sh...  33.7 us
    all_to_all x1, blocking collectives, on_device(): joined = lax.all_to_all(chunk, AXES, 0, 0, tiled=True)  15.8 us
    ppermute x8, starting transfers between devices, swap(): return lax.ppermute(values, AXES, plan.pairs(swaps))  9.48 us
    ppermute x8, waiting for transfers between devices, swap(): return lax.ppermute(values, AXES, plan.pairs(swaps))  8.73 us
    unnamed x12, local copies, waits for them, and re-layouts  3.21 us
  transfers between devices with their start and end apart: 8, of which 4 were waited for; matrix products, arithmetic and copies ran while one was open for 0% of the time, Pallas kernels for 5%

profile of v1, /device:TPU:0, one launch (start us, length us, event | category | flops | bytes accessed | tf_op | source)
XLA Modules:
  0.0 70.9 jit_solution(3589103729279645596)
XLA Ops:
  0.0 3.0 %collective-permute-start = (f32[16,16,128]{2,1,0:T(8,128)}, f32[16,16,128]{2,1,0:T(8,128)S(1)}, u32[]{:S(2)}, u32[]{:S(2)}) collective-permute-start(f32[16,16,128]{2,1,0:T(8,128)} %refs_1_.4), channel_id=1, source_target_pairs={{0,4},{1,5},{2,6},{3,7},{4,0},{5,1},{6,2},{7,3},{8,12},{9,13},{10,... | collective-permute-start | bytes 393224 | tf_op jit(solution)/shard_map/ppermute | solution.py:773
  3.0 0.0 collective-permute-start.1
  3.0 0.0 copy-start
  3.0 0.9 %copy-done = f32[16,16,128]{2,1,0:T(8,128)S(1)} copy-done((f32[16,16,128]{2,1,0:T(8,128)S(1)}, f32[16,16,128]{2,1,0:T(8,128)}, u32[]{:S(2)}) %copy-start) | copy-done | bytes 131096
  3.9 0.0 copy-start.1
  3.9 0.9 %copy-done.1 = f32[16,16,128]{2,1,0:T(8,128)S(1)} copy-done((f32[16,16,128]{2,1,0:T(8,128)S(1)}, f32[16,16,128]{2,1,0:T(8,128)}, u32[]{:S(2)}) %copy-start.1) | copy-done | bytes 131096
  4.8 0.0 copy-start.2
  4.8 0.0 copy-start.3
  4.8 0.2 shard_map.64
  5.0 0.9 %collective-permute-start.4 = (f32[4,16,128]{2,1,0:T(8,128)S(1)}, f32[4,16,128]{2,1,0:T(8,128)S(1)}, u32[]{:S(2)}, u32[]{:S(2)}) collective-permute-start(f32[4,16,128]{2,1,0:T(8,128)S(1)} %get-tuple-element.18), channel_id=1, source_target_pairs={{0,5},{1,4},{2,7},{3,6},{4,1},{5,0},{6,3},{7,2},{8,13},{9,12},{10,... | collective-permute-start | bytes 98312 | tf_op jit(solution)/shard_map/ppermute | solution.py:773
  6.0 1.2 %collective-permute-start.2 = (f32[4,16,128]{2,1,0:T(8,128)S(1)}, f32[4,16,128]{2,1,0:T(8,128)S(1)}, u32[]{:S(2)}, u32[]{:S(2)}) collective-permute-start(f32[4,16,128]{2,1,0:T(8,128)S(1)} %get-tuple-element.18), channel_id=1, source_target_pairs={{0,1},{1,0},{2,3},{3,2},{4,5},{5,4},{6,7},{7,6},{8,9},{9,8},{10,11... | collective-permute-start | bytes 98312 | tf_op jit(solution)/shard_map/ppermute | solution.py:773
  7.2 1.0 %collective-permute-start.5 = (f32[4,16,128]{2,1,0:T(8,128)S(1)}, f32[4,16,128]{2,1,0:T(8,128)S(1)}, u32[]{:S(2)}, u32[]{:S(2)}) collective-permute-start(f32[4,16,128]{2,1,0:T(8,128)S(1)} %get-tuple-element.19), channel_id=1, source_target_pairs={{0,7},{1,6},{2,5},{3,4},{4,3},{5,2},{6,1},{7,0},{8,15},{9,14},{10,... | collective-permute-start | bytes 98312 | tf_op jit(solution)/shard_map/ppermute | solution.py:773
  8.2 2.0 %collective-permute-done.4.refs_7_ = f32[4,16,128]{2,1,0:T(8,128)S(1)} collective-permute-done((f32[4,16,128]{2,1,0:T(8,128)S(1)}, f32[4,16,128]{2,1,0:T(8,128)S(1)}, u32[]{:S(2)}, u32[]{:S(2)}) %collective-permute-start.4) | collective-permute-done | bytes 32800 | tf_op jit(solution)/shard_map/ppermute | solution.py:773
  10.2 1.1 %collective-permute-start.3 = (f32[4,16,128]{2,1,0:T(8,128)S(1)}, f32[4,16,128]{2,1,0:T(8,128)S(1)}, u32[]{:S(2)}, u32[]{:S(2)}) collective-permute-start(f32[4,16,128]{2,1,0:T(8,128)S(1)} %get-tuple-element.19), channel_id=1, source_target_pairs={{0,3},{1,2},{2,1},{3,0},{4,7},{5,6},{6,5},{7,4},{8,11},{9,10},{10,... | collective-permute-start | bytes 98312 | tf_op jit(solution)/shard_map/ppermute | solution.py:773
  11.3 0.0 collective-permute-done.2.refs_5_
  11.3 0.3 collective-permute-done.5.refs_8_
  11.6 2.2 %collective-permute-done.3.refs_6_ = f32[4,16,128]{2,1,0:T(8,128)S(1)} collective-permute-done((f32[4,16,128]{2,1,0:T(8,128)S(1)}, f32[4,16,128]{2,1,0:T(8,128)S(1)}, u32[]{:S(2)}, u32[]{:S(2)}) %collective-permute-start.3) | collective-permute-done | bytes 32800 | tf_op jit(solution)/shard_map/ppermute | solution.py:773
  13.8 0.0 collective-permute-done.refs_3_
  13.8 0.0 collective-permute-done.1.refs_4_
  13.8 0.0 copy-start.5
  13.8 0.7 copy-done.5
  14.5 0.1 shard_map.66
  14.7 1.5 %collective-permute-start.6 = (f32[688,128]{1,0:T(8,128)S(1)}, f32[688,128]{1,0:T(8,128)S(1)}, u32[]{:S(2)}, u32[]{:S(2)}) collective-permute-start(f32[688,128]{1,0:T(8,128)S(1)} %get-tuple-element.20), channel_id=1, source_target_pairs={{0,8},{1,9},{2,10},{3,11},{4,12},{5,13},{6,14},{7,15},{8,0},{9,1},... | collective-permute-start | bytes 1056776 | tf_op jit(solution)/shard_map/ppermute | solution.py:773
  16.1 0.7 collective-permute-start.7
  16.8 0.0 copy-start.4
  16.8 0.7 copy-done.4
  17.5 3.2 %shard_map.65.refs_2_ = f32[2,4,4,4,8,384]{5,4,3,2,1,0:T(8,128)S(1)} custom-call(s32[4,8,128]{2,1,0:T(8,128)S(1)} %copy-done.4, f32[16,16,128]{2,1,0:T(8,128)S(1)} %copy-done, f32[16,16,128]{2,1,0:T(8,128)S(1)} %copy-done.1, f32[16,16,128]{2,1,0:T(8,128)S(1)} %collective-permute-done.refs_3_, f32[16,16,128]{2,1,0:T(8,128)S(1)} %collective-permute-done.1.refs_4_, ...), custom_call_target="tpu_custom_call" | custom-call | tf_op jit(solution)/shard_map/pallas_call | solution.py:754
  20.7 4.3 %collective-permute-done.6.refs_3_ = f32[688,128]{1,0:T(8,128)S(1)} collective-permute-done((f32[688,128]{1,0:T(8,128)S(1)}, f32[688,128]{1,0:T(8,128)S(1)}, u32[]{:S(2)}, u32[]{:S(2)}) %collective-permute-start.6) | collective-permute-done | bytes 352288 | tf_op jit(solution)/shard_map/ppermute | solution.py:773
  25.0 0.0 collective-permute-done.7.refs_4_
  25.0 0.0 copy-done.2
  25.0 0.0 copy-done.3
  25.0 14.5 %shard_map.67 = (f32[32,8,128]{2,1,0:T(8,128)S(1)}, f32[4,4,4,8,384]{4,3,2,1,0:T(8,128)S(1)}, f32[4,4,4,8,384]{4,3,2,1,0:T(8,128)S(1)}, f32[4,4,4,8,384]{4,3,2,1...) custom-call(s32[4,8,128]{2,1,0:T(8,128)S(1)} %copy-done.3, ...), custom_call_target="tpu_custom_call" | custom-call | tf_op jit(solution)/shard_map/pallas_call | solution.py:754
  39.5 15.8 %all_to_all.5.refs_1_ = f32[32,8,128]{2,1,0:T(8,128)S(1)} all-to-all(f32[32,8,128]{2,1,0:T(8,128)S(1)} %get-tuple-element.22), channel_id=1, replica_groups=mesh['grp'=4,'gy'=2,'gx'=4] {'grp','gy','gx'}, dimensions={0} | all-to-all | bytes 262144 | tf_op jit(solution)/shard_map/all_to_all | solution.py:812
  55.3 15.7 %shard_map.68 = f32[16,16,128]{2,1,0:T(8,128)} custom-call(s32[2,8,384]{2,1,0:T(8,128)S(1)} %copy-done.2, f32[32,8,128]{2,1,0:T(8,128)S(1)} %all_to_all.5.refs_1_, f32[4,4,4,8,384]{4,3,2,1,0:T(8,128)S(1)} %get-tuple-element.23.refs_2_, f32[4,4,4,8,384]{4,3,2,1,0:T(8,128)S(1)} %get-tuple-element.24.refs_3_, ...), custom_call_target="tpu_custom_call" | custom-call | tf_op jit(solution)/shard_map/pallas_call | solution.py:754
Async XLA Ops:
  0.0 13.8 %collective-permute-start = (f32[16,16,128]{2,1,0:T(8,128)}, f32[16,16,128]{2,1,0:T(8,128)S(1)}, u32[]{:S(2)}, u32[]{:S(2)}) collective-permute-start(f32[16,16,128]{2,1,0:T(8,128)} %refs_1_.4), channel_id=1, source_target_pairs={{0,4},{1,5},{2,6},{3,7},{4,0},{5,1},{6,2},{7,3},{8,12},{9,13},{10,... | collective-permute-start | bytes 393224 | tf_op jit(solution)/shard_map/ppermute | solution.py:773
  3.0 10.9 %collective-permute-start.1 = (f32[16,16,128]{2,1,0:T(8,128)}, f32[16,16,128]{2,1,0:T(8,128)S(1)}, u32[]{:S(2)}, u32[]{:S(2)}) collective-permute-start(f32[16,16,128]{2,1,0:T(8,128)} %refs_2_.3), channel_id=1, source_target_pairs={{0,4},{1,5},{2,6},{3,7},{4,0},{5,1},{6,2},{7,3},{8,12},{9,13},{10,... | collective-permute-start | bytes 393224 | tf_op jit(solution)/shard_map/ppermute | solution.py:773
  3.0 0.9 %copy-start = (f32[16,16,128]{2,1,0:T(8,128)S(1)}, f32[16,16,128]{2,1,0:T(8,128)}, u32[]{:S(2)}) copy-start(f32[16,16,128]{2,1,0:T(8,128)} %refs_1_.4) | copy-start | bytes 393220
  3.9 0.9 %copy-start.1 = (f32[16,16,128]{2,1,0:T(8,128)S(1)}, f32[16,16,128]{2,1,0:T(8,128)}, u32[]{:S(2)}) copy-start(f32[16,16,128]{2,1,0:T(8,128)} %refs_2_.3) | copy-start | bytes 393220
  4.8 20.2 %copy-start.2 = (s32[2,8,384]{2,1,0:T(8,128)S(1)}, s32[2,8,384]{2,1,0:T(8,128)}, u32[]{:S(2)}) copy-start(s32[2,8,384]{2,1,0:T(8,128)} %constant.10.clone.refs_1_.refs_0_) | copy-start | bytes 73732
  4.8 20.2 %copy-start.3 = (s32[4,8,128]{2,1,0:T(8,128)S(1)}, s32[4,8,128]{2,1,0:T(8,128)}, u32[]{:S(2)}) copy-start(s32[4,8,128]{2,1,0:T(8,128)} %constant.11.clone.refs_0_) | copy-start | bytes 49156
  5.0 5.2 %collective-permute-start.4 = (f32[4,16,128]{2,1,0:T(8,128)S(1)}, f32[4,16,128]{2,1,0:T(8,128)S(1)}, u32[]{:S(2)}, u32[]{:S(2)}) collective-permute-start(f32[4,16,128]{2,1,0:T(8,128)S(1)} %get-tuple-element.18), channel_id=1, source_target_pairs={{0,5},{1,4},{2,7},{3,6},{4,1},{5,0},{6,3},{7,2},{8,13},{9,12},{10,... | collective-permute-start | bytes 98312 | tf_op jit(solution)/shard_map/ppermute | solution.py:773
  6.0 5.4 %collective-permute-start.2 = (f32[4,16,128]{2,1,0:T(8,128)S(1)}, f32[4,16,128]{2,1,0:T(8,128)S(1)}, u32[]{:S(2)}, u32[]{:S(2)}) collective-permute-start(f32[4,16,128]{2,1,0:T(8,128)S(1)} %get-tuple-element.18), channel_id=1, source_target_pairs={{0,1},{1,0},{2,3},{3,2},{4,5},{5,4},{6,7},{7,6},{8,9},{9,8},{10,11... | collective-permute-start | bytes 98312 | tf_op jit(solution)/shard_map/ppermute | solution.py:773
  7.2 4.4 %collective-permute-start.5 = (f32[4,16,128]{2,1,0:T(8,128)S(1)}, f32[4,16,128]{2,1,0:T(8,128)S(1)}, u32[]{:S(2)}, u32[]{:S(2)}) collective-permute-start(f32[4,16,128]{2,1,0:T(8,128)S(1)} %get-tuple-element.19), channel_id=1, source_target_pairs={{0,7},{1,6},{2,5},{3,4},{4,3},{5,2},{6,1},{7,0},{8,15},{9,14},{10,... | collective-permute-start | bytes 98312 | tf_op jit(solution)/shard_map/ppermute | solution.py:773
  10.2 3.6 %collective-permute-start.3 = (f32[4,16,128]{2,1,0:T(8,128)S(1)}, f32[4,16,128]{2,1,0:T(8,128)S(1)}, u32[]{:S(2)}, u32[]{:S(2)}) collective-permute-start(f32[4,16,128]{2,1,0:T(8,128)S(1)} %get-tuple-element.19), channel_id=1, source_target_pairs={{0,3},{1,2},{2,1},{3,0},{4,7},{5,6},{6,5},{7,4},{8,11},{9,10},{10,... | collective-permute-start | bytes 98312 | tf_op jit(solution)/shard_map/ppermute | solution.py:773
  13.8 0.7 copy-start.5
  14.7 10.3 %collective-permute-start.6 = (f32[688,128]{1,0:T(8,128)S(1)}, f32[688,128]{1,0:T(8,128)S(1)}, u32[]{:S(2)}, u32[]{:S(2)}) collective-permute-start(f32[688,128]{1,0:T(8,128)S(1)} %get-tuple-element.20), channel_id=1, source_target_pairs={{0,8},{1,9},{2,10},{3,11},{4,12},{5,13},{6,14},{7,15},{8,0},{9,1},... | collective-permute-start | bytes 1056776 | tf_op jit(solution)/shard_map/ppermute | solution.py:773
  16.1 8.9 %collective-permute-start.7 = (f32[688,128]{1,0:T(8,128)S(1)}, f32[688,128]{1,0:T(8,128)S(1)}, u32[]{:S(2)}, u32[]{:S(2)}) collective-permute-start(f32[688,128]{1,0:T(8,128)S(1)} %get-tuple-element.21), channel_id=1, source_target_pairs={{8,16},{9,17},{10,18},{11,19},{12,20},{13,21},{14,22},{15,23},{16,... | collective-permute-start | bytes 1056776 | tf_op jit(solution)/shard_map/ppermute | solution.py:773
  16.8 0.7 %copy-start.4 = (s32[4,8,128]{2,1,0:T(8,128)S(1)}, s32[4,8,128]{2,1,0:T(8,128)}, u32[]{:S(2)}) copy-start(s32[4,8,128]{2,1,0:T(8,128)} %constant.9.clone.refs_0_) | copy-start | bytes 49156

commit v2 on v1

--- a/solution.py
+++ b/solution.py
@@ -291,20 +291,19 @@
 def fill_rim(plan, ref, n):
     tile = plan.tile
     row = lax.broadcasted_iota(jnp.int32, (tile, LW), 0)
-
-    def body(i, carry):
-        for j in range(n):
-            ref[0, i + 1, j + 1] = roll_lanes(ref[n, i + 1, j + 1], XW)
-            ref[n + 1, i + 1, j + 1] = roll_lanes(ref[1, i + 1, j + 1], -XW)
-            up = pltpu.roll(ref[i + 1, n, j + 1], 1, 0)
-            down = pltpu.roll(ref[i + 1, 1, j + 1], tile - 1, 0)
-            ref[i + 1, 0, j + 1] = jnp.where(row == 0, 0.0, up)
-            ref[i + 1, n + 1, j + 1] = jnp.where(row == tile - 1, 0.0, down)
-            ref[i + 1, j + 1, 0] = roll_lanes(ref[i + 1, j + 1, n], 1)
-            ref[i + 1, j + 1, n + 1] = roll_lanes(ref[i + 1, j + 1, 1], -1)
-        return carry
-
-    lax.fori_loop(0, n, body, 0)
+    for i in range(1, n + 1):
+        for j in range(1, n + 1):
+            z_low, z_high = ref[n, i, j], ref[1, i, j]
+            y_low, y_high = ref[i, n, j], ref[i, 1, j]
+            x_low, x_high = ref[i, j, n], ref[i, j, 1]
+            ref[0, i, j] = roll_lanes(z_low, XW)
+            ref[n + 1, i, j] = roll_lanes(z_high, -XW)
+            ref[i, 0, j] = jnp.where(row == 0, 0.0, pltpu.roll(y_low, 1, 0))
+            ref[i, n + 1, j] = jnp.where(
+                row == tile - 1, 0.0, pltpu.roll(y_high, tile - 1, 0)
+            )
+            ref[i, j, 0] = roll_lanes(x_low, 1)
+            ref[i, j, n + 1] = roll_lanes(x_high, -1)
 
 
 def around(ref, a, b, c):
@@ -330,6 +329,11 @@
 
 
 def over_pairs(n, step):
+    if n == 2:
+        for a, b in np.ndindex(2, 2):
+            step(a, b)
+        return
+
     def body(i, carry):
         step(lax.div(i, n), lax.rem(i, n))
         return carry
@@ -373,8 +377,8 @@
 
 def down_kernel(plan, *refs):
     (tab_ref, coord_ref, own_ref, even_ref, odd_ref) = refs[:5]
-    chunk, m0_out, h0, e0, k0, m1_out, h1, e1, k1 = refs[5:14]
-    m0, r0, v0, w0, d0, m1, r1, v1, w1, d1, planes, sides = refs[14:]
+    chunk, m0, h0, e0, k0, m1, h1, e1, k1 = refs[5:14]
+    r0, v0, w0, d0, r1, v1, w1, d1, planes, sides = refs[14:]
     near, tile = plan.near, plan.tile
     own_row, places = plan.y_places()
     z_even = is_even("grp")
@@ -438,7 +442,6 @@
                         value = jnp.where(inside[:, lanes], value, 0.0)
                         if a == 1:
                             m0[pz + 1, py + 1, px + 1, :, lanes] = value
-                            m0_out[pz, py, px, :, lanes] = value
                         else:
                             r0[pz, py, px, :, lanes] = value
                 for px in range(4):
@@ -446,7 +449,6 @@
                     value = jnp.where(inside[:, lanes], own_ref[a, pz, py, px, :, lanes], 0.0)
                     if a == 1:
                         m0[pz + 1, py + 1, px + 1, :, lanes] = value
-                        m0_out[pz, py, px, :, lanes] = value
                     else:
                         r0[pz, py, px, :, lanes] = value
         return carry
@@ -467,7 +469,6 @@
                         mobility = mobility + m0[i + 1, j + 1, k + 1]
             r1[a, b, c] = 0.125 * rest
             m1[a + 1, b + 1, c + 1] = 0.125 * mobility
-            m1_out[a, b, c] = 0.125 * mobility
 
     over_pairs(2, restrict)
     descend(plan, 2, 0.25, inside, m1, r1, v1, w1, d1, h1, e1, k1)
@@ -629,11 +630,10 @@
 
 
 def up_kernel(plan, *refs):
-    coord_ref, joined, m0_in, h0, e0, k0, m1_in, h1, e1, k1, out = refs[:11]
-    m0, v0, w0, m1, v1, w1, window = refs[11:18]
-    r2, m2, v2 = refs[18:21]
-    fine_refs = refs[21:24]
-    coarse_refs = refs[24:27]
+    coord_ref, joined, m0, h0, e0, k0, m1, h1, e1, k1, out = refs[:11]
+    v0, w0, v1, w1, window, r2, m2, v2 = refs[11:19]
+    fine_refs = refs[19:22]
+    coarse_refs = refs[22:25]
     tile = plan.tile
     gz, gy, gx = plan.counts
     iz, iy, ix = (lax.axis_index(axis) for axis in AXES)
@@ -700,16 +700,6 @@
         lanes = slice(128 * t, 128 * t + 128)
         window[:, lanes] = jnp.where(inside[:, lanes], value, 0.0)
 
-    def widen(n, source_ref, ref):
-        def step(a, b):
-            for c in range(n):
-                ref[a + 1, b + 1, c + 1] = source_ref[a, b, c]
-
-        over_pairs(n, step)
-        fill_rim(plan, ref, n)
-
-    widen(2, m1_in, m1)
-    widen(4, m0_in, m0)
     below = window[...]
 
     def keep(a, b, c, value):
@@ -718,7 +708,7 @@
     ascend(plan, 2, m1, h1, e1, k1, lambda a, b, c: below, v1, w1, keep)
 
     def from_half(a, b, c):
-        return v1[lax.div(a, 2) + 1, lax.div(b, 2) + 1, c // 2 + 1]
+        return v1[lax.shift_right_logical(a, 1) + 1, lax.shift_right_logical(b, 1) + 1, c // 2 + 1]
 
     def finish(a, b, c, value):
         v0[a + 1, b + 1, c + 1] = value
@@ -800,9 +790,9 @@
         coordinates = coordinate_rows(tile)
         chunk, *state = call(
             lambda *refs: down_kernel(plan, *refs),
-            [(plan.devices, 8, 128)] + [full] * 4 + [half] * 4,
-            [full_rim, full, full_rim, full_rim, full]
-            + [half_rim, half, half_rim, half_rim, half]
+            [(plan.devices, 8, 128)] + [full_rim] + [full] * 3 + [half_rim] + [half] * 3,
+            [full, full_rim, full_rim, full]
+            + [half, half_rim, half_rim, half]
             + [(2, 2, EDGE, plan.rows, 128), (2, 4, plan.rows, 128)],
             table(edge_far_rows()),
             coordinates,
@@ -815,8 +805,8 @@
         (out,) = call(
             lambda *refs: up_kernel(plan, *refs),
             [(16, 16, 128)],
-            [full_rim] * 3
-            + [half_rim] * 3
+            [full_rim] * 2
+            + [half_rim] * 2
             + [(tile, LW)]
             + [(z2, y2, 128)] * 2
             + [(z2 + 2 * HALO, y2 + margin, 128)]

time: 71.2 us -> 57.7 us (0.81)
  Pallas kernels: 33.7 us -> 20.2 us
    pallas_call x5, Pallas kernels: 33.7 us -> 20.2 us  [call(): pl.pallas_call(kernel, out_shape=[jax.ShapeDtypeStruct(shape, F32) for sh...]
  transfers between devices with their start and end apart: 8 -> 8, of which waited for: 4 -> 4; matrix products, arithmetic and copies ran while one was open for 0% -> 0% of each run, Pallas kernels for 5% -> 6%
where the time goes in v2:
time: 57.7 us; the launch traced here: 57.4 us
  Pallas kernels  20.2 us (35%)
  blocking collectives  15.7 us (27%)
  starting transfers between devices  9.48 us (16%)
  waiting for transfers between devices  8.73 us (15%)
  local copies, waits for them, and re-layouts  3.21 us (6%)
    pallas_call x5, Pallas kernels, call(): pl.pallas_call(kernel, out_shape=[jax.ShapeDtypeStruct(shape, F32) for sh...  20.2 us
    all_to_all x1, blocking collectives, on_device(): joined = lax.all_to_all(chunk, AXES, 0, 0, tiled=True)  15.7 us
    ppermute x8, starting transfers between devices, swap(): return lax.ppermute(values, AXES, plan.pairs(swaps))  9.48 us
    ppermute x8, waiting for transfers between devices, swap(): return lax.ppermute(values, AXES, plan.pairs(swaps))  8.73 us
    unnamed x12, local copies, waits for them, and re-layouts  3.21 us
  transfers between devices with their start and end apart: 8, of which 4 were waited for; matrix products, arithmetic and copies ran while one was open for 0% of the time, Pallas kernels for 6%

profile of v2, /device:TPU:0, one launch (start us, length us, event | category | flops | bytes accessed | tf_op | source)
XLA Modules:
  0.0 57.4 jit_solution(7592824808432997388)
XLA Ops:
  0.0 3.0 %collective-permute-start = (f32[16,16,128]{2,1,0:T(8,128)}, f32[16,16,128]{2,1,0:T(8,128)S(1)}, u32[]{:S(2)}, u32[]{:S(2)}) collective-permute-start(f32[16,16,128]{2,1,0:T(8,128)} %refs_1_.4), channel_id=1, source_target_pairs={{0,4},{1,5},{2,6},{3,7},{4,0},{5,1},{6,2},{7,3},{8,12},{9,13},{10,... | collective-permute-start | bytes 393224 | tf_op jit(solution)/shard_map/ppermute | solution.py:763
  3.0 0.0 collective-permute-start.1
  3.0 0.0 copy-start
  3.0 0.9 %copy-done = f32[16,16,128]{2,1,0:T(8,128)S(1)} copy-done((f32[16,16,128]{2,1,0:T(8,128)S(1)}, f32[16,16,128]{2,1,0:T(8,128)}, u32[]{:S(2)}) %copy-start) | copy-done | bytes 131096
  3.9 0.0 copy-start.1
  3.9 0.9 %copy-done.1 = f32[16,16,128]{2,1,0:T(8,128)S(1)} copy-done((f32[16,16,128]{2,1,0:T(8,128)S(1)}, f32[16,16,128]{2,1,0:T(8,128)}, u32[]{:S(2)}) %copy-start.1) | copy-done | bytes 131096
  4.8 0.0 copy-start.2
  4.8 0.0 copy-start.3
  4.8 0.2 shard_map.64
  5.0 0.9 %collective-permute-start.4 = (f32[4,16,128]{2,1,0:T(8,128)S(1)}, f32[4,16,128]{2,1,0:T(8,128)S(1)}, u32[]{:S(2)}, u32[]{:S(2)}) collective-permute-start(f32[4,16,128]{2,1,0:T(8,128)S(1)} %get-tuple-element.18), channel_id=1, source_target_pairs={{0,5},{1,4},{2,7},{3,6},{4,1},{5,0},{6,3},{7,2},{8,13},{9,12},{10,... | collective-permute-start | bytes 98312 | tf_op jit(solution)/shard_map/ppermute | solution.py:763
  6.0 1.2 %collective-permute-start.2 = (f32[4,16,128]{2,1,0:T(8,128)S(1)}, f32[4,16,128]{2,1,0:T(8,128)S(1)}, u32[]{:S(2)}, u32[]{:S(2)}) collective-permute-start(f32[4,16,128]{2,1,0:T(8,128)S(1)} %get-tuple-element.18), channel_id=1, source_target_pairs={{0,1},{1,0},{2,3},{3,2},{4,5},{5,4},{6,7},{7,6},{8,9},{9,8},{10,11... | collective-permute-start | bytes 98312 | tf_op jit(solution)/shard_map/ppermute | solution.py:763
  7.2 1.0 %collective-permute-start.5 = (f32[4,16,128]{2,1,0:T(8,128)S(1)}, f32[4,16,128]{2,1,0:T(8,128)S(1)}, u32[]{:S(2)}, u32[]{:S(2)}) collective-permute-start(f32[4,16,128]{2,1,0:T(8,128)S(1)} %get-tuple-element.19), channel_id=1, source_target_pairs={{0,7},{1,6},{2,5},{3,4},{4,3},{5,2},{6,1},{7,0},{8,15},{9,14},{10,... | collective-permute-start | bytes 98312 | tf_op jit(solution)/shard_map/ppermute | solution.py:763
  8.2 2.0 %collective-permute-done.4.refs_7_ = f32[4,16,128]{2,1,0:T(8,128)S(1)} collective-permute-done((f32[4,16,128]{2,1,0:T(8,128)S(1)}, f32[4,16,128]{2,1,0:T(8,128)S(1)}, u32[]{:S(2)}, u32[]{:S(2)}) %collective-permute-start.4) | collective-permute-done | bytes 32800 | tf_op jit(solution)/shard_map/ppermute | solution.py:763
  10.2 1.1 %collective-permute-start.3 = (f32[4,16,128]{2,1,0:T(8,128)S(1)}, f32[4,16,128]{2,1,0:T(8,128)S(1)}, u32[]{:S(2)}, u32[]{:S(2)}) collective-permute-start(f32[4,16,128]{2,1,0:T(8,128)S(1)} %get-tuple-element.19), channel_id=1, source_target_pairs={{0,3},{1,2},{2,1},{3,0},{4,7},{5,6},{6,5},{7,4},{8,11},{9,10},{10,... | collective-permute-start | bytes 98312 | tf_op jit(solution)/shard_map/ppermute | solution.py:763
  11.3 0.0 collective-permute-done.2.refs_5_
  11.3 0.3 collective-permute-done.5.refs_8_
  11.6 2.2 %collective-permute-done.3.refs_6_ = f32[4,16,128]{2,1,0:T(8,128)S(1)} collective-permute-done((f32[4,16,128]{2,1,0:T(8,128)S(1)}, f32[4,16,128]{2,1,0:T(8,128)S(1)}, u32[]{:S(2)}, u32[]{:S(2)}) %collective-permute-start.3) | collective-permute-done | bytes 32800 | tf_op jit(solution)/shard_map/ppermute | solution.py:763
  13.8 0.0 collective-permute-done.refs_3_
  13.8 0.0 collective-permute-done.1.refs_4_
  13.8 0.0 copy-start.5
  13.8 0.7 %copy-done.5 = s32[1,8,128]{2,1,0:T(8,128)S(1)} copy-done((s32[1,8,128]{2,1,0:T(8,128)S(1)}, s32[1,8,128]{2,1,0:T(8,128)}, u32[]{:S(2)}) %copy-start.5) | copy-done | bytes 4120
  14.5 0.1 shard_map.66
  14.7 1.5 %collective-permute-start.6 = (f32[688,128]{1,0:T(8,128)S(1)}, f32[688,128]{1,0:T(8,128)S(1)}, u32[]{:S(2)}, u32[]{:S(2)}) collective-permute-start(f32[688,128]{1,0:T(8,128)S(1)} %get-tuple-element.20), channel_id=1, source_target_pairs={{0,8},{1,9},{2,10},{3,11},{4,12},{5,13},{6,14},{7,15},{8,0},{9,1},... | collective-permute-start | bytes 1056776 | tf_op jit(solution)/shard_map/ppermute | solution.py:763
  16.1 0.7 %collective-permute-start.7 = (f32[688,128]{1,0:T(8,128)S(1)}, f32[688,128]{1,0:T(8,128)S(1)}, u32[]{:S(2)}, u32[]{:S(2)}) collective-permute-start(f32[688,128]{1,0:T(8,128)S(1)} %get-tuple-element.21), channel_id=1, source_target_pairs={{8,16},{9,17},{10,18},{11,19},{12,20},{13,21},{14,22},{15,23},{16,... | collective-permute-start | bytes 1056776 | tf_op jit(solution)/shard_map/ppermute | solution.py:763
  16.8 0.0 copy-start.4
  16.8 0.7 %copy-done.4 = s32[4,8,128]{2,1,0:T(8,128)S(1)} copy-done((s32[4,8,128]{2,1,0:T(8,128)S(1)}, s32[4,8,128]{2,1,0:T(8,128)}, u32[]{:S(2)}) %copy-start.4) | copy-done | bytes 16408
  17.5 3.2 %shard_map.65.refs_2_ = f32[2,4,4,4,8,384]{5,4,3,2,1,0:T(8,128)S(1)} custom-call(s32[4,8,128]{2,1,0:T(8,128)S(1)} %copy-done.4, f32[16,16,128]{2,1,0:T(8,128)S(1)} %copy-done, f32[16,16,128]{2,1,0:T(8,128)S(1)} %copy-done.1, f32[16,16,128]{2,1,0:T(8,128)S(1)} %collective-permute-done.refs_3_, f32[16,16,128]{2,1,0:T(8,128)S(1)} %collective-permute-done.1.refs_4_, ...), custom_call_target="tpu_custom_call" | custom-call | tf_op jit(solution)/shard_map/pallas_call | solution.py:744
  20.7 4.3 %collective-permute-done.6.refs_3_ = f32[688,128]{1,0:T(8,128)S(1)} collective-permute-done((f32[688,128]{1,0:T(8,128)S(1)}, f32[688,128]{1,0:T(8,128)S(1)}, u32[]{:S(2)}, u32[]{:S(2)}) %collective-permute-start.6) | collective-permute-done | bytes 352288 | tf_op jit(solution)/shard_map/ppermute | solution.py:763
  25.0 0.0 collective-permute-done.7.refs_4_
  25.0 0.0 copy-done.2
  25.0 0.0 copy-done.3
  25.0 7.8 %shard_map.67 = (f32[32,8,128]{2,1,0:T(8,128)S(1)}, f32[6,6,6,8,384]{4,3,2,1,0:T(8,128)}, f32[4,4,4,8,384]{4,3,2,1,0:T(8,128)S(1)}, f32[4,4,4,8,384]{4,3,2,1,0:T...) custom-call(s32[4,8,128]{2,1,0:T(8,128)S(1)} %copy-done.3, ...), custom_call_target="tpu_custom_call" | custom-call | tf_op jit(solution)/shard_map/pallas_call | solution.py:744
  32.8 15.7 %all_to_all.5.refs_1_ = f32[32,8,128]{2,1,0:T(8,128)S(1)} all-to-all(f32[32,8,128]{2,1,0:T(8,128)S(1)} %get-tuple-element.22), channel_id=1, replica_groups=mesh['grp'=4,'gy'=2,'gx'=4] {'grp','gy','gx'}, dimensions={0} | all-to-all | bytes 262144 | tf_op jit(solution)/shard_map/all_to_all | solution.py:802
  48.6 8.9 %shard_map.68 = f32[16,16,128]{2,1,0:T(8,128)} custom-call(s32[2,8,384]{2,1,0:T(8,128)S(1)} %copy-done.2, f32[32,8,128]{2,1,0:T(8,128)S(1)} %all_to_all.5.refs_1_, f32[6,6,6,8,384]{4,3,2,1,0:T(8,128)} %get-tuple-element.23.refs_2_, f32[4,4,4,8,384]{4,3,2,1,0:T(8,128)S(1)} %get-tuple-element.24.refs_3_, f32[4,4,4,8,384]{4,3,2,1,0:T(8,128)S(1)} %get-tuple-element.25.refs_4_, ...), custom_call_target="tpu_custom_call" | custom-call | tf_op jit(solution)/shard_map/pallas_call | solution.py:744
Async XLA Ops:
  0.0 13.8 %collective-permute-start = (f32[16,16,128]{2,1,0:T(8,128)}, f32[16,16,128]{2,1,0:T(8,128)S(1)}, u32[]{:S(2)}, u32[]{:S(2)}) collective-permute-start(f32[16,16,128]{2,1,0:T(8,128)} %refs_1_.4), channel_id=1, source_target_pairs={{0,4},{1,5},{2,6},{3,7},{4,0},{5,1},{6,2},{7,3},{8,12},{9,13},{10,... | collective-permute-start | bytes 393224 | tf_op jit(solution)/shard_map/ppermute | solution.py:763
  3.0 10.9 %collective-permute-start.1 = (f32[16,16,128]{2,1,0:T(8,128)}, f32[16,16,128]{2,1,0:T(8,128)S(1)}, u32[]{:S(2)}, u32[]{:S(2)}) collective-permute-start(f32[16,16,128]{2,1,0:T(8,128)} %refs_2_.3), channel_id=1, source_target_pairs={{0,4},{1,5},{2,6},{3,7},{4,0},{5,1},{6,2},{7,3},{8,12},{9,13},{10,... | collective-permute-start | bytes 393224 | tf_op jit(solution)/shard_map/ppermute | solution.py:763
  3.0 0.9 %copy-start = (f32[16,16,128]{2,1,0:T(8,128)S(1)}, f32[16,16,128]{2,1,0:T(8,128)}, u32[]{:S(2)}) copy-start(f32[16,16,128]{2,1,0:T(8,128)} %refs_1_.4) | copy-start | bytes 393220
  3.9 0.9 %copy-start.1 = (f32[16,16,128]{2,1,0:T(8,128)S(1)}, f32[16,16,128]{2,1,0:T(8,128)}, u32[]{:S(2)}) copy-start(f32[16,16,128]{2,1,0:T(8,128)} %refs_2_.3) | copy-start | bytes 393220
  4.8 20.2 %copy-start.2 = (s32[2,8,384]{2,1,0:T(8,128)S(1)}, s32[2,8,384]{2,1,0:T(8,128)}, u32[]{:S(2)}) copy-start(s32[2,8,384]{2,1,0:T(8,128)} %constant.10.clone.refs_1_.refs_0_) | copy-start | bytes 73732
  4.8 20.2 %copy-start.3 = (s32[4,8,128]{2,1,0:T(8,128)S(1)}, s32[4,8,128]{2,1,0:T(8,128)}, u32[]{:S(2)}) copy-start(s32[4,8,128]{2,1,0:T(8,128)} %constant.11.clone.refs_0_) | copy-start | bytes 49156
  5.0 5.2 %collective-permute-start.4 = (f32[4,16,128]{2,1,0:T(8,128)S(1)}, f32[4,16,128]{2,1,0:T(8,128)S(1)}, u32[]{:S(2)}, u32[]{:S(2)}) collective-permute-start(f32[4,16,128]{2,1,0:T(8,128)S(1)} %get-tuple-element.18), channel_id=1, source_target_pairs={{0,5},{1,4},{2,7},{3,6},{4,1},{5,0},{6,3},{7,2},{8,13},{9,12},{10,... | collective-permute-start | bytes 98312 | tf_op jit(solution)/shard_map/ppermute | solution.py:763
  6.0 5.4 %collective-permute-start.2 = (f32[4,16,128]{2,1,0:T(8,128)S(1)}, f32[4,16,128]{2,1,0:T(8,128)S(1)}, u32[]{:S(2)}, u32[]{:S(2)}) collective-permute-start(f32[4,16,128]{2,1,0:T(8,128)S(1)} %get-tuple-element.18), channel_id=1, source_target_pairs={{0,1},{1,0},{2,3},{3,2},{4,5},{5,4},{6,7},{7,6},{8,9},{9,8},{10,11... | collective-permute-start | bytes 98312 | tf_op jit(solution)/shard_map/ppermute | solution.py:763
  7.2 4.4 %collective-permute-start.5 = (f32[4,16,128]{2,1,0:T(8,128)S(1)}, f32[4,16,128]{2,1,0:T(8,128)S(1)}, u32[]{:S(2)}, u32[]{:S(2)}) collective-permute-start(f32[4,16,128]{2,1,0:T(8,128)S(1)} %get-tuple-element.19), channel_id=1, source_target_pairs={{0,7},{1,6},{2,5},{3,4},{4,3},{5,2},{6,1},{7,0},{8,15},{9,14},{10,... | collective-permute-start | bytes 98312 | tf_op jit(solution)/shard_map/ppermute | solution.py:763
  10.2 3.6 %collective-permute-start.3 = (f32[4,16,128]{2,1,0:T(8,128)S(1)}, f32[4,16,128]{2,1,0:T(8,128)S(1)}, u32[]{:S(2)}, u32[]{:S(2)}) collective-permute-start(f32[4,16,128]{2,1,0:T(8,128)S(1)} %get-tuple-element.19), channel_id=1, source_target_pairs={{0,3},{1,2},{2,1},{3,0},{4,7},{5,6},{6,5},{7,4},{8,11},{9,10},{10,... | collective-permute-start | bytes 98312 | tf_op jit(solution)/shard_map/ppermute | solution.py:763
  13.8 0.7 %copy-start.5 = (s32[1,8,128]{2,1,0:T(8,128)S(1)}, s32[1,8,128]{2,1,0:T(8,128)}, u32[]{:S(2)}) copy-start(s32[1,8,128]{2,1,0:T(8,128)} %constant.8.clone.refs_0_) | copy-start | bytes 12292
  14.7 10.3 %collective-permute-start.6 = (f32[688,128]{1,0:T(8,128)S(1)}, f32[688,128]{1,0:T(8,128)S(1)}, u32[]{:S(2)}, u32[]{:S(2)}) collective-permute-start(f32[688,128]{1,0:T(8,128)S(1)} %get-tuple-element.20), channel_id=1, source_target_pairs={{0,8},{1,9},{2,10},{3,11},{4,12},{5,13},{6,14},{7,15},{8,0},{9,1},... | collective-permute-start | bytes 1056776 | tf_op jit(solution)/shard_map/ppermute | solution.py:763
  16.1 8.9 %collective-permute-start.7 = (f32[688,128]{1,0:T(8,128)S(1)}, f32[688,128]{1,0:T(8,128)S(1)}, u32[]{:S(2)}, u32[]{:S(2)}) collective-permute-start(f32[688,128]{1,0:T(8,128)S(1)} %get-tuple-element.21), channel_id=1, source_target_pairs={{8,16},{9,17},{10,18},{11,19},{12,20},{13,21},{14,22},{15,23},{16,... | collective-permute-start | bytes 1056776 | tf_op jit(solution)/shard_map/ppermute | solution.py:763
  16.8 0.7 %copy-start.4 = (s32[4,8,128]{2,1,0:T(8,128)S(1)}, s32[4,8,128]{2,1,0:T(8,128)}, u32[]{:S(2)}) copy-start(s32[4,8,128]{2,1,0:T(8,128)} %constant.9.clone.refs_0_) | copy-start | bytes 49156

commit v3 on v2

--- a/solution.py
+++ b/solution.py
@@ -24,13 +24,23 @@
     return lax.broadcasted_iota(jnp.int32, (rows, 128), 1)
 
 
+LANES = lax.GatherDimensionNumbers(
+    offset_dims=(),
+    collapsed_slice_dims=(1,),
+    start_index_map=(1,),
+    operand_batching_dims=(0,),
+    start_indices_batching_dims=(0,),
+)
+
+
 def gather(source, index):
-    return jnp.take_along_axis(source, index, axis=1, mode="promise_in_bounds")
-
-
-def spread(source, offset, px):
-    rows = source.shape[0]
-    return gather(source, (4 * lane_iota(rows) + (px - 4 * offset)) & 127)
+    return lax.gather(
+        source, index[..., None], LANES, (1, 1), mode=lax.GatherScatterMode.PROMISE_IN_BOUNDS
+    )
+
+
+def every_lane(offset, px, rows):
+    return (4 * lane_iota(rows) + ((px - 4 * offset) % 128)) & 127
 
 
 def between(low, high, rows=8):
@@ -38,62 +48,48 @@
     return (lane >= low) & (lane < high)
 
 
-def table(rows):
-    return jnp.asarray(np.repeat(np.stack(rows)[:, None, :], 8, axis=1).astype(np.int32))
-
-
-def edge_send_rows():
-    row = np.zeros(128, np.int64)
-    base = 0
-    for a, width in ((1, M_EDGE), (0, R_EDGE)):
-        for side in (0, 1):
-            first = EDGE - width if side == 0 else 0
-            for z in range(HALO):
-                for k in range(width):
-                    row[base] = a * 48 + z * 12 + first + k + (1000 if side else 0)
-                    base += 1
-    return [row]
-
-
-def edge_own_rows():
-    rows = []
-    for side, tiles in ((0, (0, 1)), (1, (1, 2))):
-        for tile in tiles:
-            row = np.full(128, -1, np.int64)
-            for lane in range(128):
-                z, x = divmod(128 * tile + lane, XW)
-                x = x if side == 0 else x - (XW - HALO)
-                if HALO <= z < HALO + 4 and 0 <= x < HALO:
-                    row[lane] = (z - HALO) * 12 + 4 * x
-            rows.append(row)
-    return rows
-
-
-def edge_far_rows():
-    rows = []
-    base_of = {(1, 0): 0, (1, 1): 33, (0, 0): 66, (0, 1): 96}
-    for tile, first in ((0, 0), (2, HALO + 4)):
-        for a, width in ((0, R_EDGE), (1, M_EDGE)):
-            row = np.full(128, -1000, np.int64)
-            for lane in range(128):
-                z, x = divmod(128 * tile + lane, XW)
-                if not first <= z < first + HALO:
-                    continue
-                for side in (0, 1):
-                    k = 4 * x if side == 0 else 4 * (x - (XW - HALO))
-                    if 0 <= k < EDGE:
-                        start = base_of[a, side] + (z - first) * width
-                        row[lane] = start + k - (EDGE - width if side == 0 else 0)
-            rows.append(row)
-    return rows
-
-
-def coordinate_rows(rows):
-    cells = np.arange(LW)
-    z, x = cells // XW, cells % XW
-    z = np.where(cells < ZW * XW, z, -1000000)
-    both = np.stack([z, x])[:, None, :]
-    return jnp.asarray(np.repeat(both, rows, axis=1).astype(np.int32))
+def window_cells(t, rows):
+    cell = lane_iota(rows) + 128 * t
+    z = jnp.zeros((rows, 128), jnp.int32)
+    for k in range(1, ZW + 1):
+        z = z + (cell >= k * XW).astype(jnp.int32)
+    return z, cell - z * XW
+
+
+EDGE_STARTS = {(1, 0): 0, (1, 1): 33, (0, 0): 66, (0, 1): 96}
+
+
+def edge_send_lanes():
+    lane = lane_iota()
+    mobile = lane < 66
+    right = ((lane >= 33) & mobile) | (lane >= 96)
+    start = jnp.where(mobile, jnp.where(right, 33, 0), jnp.where(right, 96, 66))
+    width = jnp.where(mobile, M_EDGE, R_EDGE)
+    t = lane - start
+    z = (t >= width).astype(jnp.int32) + (t >= 2 * width).astype(jnp.int32)
+    first = jnp.where(right, 0, EDGE - width)
+    return jnp.minimum(jnp.where(mobile, 48, 0) + z * 12 + first + t - z * width, 95), right
+
+
+def edge_own_lanes(side, t, rows):
+    z, x = window_cells(t, rows)
+    x = x if side == 0 else x - (XW - HALO)
+    here = (z >= HALO) & (z < HALO + 4) & (x >= 0) & (x < HALO)
+    return jnp.where(here, (z - HALO) * 12 + 4 * x, 0), here
+
+
+def edge_far_lanes(side, a, rows):
+    z, x = window_cells(2 * side, rows)
+    z = z - (HALO + 4) * side
+    width = M_EDGE if a == 1 else R_EDGE
+    left, right = x < HALO, x >= XW - HALO
+    here = (z >= 0) & (z < HALO) & (left | right)
+    index = jnp.where(
+        left,
+        EDGE_STARTS[a, 0] + z * width + 4 * x - (EDGE - width),
+        EDGE_STARTS[a, 1] + z * width + 4 * (x - (XW - HALO)),
+    )
+    return jnp.where(here, index, 4), here
 
 
 class Plan:
@@ -103,12 +99,12 @@
         self.rows = 16 * (1 + self.near)
         self.cells = self.rows // 4
         self.tile = -(-self.cells // 8) * 8
-        self.z_rows = 16 + 8 * self.near
+        self.z_rows = 8 * self.near
         sizes = [
             M_DEEP * self.z_rows,
-            M_FAR * 8 * self.near,
+            M_FAR * self.z_rows,
             R_DEEP * self.z_rows,
-            R_FAR * 8 * self.near,
+            R_FAR * self.z_rows,
             4 * self.rows,
         ]
         self.starts = [sum(sizes[:i]) for i in range(len(sizes))]
@@ -126,13 +122,14 @@
                 if axis == 2:
                     j = j % n
                 there.append(j)
-            if all(0 <= j < n for j, n in zip(there, self.counts)):
-                out.append(
-                    (
-                        int(np.ravel_multi_index(index, self.counts)),
-                        int(np.ravel_multi_index(there, self.counts)),
-                    )
+            if not all(0 <= j < n for j, n in zip(there, self.counts)):
+                there = [index[0], index[1], index[2] ^ 1]
+            out.append(
+                (
+                    int(np.ravel_multi_index(index, self.counts)),
+                    int(np.ravel_multi_index(there, self.counts)),
                 )
+            )
         return out
 
     def y_places(self):
@@ -153,7 +150,23 @@
     return pl.ds(pl.multiple_of(start, 8), size)
 
 
-def edges_kernel(r_ref, m_ref, even_ref, odd_ref):
+def edges_kernel(r_hbm, m_hbm, r_ref, m_ref, even_ref, odd_ref, even_z_ref, odd_z_ref, sems):
+    copies = [
+        pltpu.make_async_copy(r_hbm, r_ref, sems.at[0]),
+        pltpu.make_async_copy(m_hbm, m_ref, sems.at[1]),
+    ]
+    for copy in copies:
+        copy.start()
+    for copy in copies:
+        copy.wait()
+    z_even = is_even("grp")
+    for swap, out in enumerate((even_z_ref, odd_z_ref)):
+        top = z_even if swap == 0 else jnp.logical_not(z_even)
+        row = 0
+        for ref, deep in ((m_ref, M_DEEP), (r_ref, R_DEEP)):
+            for d in range(1, deep + 1):
+                out[row : row + 16, :] = ref[jnp.where(top, 16 - d, d - 1)]
+                row += 16
     even = is_even("gx")
     for pz in range(4):
         for half in range(2):
@@ -174,33 +187,29 @@
 
 def z_pack_kernel(plan, *refs):
     near = plan.near
-    tab_ref, r_ref, m_ref = refs[:3]
-    beside = [refs[3 + 2 * i : 5 + 2 * i] for i in range(near)]
-    edges = [refs[3 + 2 * near + 2 * i : 5 + 2 * near + 2 * i] for i in range(1 + near)]
+    beside = [refs[2 * i : 2 + 2 * i] for i in range(near)]
+    edges = [refs[2 * near + 2 * i : 2 + 2 * near + 2 * i] for i in range(1 + near)]
     outs = refs[-2:]
     own_row, places = plan.y_places()
     x_even = is_even("gx")
     z_even = is_even("grp")
-    index = tab_ref[0]
+    lanes_0, use_right = edge_send_lanes()
     for swap, out in enumerate(outs):
         top = z_even if swap == 0 else jnp.logical_not(z_even)
-        for a, ref, deep, far, start, far_start in (
-            (1, m_ref, M_DEEP, M_FAR, plan.starts[0], plan.starts[1]),
-            (0, r_ref, R_DEEP, R_FAR, plan.starts[2], plan.starts[3]),
+        for a, deep, far, start, far_start in (
+            (1, M_DEEP, M_FAR, plan.starts[0], plan.starts[1]),
+            (0, R_DEEP, R_FAR, plan.starts[2], plan.starts[3]),
         ):
             for d in range(1, deep + 1):
                 plane = jnp.where(top, 16 - d, d - 1)
-                row = start + (d - 1) * plan.z_rows
-                out[row : row + 16, :] = ref[plane]
+                row = (d - 1) * plan.z_rows
                 for i, (side, _) in enumerate(places):
-                    to = row + 16 + 8 * i
+                    to = start + row + 8 * i
                     out[to : to + 8, :] = beside[i][a][plane, at(8 * (1 - side), 8), :]
                     if d <= far:
-                        to = far_start + ((d - 1) * near + i) * 8
+                        to = far_start + row + 8 * i
                         out[to : to + 8, :] = beside[i][a][plane, at(8 * side, 8), :]
-        first = jnp.where(top, 12, 0)
-        use_right = index >= 1000
-        lanes = jnp.where(use_right, index - 1000, index) + first
+        lanes = lanes_0 + jnp.where(top, 12, 0)
         for i in range(1 + near):
             base = own_row if i == 0 else places[i - 1][1]
             even_ref, odd_ref = edges[i]
@@ -228,9 +237,9 @@
 
 def own_kernel(plan, *refs):
     near = plan.near
-    tab_ref, r_ref, m_ref = refs[:3]
-    beside = [refs[3 + 2 * i : 5 + 2 * i] for i in range(near)]
-    edges = [refs[3 + 2 * near + 2 * i : 5 + 2 * near + 2 * i] for i in range(1 + near)]
+    r_ref, m_ref = refs[:2]
+    beside = [refs[2 + 2 * i : 4 + 2 * i] for i in range(near)]
+    edges = [refs[2 + 2 * near + 2 * i : 4 + 2 * near + 2 * i] for i in range(1 + near)]
     out, planes, sides = refs[-3:]
     tile = plan.tile
     own_row, places = plan.y_places()
@@ -243,45 +252,50 @@
         sides[0, :, at(base, 16), :] = jnp.where(x_even, odd, even)
         sides[1, :, at(base, 16), :] = jnp.where(x_even, even, odd)
 
+    offsets = [(z + HALO) * XW + HALO for z in range(4)]
+    index = [[every_lane(offset, px, tile) for px in range(4)] for offset in offsets]
+    from_edge = {(s, t): edge_own_lanes(s, t, tile) for s, t in ((0, 0), (0, 1), (1, 1), (1, 2))}
+
     def body(pz, carry):
         for a in range(2):
             for py in range(4):
                 cells = [every_fourth(plan, planes, (a, 4 * z + pz), py) for z in range(4)]
                 side = [every_fourth(plan, sides, (s, pz), py) for s in range(2)]
                 for px in range(4):
+                    parts = [gather(cells[z], index[z][px]) for z in range(4)]
                     for t in range(3):
                         value = jnp.zeros((tile, 128), F32)
                         for z in range(4):
-                            offset = (z + HALO) * XW + HALO - 128 * t
+                            offset = offsets[z] - 128 * t
                             low, high = max(offset, 0), min(offset + 32, 128)
                             if low < high:
-                                value = jnp.where(
-                                    between(low, high, tile),
-                                    spread(cells[z], offset % 32, px),
-                                    value,
-                                )
+                                value = jnp.where(between(low, high, tile), parts[z], value)
                         for s in range(2):
-                            if t - s in (0, 1):
-                                index = tab_ref[2 * s + t - s]
-                                index = jnp.concatenate([index] * (tile // 8), axis=0)
-                                lanes = jnp.maximum(index, 0) + (48 * a + px)
-                                value = jnp.where(index >= 0, gather(side[s], lanes), value)
+                            if (s, t) in from_edge:
+                                lanes, here = from_edge[s, t]
+                                lanes = lanes + (48 * a + px)
+                                value = jnp.where(here, gather(side[s], lanes), value)
                         out[a, pz, py, px, :, 128 * t : 128 * t + 128] = value
         return carry
 
     lax.fori_loop(0, 4, body, 0)
 
 
-def inside_mask(plan, coord_ref):
+def inside_mask(plan):
     tile = plan.tile
-    z = coord_ref[0] + (4 * lax.axis_index("grp") - HALO)
-    x = coord_ref[1] + (32 * lax.axis_index("gx") - HALO)
-    mask = (z >= 0) & (z < plan.coarse[0]) & (x >= 0) & (x < plan.coarse[2])
-    if plan.near == 2:
-        row = lax.broadcasted_iota(jnp.int32, (tile, LW), 0)
-        y = row + (4 * lax.axis_index("gy") - 4)
-        mask = mask & (row < plan.cells) & (y >= 0) & (y < plan.coarse[1])
-    return mask
+    masks = []
+    for t in range(3):
+        z, x = window_cells(t, tile)
+        here = z < ZW
+        z = z + (4 * lax.axis_index("grp") - HALO)
+        x = x + (32 * lax.axis_index("gx") - HALO)
+        here = here & (z >= 0) & (z < plan.coarse[0]) & (x >= 0) & (x < plan.coarse[2])
+        if plan.near == 2:
+            row = lax.broadcasted_iota(jnp.int32, (tile, 128), 0)
+            y = row + (4 * lax.axis_index("gy") - 4)
+            here = here & (row < plan.cells) & (y >= 0) & (y < plan.coarse[1])
+        masks.append(jnp.where(here, 1.0, 0.0))
+    return jnp.concatenate(masks, axis=1) > 0.5
 
 
 def roll_lanes(value, shift):
@@ -376,23 +390,23 @@
 
 
 def down_kernel(plan, *refs):
-    (tab_ref, coord_ref, own_ref, even_ref, odd_ref) = refs[:5]
+    own_ref, even_own, odd_own, even_ref, odd_ref = refs[:5]
     chunk, m0, h0, e0, k0, m1, h1, e1, k1 = refs[5:14]
     r0, v0, w0, d0, r1, v1, w1, d1, planes, sides = refs[14:]
     near, tile = plan.near, plan.tile
     own_row, places = plan.y_places()
     z_even = is_even("grp")
-    inside = inside_mask(plan, coord_ref)
+    inside = inside_mask(plan)
 
     for side in range(2):
         use_even = jnp.logical_not(z_even) if side == 0 else z_even
 
-        def read(rows):
-            return jnp.where(use_even, even_ref[rows, :], odd_ref[rows, :])
-
-        for a, deep, far, start, far_start in (
-            (1, M_DEEP, M_FAR, plan.starts[0], plan.starts[1]),
-            (0, R_DEEP, R_FAR, plan.starts[2], plan.starts[3]),
+        def read(rows, even=even_ref, odd=odd_ref):
+            return jnp.where(use_even, even[rows, :], odd[rows, :])
+
+        for a, deep, far, start, far_start, own_start in (
+            (1, M_DEEP, M_FAR, plan.starts[0], plan.starts[1], 0),
+            (0, R_DEEP, R_FAR, plan.starts[2], plan.starts[3], 16 * M_DEEP),
         ):
             for d in range(1, EDGE + 1):
                 plane = EDGE - d if side == 0 else d - 1
@@ -400,15 +414,18 @@
                     planes[side, a, plane] = jnp.zeros((plan.rows, 128), F32)
                 if d > deep:
                     continue
-                row = start + (d - 1) * plan.z_rows
-                planes[side, a, plane, at(own_row, 16), :] = read(slice(row, row + 16))
+                row = own_start + 16 * (d - 1)
+                planes[side, a, plane, at(own_row, 16), :] = read(
+                    slice(row, row + 16), even_own, odd_own
+                )
+                row = (d - 1) * plan.z_rows
                 for i, (y_side, base) in enumerate(places):
-                    row_i = row + 16 + 8 * i
+                    row_i = start + row + 8 * i
                     planes[side, a, plane, at(base + 8 * (1 - y_side), 8), :] = read(
                         slice(row_i, row_i + 8)
                     )
                     if d <= far:
-                        row_i = far_start + ((d - 1) * near + i) * 8
+                        row_i = far_start + row + 8 * i
                         planes[side, a, plane, at(base + 8 * y_side, 8), :] = read(
                             slice(row_i, row_i + 8)
                         )
@@ -416,41 +433,42 @@
             row = plan.starts[4] + pz * plan.rows
             sides[side, pz] = read(slice(row, row + plan.rows))
 
+    first = [HALO, (HALO + 4) * XW + HALO - 256]
+    index = [
+        [[every_lane(first[side] + z * XW, px, tile) for px in range(4)] for z in range(HALO)]
+        for side in range(2)
+    ]
+    here = [
+        [between(first[side] + z * XW, first[side] + z * XW + 32, tile) for z in range(HALO)]
+        for side in range(2)
+    ]
+    from_edge = {(s, a): edge_far_lanes(s, a, tile) for s in range(2) for a in range(2)}
+
     def place(pz, carry):
         for a in range(2):
             for py in range(4):
-                for side, t in ((0, 0), (1, 2)):
-                    cells = [
-                        every_fourth(plan, planes, (side, a, 4 * z + pz), py)
-                        for z in range(HALO)
-                    ]
-                    edge = every_fourth(plan, sides, (side, pz), py)
-                    index = tab_ref[2 * side + a]
-                    index = jnp.concatenate([index] * (tile // 8), axis=0)
-                    lanes = slice(128 * t, 128 * t + 128)
-                    for px in range(4):
+                cells = [
+                    [every_fourth(plan, planes, (s, a, 4 * z + pz), py) for z in range(HALO)]
+                    for s in range(2)
+                ]
+                edge = [every_fourth(plan, sides, (s, pz), py) for s in range(2)]
+                for px in range(4):
+                    for t in range(3):
+                        lanes = slice(128 * t, 128 * t + 128)
                         value = own_ref[a, pz, py, px, :, lanes]
-                        for z in range(HALO):
-                            offset = (z if side == 0 else z + HALO + 4) * XW + HALO - 128 * t
-                            value = jnp.where(
-                                between(offset, offset + 32, tile),
-                                spread(cells[z], offset % 32, px),
-                                value,
-                            )
-                        from_edge = jnp.clip(index + px, 0, 127)
-                        value = jnp.where(index > -100, gather(edge, from_edge), value)
+                        if t != 1:
+                            s = t // 2
+                            for z in range(HALO):
+                                part = gather(cells[s][z], index[s][z][px])
+                                value = jnp.where(here[s][z], part, value)
+                            place_of, at_edge = from_edge[s, a]
+                            part = gather(edge[s], place_of + px)
+                            value = jnp.where(at_edge, part, value)
                         value = jnp.where(inside[:, lanes], value, 0.0)
                         if a == 1:
                             m0[pz + 1, py + 1, px + 1, :, lanes] = value
                         else:
                             r0[pz, py, px, :, lanes] = value
-                for px in range(4):
-                    lanes = slice(128, 256)
-                    value = jnp.where(inside[:, lanes], own_ref[a, pz, py, px, :, lanes], 0.0)
-                    if a == 1:
-                        m0[pz + 1, py + 1, px + 1, :, lanes] = value
-                    else:
-                        r0[pz, py, px, :, lanes] = value
         return carry
 
     lax.fori_loop(0, 4, place, 0)
@@ -630,14 +648,14 @@
 
 
 def up_kernel(plan, *refs):
-    coord_ref, joined, m0, h0, e0, k0, m1, h1, e1, k1, out = refs[:11]
-    v0, w0, v1, w1, window, r2, m2, v2 = refs[11:19]
-    fine_refs = refs[19:22]
-    coarse_refs = refs[22:25]
+    joined, m0, h0, e0, k0, m1, h1, e1, k1, out = refs[:10]
+    v0, w0, v1, w1, window, r2, m2, v2 = refs[10:18]
+    fine_refs = refs[18:21]
+    coarse_refs = refs[21:24]
     tile = plan.tile
     gz, gy, gx = plan.counts
     iz, iy, ix = (lax.axis_index(axis) for axis in AXES)
-    inside = inside_mask(plan, coord_ref)
+    inside = inside_mask(plan)
 
     def unpack(z_block, carry):
         for z in range(4):
@@ -715,37 +733,44 @@
 
     ascend(plan, 4, m0, h0, e0, k0, from_half, v0, w0, finish)
 
+    lane = lane_iota(tile)
+    turns = [(lane & 3) == px for px in range(4)]
+    starts = [(z + HALO) * XW + HALO for z in range(4)]
+    index = [(lax.shift_right_logical(lane, 2) + start % 128) & 127 for start in starts]
+
     def store(pz, carry):
         for py in range(4):
-            for z in range(4):
-                base = (z + HALO) * XW + HALO
-                value = jnp.zeros((tile, 128), F32)
-                lane = lane_iota(tile)
+            parts = [
+                [v0[pz + 1, py + 1, px + 1, :, 128 * t : 128 * t + 128] for t in range(3)]
+                for px in range(4)
+            ]
+            for z, start in enumerate(starts):
+                low, high = start // 128, (start + 31) // 128
+                value = None
                 for px in range(4):
-                    for t in range(3):
-                        offset = base - 128 * t
-                        low, high = max(offset, 0), min(offset + 32, 128)
-                        if low < high:
-                            index = (lax.shift_right_logical(lane, 2) + offset) & 127
-                            here = (
-                                ((lane & 3) == px)
-                                & (lane >= 4 * (low - offset))
-                                & (lane < 4 * (high - offset))
-                            )
-                            part = v0[pz + 1, py + 1, px + 1, :, 128 * t : 128 * t + 128]
-                            value = jnp.where(here, gather(part, index), value)
+                    part = parts[px][low]
+                    if low != high:
+                        part = jnp.where(lane >= 64, part, parts[px][high])
+                    part = gather(part, index[z])
+                    value = part if value is None else jnp.where(turns[px], part, value)
                 out[4 * z + pz, pl.ds(py, 4, 4), :] = own_rows(plan, value)
         return carry
 
     lax.fori_loop(0, 4, store, 0)
 
 
-def call(kernel, outs, scratch, *args):
+def call(plan, kernel, outs, scratch, *args, specs=None):
+    more = {} if specs is None else dict(in_specs=specs)
     return pl.pallas_call(
         kernel,
         out_shape=[jax.ShapeDtypeStruct(shape, F32) for shape in outs],
-        scratch_shapes=[pltpu.VMEM(shape, F32) for shape in scratch],
-        compiler_params=pltpu.CompilerParams(vmem_limit_bytes=48 * 1024 * 1024),
+        scratch_shapes=[
+            pltpu.VMEM(shape, F32) if isinstance(shape, tuple) else shape for shape in scratch
+        ],
+        compiler_params=pltpu.CompilerParams(
+            vmem_limit_bytes=(3 * plan.tile + plan.coarse[0] // 4) * 1024 * 1024
+        ),
+        **more,
     )(*args)
 
 
@@ -767,42 +792,54 @@
         beside = []
         for y in y_swaps:
             beside += [swap(residual, None, y, None), swap(mobility, None, y, None)]
-        even, odd = call(edges_kernel, [(4, 16, 128)] * 2, [], residual, mobility)
+        residual, mobility, even, odd, even_z, odd_z = call(
+            plan,
+            edges_kernel,
+            [(16, 16, 128)] * 2 + [(4, 16, 128)] * 2 + [(16 * (M_DEEP + R_DEEP), 128)] * 2,
+            [pltpu.SemaphoreType.DMA((2,))],
+            residual,
+            mobility,
+            specs=[pl.BlockSpec(memory_space=pltpu.HBM)] * 2,
+        )
+        z_own = [swap(even_z, 0, None, None), swap(odd_z, 1, None, None)]
         edges = [swap(even, None, None, 0), swap(odd, None, None, 1)]
         for y in y_swaps:
             edges += [swap(even, None, y, 0), swap(odd, None, y, 1)]
-        pieces = (residual, mobility, *beside, *edges)
         sends = call(
+            plan,
             lambda *refs: z_pack_kernel(plan, *refs),
             [(plan.payload, 128)] * 2,
             [],
-            table(edge_send_rows()),
-            *pieces,
+            *beside,
+            *edges,
         )
         arrived = [swap(sends[0], 0, None, None), swap(sends[1], 1, None, None)]
         (own,) = call(
+            plan,
             lambda *refs: own_kernel(plan, *refs),
             [(2, *full)],
             [(2, 16, plan.rows, 128), (2, 4, plan.rows, 128)],
-            table(edge_own_rows()),
-            *pieces,
+            residual,
+            mobility,
+            *beside,
+            *edges,
         )
-        coordinates = coordinate_rows(tile)
         chunk, *state = call(
+            plan,
             lambda *refs: down_kernel(plan, *refs),
             [(plan.devices, 8, 128)] + [full_rim] + [full] * 3 + [half_rim] + [half] * 3,
             [full, full_rim, full_rim, full]
             + [half, half_rim, half_rim, half]
             + [(2, 2, EDGE, plan.rows, 128), (2, 4, plan.rows, 128)],
-            table(edge_far_rows()),
-            coordinates,
             own,
+            *z_own,
             *arrived,
         )
         joined = lax.all_to_all(chunk, AXES, 0, 0, tiled=True)
         levels = [Level(plan, level) for level in range(2, LEVELS + 1)]
         margin = 0 if near == 1 else 16
         (out,) = call(
+            plan,
             lambda *refs: up_kernel(plan, *refs),
             [(16, 16, 128)],
             [full_rim] * 2
@@ -812,7 +849,6 @@
             + [(z2 + 2 * HALO, y2 + margin, 128)]
             + [level.shape for level in levels[:-1]]
             + [level.shape for level in levels[1:]],
-            coordinates,
             joined,
             *state,
         )

time: 57.7 us -> 51.6 us (0.89)
  Pallas kernels: 20.2 us -> 16.8 us
  starting transfers between devices: 9.48 us -> 11.4 us
  waiting for transfers between devices: 8.73 us -> 7.14 us
  blocking collectives: 15.7 us -> 14.2 us
  local copies, waits for them, and re-layouts: 3.21 us -> 1.81 us
    pallas_call x5, Pallas kernels: 20.2 us -> 16.8 us  [call(): pl.pallas_call(kernel, out_shape=[jax.ShapeDtypeStruct(shape, F32) for sh...]
    ppermute x8 -> x10, starting transfers between devices: 9.48 us -> 11.4 us  [swap(): return lax.ppermute(values, AXES, plan.pairs(swaps))]
    ppermute x8 -> x10, waiting for transfers between devices: 8.73 us -> 7.14 us  [swap(): return lax.ppermute(values, AXES, plan.pairs(swaps))]
    all_to_all x1, blocking collectives: 15.7 us -> 14.2 us  [on_device(): joined = lax.all_to_all(chunk, AXES, 0, 0, tiled=True)]
    unnamed x12 -> x4, local copies, waits for them, and re-layouts: 3.21 us -> 1.81 us
  transfers between devices with their start and end apart: 8 -> 10, of which waited for: 4 -> 4; matrix products, arithmetic and copies ran while one was open for 0% -> 0% of each run, Pallas kernels for 6% -> 7%
where the time goes in v3:
time: 51.6 us; the launch traced here: 51.4 us
  Pallas kernels  16.8 us (33%)
  blocking collectives  14.2 us (28%)
  starting transfers between devices  11.4 us (22%)
  waiting for transfers between devices  7.14 us (14%)
  local copies, waits for them, and re-layouts  1.81 us (4%)
    pallas_call x5, Pallas kernels, call(): pl.pallas_call(kernel, out_shape=[jax.ShapeDtypeStruct(shape, F32) for sh...  16.8 us
    all_to_all x1, blocking collectives, on_device(): joined = lax.all_to_all(chunk, AXES, 0, 0, tiled=True)  14.2 us
    ppermute x10, starting transfers between devices, swap(): return lax.ppermute(values, AXES, plan.pairs(swaps))  11.4 us
    ppermute x10, waiting for transfers between devices, swap(): return lax.ppermute(values, AXES, plan.pairs(swaps))  7.14 us
    unnamed x4, local copies, waits for them, and re-layouts  1.81 us
  transfers between devices with their start and end apart: 10, of which 4 were waited for; matrix products, arithmetic and copies ran while one was open for 0% of the time, Pallas kernels for 7%

profile of v3, /device:TPU:0, one launch (start us, length us, event | category | flops | bytes accessed | tf_op | source)
XLA Modules:
  0.0 51.4 jit_solution(4286389894795736717)
XLA Ops:
  0.0 3.0 %collective-permute-start = (f32[16,16,128]{2,1,0:T(8,128)}, f32[16,16,128]{2,1,0:T(8,128)S(1)}, u32[]{:S(2)}, u32[]{:S(2)}) collective-permute-start(f32[16,16,128]{2,1,0:T(8,128)} %r_hbm.1), channel_id=1, source_target_pairs={{0,4},{1,5},{2,6},{3,7},{4,0},{5,1},{6,2},{7,3},{8,12},{9,13},{10,... | collective-permute-start | bytes 393224 | tf_op jit(solution)/shard_map/ppermute | solution.py:788
  3.0 0.0 collective-permute-start.1
  3.0 0.0 copy-start
  3.0 0.9 %copy-done = f32[16,16,128]{2,1,0:T(8,128)S(1)} copy-done((f32[16,16,128]{2,1,0:T(8,128)S(1)}, f32[16,16,128]{2,1,0:T(8,128)}, u32[]{:S(2)}) %copy-start) | copy-done | bytes 131096
  3.9 0.0 copy-start.1
  3.9 0.9 %copy-done.1 = f32[16,16,128]{2,1,0:T(8,128)S(1)} copy-done((f32[16,16,128]{2,1,0:T(8,128)S(1)}, f32[16,16,128]{2,1,0:T(8,128)}, u32[]{:S(2)}) %copy-start.1) | copy-done | bytes 131096
  4.8 0.5 %shard_map.28 = (f32[16,16,128]{2,1,0:T(8,128)S(1)}, f32[16,16,128]{2,1,0:T(8,128)S(1)}, f32[4,16,128]{2,1,0:T(8,128)S(1)}, f32[4,16,128]{2,1,0:T(8,128)S(1)}, f...) custom-call(f32[16,16,128]{2,1,0:T(8,128)S(1)} %copy-done, f32[16,16,128]{2,1,0:T(8,128)S(1)} %copy-done.1), custom_call_target="tpu_custom_call" | custom-call | tf_op jit(solution)/shard_map/pallas_call | solution.py:764
  5.3 0.9 %collective-permute-start.4 = (f32[4,16,128]{2,1,0:T(8,128)S(1)}, f32[4,16,128]{2,1,0:T(8,128)S(1)}, u32[]{:S(2)}, u32[]{:S(2)}) collective-permute-start(f32[4,16,128]{2,1,0:T(8,128)S(1)} %get-tuple-element.24), channel_id=1, source_target_pairs={{0,5},{1,4},{2,7},{3,6},{4,1},{5,0},{6,3},{7,2},{8,13},{9,12},{10,... | collective-permute-start | bytes 98312 | tf_op jit(solution)/shard_map/ppermute | solution.py:788
  6.3 1.2 %collective-permute-start.2 = (f32[4,16,128]{2,1,0:T(8,128)S(1)}, f32[4,16,128]{2,1,0:T(8,128)S(1)}, u32[]{:S(2)}, u32[]{:S(2)}) collective-permute-start(f32[4,16,128]{2,1,0:T(8,128)S(1)} %get-tuple-element.24), channel_id=1, source_target_pairs={{0,1},{1,0},{2,3},{3,2},{4,5},{5,4},{6,7},{7,6},{8,9},{9,8},{10,11... | collective-permute-start | bytes 98312 | tf_op jit(solution)/shard_map/ppermute | solution.py:788
  7.5 1.0 %collective-permute-start.5 = (f32[4,16,128]{2,1,0:T(8,128)S(1)}, f32[4,16,128]{2,1,0:T(8,128)S(1)}, u32[]{:S(2)}, u32[]{:S(2)}) collective-permute-start(f32[4,16,128]{2,1,0:T(8,128)S(1)} %get-tuple-element.25), channel_id=1, source_target_pairs={{0,7},{1,6},{2,5},{3,4},{4,3},{5,2},{6,1},{7,0},{8,15},{9,14},{10,... | collective-permute-start | bytes 98312 | tf_op jit(solution)/shard_map/ppermute | solution.py:788
  8.6 1.6 %collective-permute-done.4.refs_6_.refs_4_ = f32[4,16,128]{2,1,0:T(8,128)S(1)} collective-permute-done((f32[4,16,128]{2,1,0:T(8,128)S(1)}, f32[4,16,128]{2,1,0:T(8,128)S(1)}, u32[]{:S(2)}, u32[]{:S(2)}) %collective-permute-start.4) | collective-permute-done | bytes 32800 | tf_op jit(solution)/shard_map/ppermute | solution.py:788
  10.1 1.2 %collective-permute-start.3 = (f32[4,16,128]{2,1,0:T(8,128)S(1)}, f32[4,16,128]{2,1,0:T(8,128)S(1)}, u32[]{:S(2)}, u32[]{:S(2)}) collective-permute-start(f32[4,16,128]{2,1,0:T(8,128)S(1)} %get-tuple-element.25), channel_id=1, source_target_pairs={{0,3},{1,2},{2,1},{3,0},{4,7},{5,6},{6,5},{7,4},{8,11},{9,10},{10,... | collective-permute-start | bytes 98312 | tf_op jit(solution)/shard_map/ppermute | solution.py:788
  11.3 0.0 collective-permute-done.2.refs_4_.refs_2_
  11.3 0.6 %collective-permute-done.5.refs_7_.refs_5_ = f32[4,16,128]{2,1,0:T(8,128)S(1)} collective-permute-done((f32[4,16,128]{2,1,0:T(8,128)S(1)}, f32[4,16,128]{2,1,0:T(8,128)S(1)}, u32[]{:S(2)}, u32[]{:S(2)}) %collective-permute-start.5) | collective-permute-done | bytes 32800 | tf_op jit(solution)/shard_map/ppermute | solution.py:788
  11.9 1.8 %collective-permute-done.3.refs_5_.refs_3_ = f32[4,16,128]{2,1,0:T(8,128)S(1)} collective-permute-done((f32[4,16,128]{2,1,0:T(8,128)S(1)}, f32[4,16,128]{2,1,0:T(8,128)S(1)}, u32[]{:S(2)}, u32[]{:S(2)}) %collective-permute-start.3) | collective-permute-done | bytes 32800 | tf_op jit(solution)/shard_map/ppermute | solution.py:788
  13.8 0.0 collective-permute-done.refs_2_.refs_0_
  13.8 0.0 collective-permute-done.1.refs_3_.refs_1_
  13.8 0.2 shard_map.30
  13.9 0.9 %collective-permute-start.8 = (f32[352,128]{1,0:T(8,128)S(1)}, f32[352,128]{1,0:T(8,128)S(1)}, u32[]{:S(2)}, u32[]{:S(2)}) collective-permute-start(f32[352,128]{1,0:T(8,128)S(1)} %get-tuple-element.28), channel_id=1, source_target_pairs={{0,8},{1,9},{2,10},{3,11},{4,12},{5,13},{6,14},{7,15},{8,0},{9,1},... | collective-permute-start | bytes 540680 | tf_op jit(solution)/shard_map/ppermute | solution.py:788
  14.8 0.3 collective-permute-start.9
  15.1 2.8 %collective-permute-start.6 = (f32[336,128]{1,0:T(8,128)S(1)}, f32[336,128]{1,0:T(8,128)S(1)}, u32[]{:S(2)}, u32[]{:S(2)}) collective-permute-start(f32[336,128]{1,0:T(8,128)S(1)} %get-tuple-element.26), channel_id=1, source_target_pairs={{0,8},{1,9},{2,10},{3,11},{4,12},{5,13},{6,14},{7,15},{8,0},{9,1},... | collective-permute-start | bytes 516104 | tf_op jit(solution)/shard_map/ppermute | solution.py:788
  17.9 0.0 collective-permute-start.7
  17.9 3.2 %shard_map.29.refs_0_ = f32[2,4,4,4,8,384]{5,4,3,2,1,0:T(8,128)S(1)} custom-call(f32[16,16,128]{2,1,0:T(8,128)S(1)} %get-tuple-element.22.refs_0_, f32[16,16,128]{2,1,0:T(8,128)S(1)} %get-tuple-element.23.refs_1_, f32[16,16,128]{2,1,0:T(8,128)S(1)} %collective-permute-done.refs_2_.refs_0_, f32[16,16,128]{2,1,0:T(8,128)S(1)} %collective-permute-done.1.refs_3_.refs_1_, ...), custom_call_target="tpu_custom_call" | custom-call | tf_op jit(solution)/shard_map/pallas_call | solution.py:764
  21.1 3.1 %collective-permute-done.6.refs_1_ = f32[336,128]{1,0:T(8,128)S(1)} collective-permute-done((f32[336,128]{1,0:T(8,128)S(1)}, f32[336,128]{1,0:T(8,128)S(1)}, u32[]{:S(2)}, u32[]{:S(2)}) %collective-permute-start.6) | collective-permute-done | bytes 172064 | tf_op jit(solution)/shard_map/ppermute | solution.py:788
  24.2 0.0 collective-permute-done.7.refs_2_
  24.3 0.0 collective-permute-done.8.refs_3_
  24.3 0.0 collective-permute-done.9.refs_4_
  24.3 6.3 %shard_map.31 = (f32[32,8,128]{2,1,0:T(8,128)S(1)}, f32[6,6,6,8,384]{4,3,2,1,0:T(8,128)S(1)}, f32[4,4,4,8,384]{4,3,2,1,0:T(8,128)S(1)}, f32[4,4,4,8,384]{4,3,2,1...) custom-call(f32[2,4,4,4,8,384]{5,4,3,2,1,0:T(8,128)S(1)} %shard_map., ...), custom_call_target="tpu_custom_call" | custom-call | tf_op jit(solution)/shard_map/pallas_call | solution.py:764
  30.5 14.2 %all_to_all.5.refs_0_ = f32[32,8,128]{2,1,0:T(8,128)S(1)} all-to-all(f32[32,8,128]{2,1,0:T(8,128)S(1)} %get-tuple-element.30), channel_id=1, replica_groups=mesh['grp'=4,'gy'=2,'gx'=4] {'grp','gy','gx'}, dimensions={0} | all-to-all | bytes 262144 | tf_op jit(solution)/shard_map/all_to_all | solution.py:838
  44.7 6.7 %shard_map.32 = f32[16,16,128]{2,1,0:T(8,128)} custom-call(f32[32,8,128]{2,1,0:T(8,128)S(1)} %all_to_all.5.refs_0_, f32[6,6,6,8,384]{4,3,2,1,0:T(8,128)S(1)} %get-tuple-element.31.refs_1_, f32[4,4,4,8,384]{4,3,2,1,0:T(8,128)S(1)} %get-tuple-element.32.refs_2_, f32[4,4,4,8,384]{4,3,2,1,0:T(8,128)S(1)} %get-tuple-element.33.refs_3_, ...), custom_call_target="tpu_custom_call" | custom-call | tf_op jit(solution)/shard_map/pallas_call | solution.py:764
Async XLA Ops:
  0.0 13.8 %collective-permute-start = (f32[16,16,128]{2,1,0:T(8,128)}, f32[16,16,128]{2,1,0:T(8,128)S(1)}, u32[]{:S(2)}, u32[]{:S(2)}) collective-permute-start(f32[16,16,128]{2,1,0:T(8,128)} %r_hbm.1), channel_id=1, source_target_pairs={{0,4},{1,5},{2,6},{3,7},{4,0},{5,1},{6,2},{7,3},{8,12},{9,13},{10,... | collective-permute-start | bytes 393224 | tf_op jit(solution)/shard_map/ppermute | solution.py:788
  3.0 10.8 %collective-permute-start.1 = (f32[16,16,128]{2,1,0:T(8,128)}, f32[16,16,128]{2,1,0:T(8,128)S(1)}, u32[]{:S(2)}, u32[]{:S(2)}) collective-permute-start(f32[16,16,128]{2,1,0:T(8,128)} %m_hbm.1), channel_id=1, source_target_pairs={{0,4},{1,5},{2,6},{3,7},{4,0},{5,1},{6,2},{7,3},{8,12},{9,13},{10,... | collective-permute-start | bytes 393224 | tf_op jit(solution)/shard_map/ppermute | solution.py:788
  3.0 0.9 %copy-start = (f32[16,16,128]{2,1,0:T(8,128)S(1)}, f32[16,16,128]{2,1,0:T(8,128)}, u32[]{:S(2)}) copy-start(f32[16,16,128]{2,1,0:T(8,128)} %r_hbm.1) | copy-start | bytes 393220
  3.9 0.9 %copy-start.1 = (f32[16,16,128]{2,1,0:T(8,128)S(1)}, f32[16,16,128]{2,1,0:T(8,128)}, u32[]{:S(2)}) copy-start(f32[16,16,128]{2,1,0:T(8,128)} %m_hbm.1) | copy-start | bytes 393220
  5.3 4.8 %collective-permute-start.4 = (f32[4,16,128]{2,1,0:T(8,128)S(1)}, f32[4,16,128]{2,1,0:T(8,128)S(1)}, u32[]{:S(2)}, u32[]{:S(2)}) collective-permute-start(f32[4,16,128]{2,1,0:T(8,128)S(1)} %get-tuple-element.24), channel_id=1, source_target_pairs={{0,5},{1,4},{2,7},{3,6},{4,1},{5,0},{6,3},{7,2},{8,13},{9,12},{10,... | collective-permute-start | bytes 98312 | tf_op jit(solution)/shard_map/ppermute | solution.py:788
  6.3 5.1 %collective-permute-start.2 = (f32[4,16,128]{2,1,0:T(8,128)S(1)}, f32[4,16,128]{2,1,0:T(8,128)S(1)}, u32[]{:S(2)}, u32[]{:S(2)}) collective-permute-start(f32[4,16,128]{2,1,0:T(8,128)S(1)} %get-tuple-element.24), channel_id=1, source_target_pairs={{0,1},{1,0},{2,3},{3,2},{4,5},{5,4},{6,7},{7,6},{8,9},{9,8},{10,11... | collective-permute-start | bytes 98312 | tf_op jit(solution)/shard_map/ppermute | solution.py:788
  7.5 4.4 %collective-permute-start.5 = (f32[4,16,128]{2,1,0:T(8,128)S(1)}, f32[4,16,128]{2,1,0:T(8,128)S(1)}, u32[]{:S(2)}, u32[]{:S(2)}) collective-permute-start(f32[4,16,128]{2,1,0:T(8,128)S(1)} %get-tuple-element.25), channel_id=1, source_target_pairs={{0,7},{1,6},{2,5},{3,4},{4,3},{5,2},{6,1},{7,0},{8,15},{9,14},{10,... | collective-permute-start | bytes 98312 | tf_op jit(solution)/shard_map/ppermute | solution.py:788
  10.1 3.6 %collective-permute-start.3 = (f32[4,16,128]{2,1,0:T(8,128)S(1)}, f32[4,16,128]{2,1,0:T(8,128)S(1)}, u32[]{:S(2)}, u32[]{:S(2)}) collective-permute-start(f32[4,16,128]{2,1,0:T(8,128)S(1)} %get-tuple-element.25), channel_id=1, source_target_pairs={{0,3},{1,2},{2,1},{3,0},{4,7},{5,6},{6,5},{7,4},{8,11},{9,10},{10,... | collective-permute-start | bytes 98312 | tf_op jit(solution)/shard_map/ppermute | solution.py:788
  13.9 10.3 %collective-permute-start.8 = (f32[352,128]{1,0:T(8,128)S(1)}, f32[352,128]{1,0:T(8,128)S(1)}, u32[]{:S(2)}, u32[]{:S(2)}) collective-permute-start(f32[352,128]{1,0:T(8,128)S(1)} %get-tuple-element.28), channel_id=1, source_target_pairs={{0,8},{1,9},{2,10},{3,11},{4,12},{5,13},{6,14},{7,15},{8,0},{9,1},... | collective-permute-start | bytes 540680 | tf_op jit(solution)/shard_map/ppermute | solution.py:788
  14.8 9.5 %collective-permute-start.9 = (f32[352,128]{1,0:T(8,128)S(1)}, f32[352,128]{1,0:T(8,128)S(1)}, u32[]{:S(2)}, u32[]{:S(2)}) collective-permute-start(f32[352,128]{1,0:T(8,128)S(1)} %get-tuple-element.29), channel_id=1, source_target_pairs={{0,1},{1,0},{2,3},{3,2},{4,5},{5,4},{6,7},{7,6},{8,16},{9,17},{10,... | collective-permute-start | bytes 540680 | tf_op jit(solution)/shard_map/ppermute | solution.py:788
  15.1 9.1 %collective-permute-start.6 = (f32[336,128]{1,0:T(8,128)S(1)}, f32[336,128]{1,0:T(8,128)S(1)}, u32[]{:S(2)}, u32[]{:S(2)}) collective-permute-start(f32[336,128]{1,0:T(8,128)S(1)} %get-tuple-element.26), channel_id=1, source_target_pairs={{0,8},{1,9},{2,10},{3,11},{4,12},{5,13},{6,14},{7,15},{8,0},{9,1},... | collective-permute-start | bytes 516104 | tf_op jit(solution)/shard_map/ppermute | solution.py:788
  17.9 6.3 %collective-permute-start.7 = (f32[336,128]{1,0:T(8,128)S(1)}, f32[336,128]{1,0:T(8,128)S(1)}, u32[]{:S(2)}, u32[]{:S(2)}) collective-permute-start(f32[336,128]{1,0:T(8,128)S(1)} %get-tuple-element.27), channel_id=1, source_target_pairs={{0,1},{1,0},{2,3},{3,2},{4,5},{5,4},{6,7},{7,6},{8,16},{9,17},{10,... | collective-permute-start | bytes 516104 | tf_op jit(solution)/shard_map/ppermute | solution.py:788

commit v4 on v3

--- a/solution.py
+++ b/solution.py
@@ -18,6 +18,8 @@
 EDGE = 4 * HALO
 M_DEEP, M_FAR, R_DEEP, R_FAR = 11, 4, 10, 3
 M_EDGE, R_EDGE = 11, 10
+Y_FAR = 3
+Y_ROWS = 16 * (8 + Y_FAR)
 
 
 def lane_iota(rows=8):
@@ -150,47 +152,71 @@
     return pl.ds(pl.multiple_of(start, 8), size)
 
 
-def edges_kernel(r_hbm, m_hbm, r_ref, m_ref, even_ref, odd_ref, even_z_ref, odd_z_ref, sems):
-    copies = [
-        pltpu.make_async_copy(r_hbm, r_ref, sems.at[0]),
-        pltpu.make_async_copy(m_hbm, m_ref, sems.at[1]),
-    ]
-    for copy in copies:
-        copy.start()
-    for copy in copies:
-        copy.wait()
+def first_kernel(plan, cells_ref, *outs):
     z_even = is_even("grp")
-    for swap, out in enumerate((even_z_ref, odd_z_ref)):
+    for swap, out in enumerate(outs[:2]):
         top = z_even if swap == 0 else jnp.logical_not(z_even)
         row = 0
-        for ref, deep in ((m_ref, M_DEEP), (r_ref, R_DEEP)):
+        for a, deep in ((1, M_DEEP), (0, R_DEEP)):
             for d in range(1, deep + 1):
-                out[row : row + 16, :] = ref[jnp.where(top, 16 - d, d - 1)]
+                out[row : row + 16, :] = cells_ref[a, jnp.where(top, 16 - d, d - 1)]
                 row += 16
+    for out, (side, _) in zip(outs[2:], plan.y_places()[1]):
+        last = side == 1
+        for a in range(2):
+            near, far = a * Y_ROWS, a * Y_ROWS + 128
+            for plane in range(16):
+                cells = cells_ref[a, plane]
+                rows = jnp.where(last, cells[8:16], cells[0:8])
+                out[near + 8 * plane : near + 8 * plane + 8, :] = rows
+                rows = jnp.where(last, cells[8 - Y_FAR : 8], cells[8 : 8 + Y_FAR])
+                out[far + Y_FAR * plane : far + Y_FAR * (plane + 1), :] = rows
+
+
+def edges_kernel(plan, *refs):
+    cells_ref = refs[0]
+    arrived = refs[1 : 1 + plan.near]
+    beside = refs[1 + plan.near : 1 + 2 * plan.near]
+    even_ref, odd_ref = refs[-2:]
+    own_row, places = plan.y_places()
     even = is_even("gx")
-    for pz in range(4):
-        for half in range(2):
-            to_right = jnp.zeros((8, 128), F32)
-            to_left = jnp.zeros((8, 128), F32)
-            for a, ref in enumerate((r_ref, m_ref)):
-                for z in range(4):
-                    cells = ref[4 * z + pz, 8 * half : 8 * half + 8, :]
-                    base = a * 48 + z * 12
-                    here = between(base, base + EDGE)
-                    shift = (base - (128 - EDGE)) % 128
-                    to_right = jnp.where(here, pltpu.roll(cells, shift, 1), to_right)
-                    to_left = jnp.where(here, pltpu.roll(cells, base, 1), to_left)
-            rows = slice(8 * half, 8 * half + 8)
-            even_ref[pz, rows, :] = jnp.where(even, to_right, to_left)
-            odd_ref[pz, rows, :] = jnp.where(even, to_left, to_right)
+    for ref, out, (side, _) in zip(arrived, beside, places):
+        following = side == 1
+        for a in range(2):
+            near, far = a * Y_ROWS, a * Y_ROWS + 128
+            for plane in range(16):
+                rows = ref[near + 8 * plane : near + 8 * plane + 8, :]
+                more = ref[far + Y_FAR * plane : far + Y_FAR * (plane + 1), :]
+                none = jnp.zeros((8 - Y_FAR, 128), F32)
+                after = jnp.concatenate([more, none], axis=0)
+                before = jnp.concatenate([none, more], axis=0)
+                out[a, plane, 0:8, :] = jnp.where(following, rows, before)
+                out[a, plane, 8:16, :] = jnp.where(following, after, rows)
+    for i, block in enumerate((cells_ref, *beside)):
+        start = own_row if i == 0 else places[i - 1][1]
+        for pz in range(4):
+            for half in range(2):
+                to_right = jnp.zeros((8, 128), F32)
+                to_left = jnp.zeros((8, 128), F32)
+                for a in range(2):
+                    for z in range(4):
+                        cells = block[a, 4 * z + pz, 8 * half : 8 * half + 8, :]
+                        base = a * 48 + z * 12
+                        here = between(base, base + EDGE)
+                        shift = (base - (128 - EDGE)) % 128
+                        to_right = jnp.where(here, pltpu.roll(cells, shift, 1), to_right)
+                        to_left = jnp.where(here, pltpu.roll(cells, base, 1), to_left)
+                rows = at(start + 8 * half, 8)
+                even_ref[pz, rows, :] = jnp.where(even, to_right, to_left)
+                odd_ref[pz, rows, :] = jnp.where(even, to_left, to_right)
 
 
 def z_pack_kernel(plan, *refs):
     near = plan.near
-    beside = [refs[2 * i : 2 + 2 * i] for i in range(near)]
-    edges = [refs[2 * near + 2 * i : 2 + 2 * near + 2 * i] for i in range(1 + near)]
+    beside = refs[:near]
+    x_even_ref, x_odd_ref = refs[near : near + 2]
     outs = refs[-2:]
-    own_row, places = plan.y_places()
+    places = plan.y_places()[1]
     x_even = is_even("gx")
     z_even = is_even("grp")
     lanes_0, use_right = edge_send_lanes()
@@ -205,22 +231,18 @@
                 row = (d - 1) * plan.z_rows
                 for i, (side, _) in enumerate(places):
                     to = start + row + 8 * i
-                    out[to : to + 8, :] = beside[i][a][plane, at(8 * (1 - side), 8), :]
+                    out[to : to + 8, :] = beside[i][a, plane, at(8 * (1 - side), 8), :]
                     if d <= far:
                         to = far_start + row + 8 * i
-                        out[to : to + 8, :] = beside[i][a][plane, at(8 * side, 8), :]
+                        out[to : to + 8, :] = beside[i][a, plane, at(8 * side, 8), :]
         lanes = lanes_0 + jnp.where(top, 12, 0)
-        for i in range(1 + near):
-            base = own_row if i == 0 else places[i - 1][1]
-            even_ref, odd_ref = edges[i]
-            for pz in range(4):
-                for half in range(2):
-                    rows = slice(8 * half, 8 * half + 8)
-                    even, odd = even_ref[pz, rows, :], odd_ref[pz, rows, :]
-                    left = gather(jnp.where(x_even, odd, even), lanes)
-                    right = gather(jnp.where(x_even, even, odd), lanes)
-                    to = at(plan.starts[4] + pz * plan.rows + base + 8 * half, 8)
-                    out[to, :] = jnp.where(use_right, right, left)
+        for pz in range(4):
+            for row in range(0, plan.rows, 8):
+                even, odd = x_even_ref[pz, row : row + 8, :], x_odd_ref[pz, row : row + 8, :]
+                left = gather(jnp.where(x_even, odd, even), lanes)
+                right = gather(jnp.where(x_even, even, odd), lanes)
+                to = plan.starts[4] + pz * plan.rows + row
+                out[to : to + 8, :] = jnp.where(use_right, right, left)
 
 
 def padded_rows(plan, cells):
@@ -237,20 +259,18 @@
 
 def own_kernel(plan, *refs):
     near = plan.near
-    r_ref, m_ref = refs[:2]
-    beside = [refs[2 + 2 * i : 4 + 2 * i] for i in range(near)]
-    edges = [refs[2 + 2 * near + 2 * i : 4 + 2 * near + 2 * i] for i in range(1 + near)]
+    cells_ref, *beside = refs[: 1 + near]
+    x_even_ref, x_odd_ref = refs[1 + near : 3 + near]
     out, planes, sides = refs[-3:]
     tile = plan.tile
     own_row, places = plan.y_places()
     x_even = is_even("gx")
-    blocks = [(own_row, (r_ref, m_ref))] + [(place[1], b) for place, b in zip(places, beside)]
-    for i, (base, pair) in enumerate(blocks):
-        for a in range(2):
-            planes[a, :, at(base, 16), :] = pair[a][...]
-        even, odd = edges[i][0][...], edges[i][1][...]
-        sides[0, :, at(base, 16), :] = jnp.where(x_even, odd, even)
-        sides[1, :, at(base, 16), :] = jnp.where(x_even, even, odd)
+    planes[:, :, at(own_row, 16), :] = cells_ref[...]
+    for (_, base), block in zip(places, beside):
+        planes[:, :, at(base, 16), :] = block[...]
+    even, odd = x_even_ref[...], x_odd_ref[...]
+    sides[0] = jnp.where(x_even, odd, even)
+    sides[1] = jnp.where(x_even, even, odd)
 
     offsets = [(z + HALO) * XW + HALO for z in range(4)]
     index = [[every_lane(offset, px, tile) for px in range(4)] for offset in offsets]
@@ -759,18 +779,14 @@
     lax.fori_loop(0, 4, store, 0)
 
 
-def call(plan, kernel, outs, scratch, *args, specs=None):
-    more = {} if specs is None else dict(in_specs=specs)
+def call(plan, kernel, outs, scratch, *args):
     return pl.pallas_call(
         kernel,
         out_shape=[jax.ShapeDtypeStruct(shape, F32) for shape in outs],
-        scratch_shapes=[
-            pltpu.VMEM(shape, F32) if isinstance(shape, tuple) else shape for shape in scratch
-        ],
+        scratch_shapes=[pltpu.VMEM(shape, F32) for shape in scratch],
         compiler_params=pltpu.CompilerParams(
             vmem_limit_bytes=(3 * plan.tile + plan.coarse[0] // 4) * 1024 * 1024
         ),
-        **more,
     )(*args)
 
 
@@ -782,29 +798,31 @@
     half = (2, 2, 2, tile, LW)
     full_rim = (6, 6, 6, tile, LW)
     half_rim = (4, 4, 4, tile, LW)
-    y_swaps = list(range(near))
 
     def swap(values, *swaps):
         return lax.ppermute(values, AXES, plan.pairs(swaps))
 
     def on_device(residual, mobility):
         assert residual.shape == (16, 16, 128)
-        beside = []
-        for y in y_swaps:
-            beside += [swap(residual, None, y, None), swap(mobility, None, y, None)]
-        residual, mobility, even, odd, even_z, odd_z = call(
+        cells = jnp.stack([residual, mobility])
+        even, odd, *rows = call(
             plan,
-            edges_kernel,
-            [(16, 16, 128)] * 2 + [(4, 16, 128)] * 2 + [(16 * (M_DEEP + R_DEEP), 128)] * 2,
-            [pltpu.SemaphoreType.DMA((2,))],
-            residual,
-            mobility,
-            specs=[pl.BlockSpec(memory_space=pltpu.HBM)] * 2,
+            lambda *refs: first_kernel(plan, *refs),
+            [(16 * (M_DEEP + R_DEEP), 128)] * 2 + [(2 * Y_ROWS, 128)] * near,
+            [],
+            cells,
         )
-        z_own = [swap(even_z, 0, None, None), swap(odd_z, 1, None, None)]
+        arrived = [swap(values, None, y, None) for y, values in enumerate(rows)]
+        z_own = [swap(even, 0, None, None), swap(odd, 1, None, None)]
+        *beside, even, odd = call(
+            plan,
+            lambda *refs: edges_kernel(plan, *refs),
+            [(2, 16, 16, 128)] * near + [(4, plan.rows, 128)] * 2,
+            [],
+            cells,
+            *arrived,
+        )
         edges = [swap(even, None, None, 0), swap(odd, None, None, 1)]
-        for y in y_swaps:
-            edges += [swap(even, None, y, 0), swap(odd, None, y, 1)]
         sends = call(
             plan,
             lambda *refs: z_pack_kernel(plan, *refs),
@@ -812,6 +830,7 @@
             [],
             *beside,
             *edges,
+            *z_own,
         )
         arrived = [swap(sends[0], 0, None, None), swap(sends[1], 1, None, None)]
         (own,) = call(
@@ -819,8 +838,7 @@
             lambda *refs: own_kernel(plan, *refs),
             [(2, *full)],
             [(2, 16, plan.rows, 128), (2, 4, plan.rows, 128)],
-            residual,
-            mobility,
+            cells,
             *beside,
             *edges,
         )

time: 51.6 us -> 47.6 us (0.922)
  starting transfers between devices: 11.4 us -> 8.48 us
  local copies, waits for them, and re-layouts: 1.81 us -> 0 us
  other arithmetic: 0 us -> 0.99 us
    ppermute x10 -> x7, starting transfers between devices: 11.4 us -> 8.48 us  [swap(): return lax.ppermute(values, AXES, plan.pairs(swaps))]
    unnamed x4 -> x0, local copies, waits for them, and re-layouts: 1.81 us -> none
    another operation x0 -> x1, other arithmetic: none -> 0.99 us  [on_device(): cells = jnp.stack([residual, mobility])]
    ppermute x10 -> x7, waiting for transfers between devices: 7.14 us -> 6.85 us  [swap(): return lax.ppermute(values, AXES, plan.pairs(swaps))]
    pallas_call x5 -> x6, Pallas kernels: 16.8 us -> 16.7 us  [call(): pl.pallas_call(kernel, out_shape=[jax.ShapeDtypeStruct(shape, F32) for sh...]
  transfers between devices with their start and end apart: 10 -> 7, of which waited for: 4 -> 3; matrix products, arithmetic and copies ran while one was open for 0% -> 0% of each run, Pallas kernels for 7% -> 7%
where the time goes in v4:
time: 47.6 us; the launch traced here: 47.4 us
  Pallas kernels  16.7 us (35%)
  blocking collectives  14.3 us (30%)
  starting transfers between devices  8.48 us (18%)
  waiting for transfers between devices  6.85 us (14%)
  other arithmetic  0.99 us (2%)
    pallas_call x6, Pallas kernels, call(): pl.pallas_call(kernel, out_shape=[jax.ShapeDtypeStruct(shape, F32) for sh...  16.7 us
    all_to_all x1, blocking collectives, on_device(): joined = lax.all_to_all(chunk, AXES, 0, 0, tiled=True)  14.3 us
    ppermute x7, starting transfers between devices, swap(): return lax.ppermute(values, AXES, plan.pairs(swaps))  8.48 us
    ppermute x7, waiting for transfers between devices, swap(): return lax.ppermute(values, AXES, plan.pairs(swaps))  6.85 us
    another operation x1, other arithmetic, on_device(): cells = jnp.stack([residual, mobility])  0.99 us
  transfers between devices with their start and end apart: 7, of which 3 were waited for; matrix products, arithmetic and copies ran while one was open for 0% of the time, Pallas kernels for 7%

profile of v4, /device:TPU:0, one launch (start us, length us, event | category | flops | bytes accessed | tf_op | source)
XLA Modules:
  0.0 47.4 jit_solution(7986823330857569099)
XLA Ops:
  0.0 1.0 %pad_maximum_fusion.refs_0_ = f32[2,16,16,128]{3,2,1,0:T(8,128)S(1)} fusion(f32[1,16,16,128]{3,2,1,0:T(8,128)} %bitcast.2, f32[1,16,16,128]{3,2,1,0:T(8,128)} %bitcast.3), kind=kLoop, calls=%fused_computation | loop fusion | flops 65536 | bytes 524288 | tf_op jit(solution)/shard_map/stack | solution.py:807
  1.0 0.1 shard_map.28
  1.1 3.0 %collective-permute-start = (f32[352,128]{1,0:T(8,128)S(1)}, f32[352,128]{1,0:T(8,128)S(1)}, u32[]{:S(2)}, u32[]{:S(2)}) collective-permute-start(f32[352,128]{1,0:T(8,128)S(1)} %get-tuple-element.22), channel_id=1, source_target_pairs={{0,4},{1,5},{2,6},{3,7},{4,0},{5,1},{6,2},{7,3},{8,12},{9,13},{10,... | collective-permute-start | bytes 540680 | tf_op jit(solution)/shard_map/ppermute | solution.py:803
  4.1 1.6 %collective-permute-start.3 = (f32[336,128]{1,0:T(8,128)S(1)}, f32[336,128]{1,0:T(8,128)S(1)}, u32[]{:S(2)}, u32[]{:S(2)}) collective-permute-start(f32[336,128]{1,0:T(8,128)S(1)} %get-tuple-element.26), channel_id=1, source_target_pairs={{0,8},{1,9},{2,10},{3,11},{4,12},{5,13},{6,14},{7,15},{8,0},{9,1},... | collective-permute-start | bytes 516104 | tf_op jit(solution)/shard_map/ppermute | solution.py:803
  5.7 0.0 collective-permute-start.4
  5.7 3.0 %collective-permute-done.refs_1_ = f32[352,128]{1,0:T(8,128)S(1)} collective-permute-done((f32[352,128]{1,0:T(8,128)S(1)}, f32[352,128]{1,0:T(8,128)S(1)}, u32[]{:S(2)}, u32[]{:S(2)}) %collective-permute-start) | collective-permute-done | bytes 180256 | tf_op jit(solution)/shard_map/ppermute | solution.py:803
  8.6 0.3 shard_map.29
  9.0 0.1 collective-permute-start.1
  9.0 1.8 %collective-permute-start.2 = (f32[4,32,128]{2,1,0:T(8,128)S(1)}, f32[4,32,128]{2,1,0:T(8,128)S(1)}, u32[]{:S(2)}, u32[]{:S(2)}) collective-permute-start(f32[4,32,128]{2,1,0:T(8,128)S(1)} %get-tuple-element.25), channel_id=1, source_target_pairs={{0,3},{1,2},{2,1},{3,0},{4,7},{5,6},{6,5},{7,4},{8,11},{9,10},{10,... | collective-permute-start | bytes 196616 | tf_op jit(solution)/shard_map/ppermute | solution.py:803
  10.9 0.0 collective-permute-done.3.refs_3_.refs_1_
  10.9 0.0 collective-permute-done.4.refs_4_.refs_2_
  10.9 0.0 collective-permute-done.1.refs_2_.refs_1_
  10.9 2.1 %collective-permute-done.2.refs_3_.refs_2_ = f32[4,32,128]{2,1,0:T(8,128)S(1)} collective-permute-done((f32[4,32,128]{2,1,0:T(8,128)S(1)}, f32[4,32,128]{2,1,0:T(8,128)S(1)}, u32[]{:S(2)}, u32[]{:S(2)}) %collective-permute-start.2) | collective-permute-done | bytes 65568 | tf_op jit(solution)/shard_map/ppermute | solution.py:803
  12.9 0.2 shard_map.31
  13.1 1.9 %collective-permute-start.5 = (f32[352,128]{1,0:T(8,128)S(1)}, f32[352,128]{1,0:T(8,128)S(1)}, u32[]{:S(2)}, u32[]{:S(2)}) collective-permute-start(f32[352,128]{1,0:T(8,128)S(1)} %get-tuple-element.28), channel_id=1, source_target_pairs={{0,8},{1,9},{2,10},{3,11},{4,12},{5,13},{6,14},{7,15},{8,0},{9,1},... | collective-permute-start | bytes 540680 | tf_op jit(solution)/shard_map/ppermute | solution.py:803
  15.0 0.1 collective-permute-start.6
  15.1 3.2 %shard_map.30.refs_0_ = f32[2,4,4,4,8,384]{5,4,3,2,1,0:T(8,128)S(1)} custom-call(f32[2,16,16,128]{3,2,1,0:T(8,128)S(1)} %pad_maximum_fusion.refs_0_, f32[2,16,16,128]{3,2,1,0:T(8,128)S(1)} %get-tuple-element.23.refs_1_.refs_0_, f32[4,32,128]{2,1,0:T(8,128)S(1)} %collective-permute-done.1.refs_2_.refs_1_, f32[4,32,128]{2,1,0:T(8,128)S(1)} %collective-permute-done.2.refs_3_.refs_2_), custom_call_target="tpu_custom_call" | custom-call | tf_op jit(solution)/shard_map/pallas_call | solution.py:783
  18.3 1.8 %collective-permute-done.5.refs_3_ = f32[352,128]{1,0:T(8,128)S(1)} collective-permute-done((f32[352,128]{1,0:T(8,128)S(1)}, f32[352,128]{1,0:T(8,128)S(1)}, u32[]{:S(2)}, u32[]{:S(2)}) %collective-permute-start.5) | collective-permute-done | bytes 180256 | tf_op jit(solution)/shard_map/ppermute | solution.py:803
  20.1 0.0 collective-permute-done.6.refs_4_
  20.1 6.3 %shard_map.32 = (f32[32,8,128]{2,1,0:T(8,128)S(1)}, f32[6,6,6,8,384]{4,3,2,1,0:T(8,128)S(1)}, f32[4,4,4,8,384]{4,3,2,1,0:T(8,128)S(1)}, f32[4,4,4,8,384]{4,3,2,1...) custom-call(f32[2,4,4,4,8,384]{5,4,3,2,1,0:T(8,128)S(1)} %shard_map., ...), custom_call_target="tpu_custom_call" | custom-call | tf_op jit(solution)/shard_map/pallas_call | solution.py:783
  26.3 14.3 %all_to_all.5.refs_0_ = f32[32,8,128]{2,1,0:T(8,128)S(1)} all-to-all(f32[32,8,128]{2,1,0:T(8,128)S(1)} %get-tuple-element.30), channel_id=1, replica_groups=mesh['grp'=4,'gy'=2,'gx'=4] {'grp','gy','gx'}, dimensions={0} | all-to-all | bytes 262144 | tf_op jit(solution)/shard_map/all_to_all | solution.py:856
  40.7 6.7 %shard_map.33 = f32[16,16,128]{2,1,0:T(8,128)} custom-call(f32[32,8,128]{2,1,0:T(8,128)S(1)} %all_to_all.5.refs_0_, f32[6,6,6,8,384]{4,3,2,1,0:T(8,128)S(1)} %get-tuple-element.31.refs_1_, f32[4,4,4,8,384]{4,3,2,1,0:T(8,128)S(1)} %get-tuple-element.32.refs_2_, f32[4,4,4,8,384]{4,3,2,1,0:T(8,128)S(1)} %get-tuple-element.33.refs_3_, ...), custom_call_target="tpu_custom_call" | custom-call | tf_op jit(solution)/shard_map/pallas_call | solution.py:783
Async XLA Ops:
  1.1 7.6 %collective-permute-start = (f32[352,128]{1,0:T(8,128)S(1)}, f32[352,128]{1,0:T(8,128)S(1)}, u32[]{:S(2)}, u32[]{:S(2)}) collective-permute-start(f32[352,128]{1,0:T(8,128)S(1)} %get-tuple-element.22), channel_id=1, source_target_pairs={{0,4},{1,5},{2,6},{3,7},{4,0},{5,1},{6,2},{7,3},{8,12},{9,13},{10,... | collective-permute-start | bytes 540680 | tf_op jit(solution)/shard_map/ppermute | solution.py:803
  4.1 6.8 %collective-permute-start.3 = (f32[336,128]{1,0:T(8,128)S(1)}, f32[336,128]{1,0:T(8,128)S(1)}, u32[]{:S(2)}, u32[]{:S(2)}) collective-permute-start(f32[336,128]{1,0:T(8,128)S(1)} %get-tuple-element.26), channel_id=1, source_target_pairs={{0,8},{1,9},{2,10},{3,11},{4,12},{5,13},{6,14},{7,15},{8,0},{9,1},... | collective-permute-start | bytes 516104 | tf_op jit(solution)/shard_map/ppermute | solution.py:803
  5.7 5.2 %collective-permute-start.4 = (f32[336,128]{1,0:T(8,128)S(1)}, f32[336,128]{1,0:T(8,128)S(1)}, u32[]{:S(2)}, u32[]{:S(2)}) collective-permute-start(f32[336,128]{1,0:T(8,128)S(1)} %get-tuple-element.27), channel_id=1, source_target_pairs={{0,1},{1,0},{2,3},{3,2},{4,5},{5,4},{6,7},{7,6},{8,16},{9,17},{10,... | collective-permute-start | bytes 516104 | tf_op jit(solution)/shard_map/ppermute | solution.py:803
  9.0 1.9 %collective-permute-start.1 = (f32[4,32,128]{2,1,0:T(8,128)S(1)}, f32[4,32,128]{2,1,0:T(8,128)S(1)}, u32[]{:S(2)}, u32[]{:S(2)}) collective-permute-start(f32[4,32,128]{2,1,0:T(8,128)S(1)} %get-tuple-element.24), channel_id=1, source_target_pairs={{0,1},{1,0},{2,3},{3,2},{4,5},{5,4},{6,7},{7,6},{8,9},{9,8},{10,11... | collective-permute-start | bytes 196616 | tf_op jit(solution)/shard_map/ppermute | solution.py:803
  9.0 3.9 %collective-permute-start.2 = (f32[4,32,128]{2,1,0:T(8,128)S(1)}, f32[4,32,128]{2,1,0:T(8,128)S(1)}, u32[]{:S(2)}, u32[]{:S(2)}) collective-permute-start(f32[4,32,128]{2,1,0:T(8,128)S(1)} %get-tuple-element.25), channel_id=1, source_target_pairs={{0,3},{1,2},{2,1},{3,0},{4,7},{5,6},{6,5},{7,4},{8,11},{9,10},{10,... | collective-permute-start | bytes 196616 | tf_op jit(solution)/shard_map/ppermute | solution.py:803
  13.1 7.0 %collective-permute-start.5 = (f32[352,128]{1,0:T(8,128)S(1)}, f32[352,128]{1,0:T(8,128)S(1)}, u32[]{:S(2)}, u32[]{:S(2)}) collective-permute-start(f32[352,128]{1,0:T(8,128)S(1)} %get-tuple-element.28), channel_id=1, source_target_pairs={{0,8},{1,9},{2,10},{3,11},{4,12},{5,13},{6,14},{7,15},{8,0},{9,1},... | collective-permute-start | bytes 540680 | tf_op jit(solution)/shard_map/ppermute | solution.py:803
  15.0 5.1 %collective-permute-start.6 = (f32[352,128]{1,0:T(8,128)S(1)}, f32[352,128]{1,0:T(8,128)S(1)}, u32[]{:S(2)}, u32[]{:S(2)}) collective-permute-start(f32[352,128]{1,0:T(8,128)S(1)} %get-tuple-element.29), channel_id=1, source_target_pairs={{0,1},{1,0},{2,3},{3,2},{4,5},{5,4},{6,7},{7,6},{8,16},{9,17},{10,... | collective-permute-start | bytes 540680 | tf_op jit(solution)/shard_map/ppermute | solution.py:803

commit v5 on v4

--- a/solution.py
+++ b/solution.py
@@ -80,18 +80,36 @@
     return jnp.where(here, (z - HALO) * 12 + 4 * x, 0), here
 
 
+def halo_start(side):
+    return 0 if side == 0 else (HALO + 4) * XW - 256
+
+
+def halo_cells(side, px, rows):
+    p = (lane_iota(rows) - (halo_start(side) + 32 * px)) & 127
+    z = (p >= XW).astype(jnp.int32) + (p >= 2 * XW).astype(jnp.int32)
+    return z, p - z * XW, p < HALO * XW
+
+
+def halo_turn(side, px, rows):
+    z, x, _ = halo_cells(side, px, rows)
+    return jnp.where((x >= HALO) & (x < XW - HALO), z, 3)
+
+
+def halo_lanes(side, z, rows):
+    q = (lane_iota(rows) - (halo_start(side) + z * XW + HALO)) & 127
+    return 4 * (q & 31) + lax.shift_right_logical(q, 5)
+
+
 def edge_far_lanes(side, a, rows):
-    z, x = window_cells(2 * side, rows)
-    z = z - (HALO + 4) * side
     width = M_EDGE if a == 1 else R_EDGE
-    left, right = x < HALO, x >= XW - HALO
-    here = (z >= 0) & (z < HALO) & (left | right)
-    index = jnp.where(
-        left,
-        EDGE_STARTS[a, 0] + z * width + 4 * x - (EDGE - width),
-        EDGE_STARTS[a, 1] + z * width + 4 * (x - (XW - HALO)),
-    )
-    return jnp.where(here, index, 4), here
+    index = jnp.zeros((rows, 128), jnp.int32)
+    for px in range(4):
+        z, x, here = halo_cells(side, px, rows)
+        left = EDGE_STARTS[a, 0] + z * width + 4 * x + px - (EDGE - width)
+        right = EDGE_STARTS[a, 1] + z * width + 4 * (x - (XW - HALO)) + px
+        index = jnp.where(here & (x < HALO), left, index)
+        index = jnp.where(here & (x >= XW - HALO), right, index)
+    return jnp.clip(index, 0, 127)
 
 
 class Plan:
@@ -214,7 +232,7 @@
 def z_pack_kernel(plan, *refs):
     near = plan.near
     beside = refs[:near]
-    x_even_ref, x_odd_ref = refs[near : near + 2]
+    x_odd_ref, x_even_ref = refs[near : near + 2]
     outs = refs[-2:]
     places = plan.y_places()[1]
     x_even = is_even("gx")
@@ -260,7 +278,7 @@
 def own_kernel(plan, *refs):
     near = plan.near
     cells_ref, *beside = refs[: 1 + near]
-    x_even_ref, x_odd_ref = refs[1 + near : 3 + near]
+    x_odd_ref, x_even_ref = refs[1 + near : 3 + near]
     out, planes, sides = refs[-3:]
     tile = plan.tile
     own_row, places = plan.y_places()
@@ -272,6 +290,7 @@
     sides[0] = jnp.where(x_even, odd, even)
     sides[1] = jnp.where(x_even, even, odd)
 
+    inside = inside_mask(plan)
     offsets = [(z + HALO) * XW + HALO for z in range(4)]
     index = [[every_lane(offset, px, tile) for px in range(4)] for offset in offsets]
     from_edge = {(s, t): edge_own_lanes(s, t, tile) for s, t in ((0, 0), (0, 1), (1, 1), (1, 2))}
@@ -295,7 +314,8 @@
                                 lanes, here = from_edge[s, t]
                                 lanes = lanes + (48 * a + px)
                                 value = jnp.where(here, gather(side[s], lanes), value)
-                        out[a, pz, py, px, :, 128 * t : 128 * t + 128] = value
+                        lanes = slice(128 * t, 128 * t + 128)
+                        out[a, pz, py, px, :, lanes] = jnp.where(inside[:, lanes], value, 0.0)
         return carry
 
     lax.fori_loop(0, 4, body, 0)
@@ -351,8 +371,23 @@
     )
 
 
-def pull(m_ref, v_ref, h_ref, a, b, c):
-    cells = around(v_ref, a, b, c)
+def around_rimless(plan, ref, n, a, b, c):
+    tile = plan.tile
+    row = lax.broadcasted_iota(jnp.int32, (tile, LW), 0)
+    return (
+        ref[a - 1, b, c] if a > 0 else roll_lanes(ref[n - 1, b, c], XW),
+        ref[a + 1, b, c] if a < n - 1 else roll_lanes(ref[0, b, c], -XW),
+        ref[a, b - 1, c] if b > 0 else jnp.where(row == 0, 0.0, pltpu.roll(ref[a, n - 1, c], 1, 0)),
+        ref[a, b + 1, c]
+        if b < n - 1
+        else jnp.where(row == tile - 1, 0.0, pltpu.roll(ref[a, 0, c], tile - 1, 0)),
+        ref[a, b, c - 1] if c > 0 else roll_lanes(ref[a, b, n - 1], 1),
+        ref[a, b, c + 1] if c < n - 1 else roll_lanes(ref[a, b, 0], -1),
+    )
+
+
+def pull(plan, n, m_ref, v_ref, h_ref, a, b, c):
+    cells = around_rimless(plan, v_ref, n, a, b, c)
     mobility = around(m_ref, a, b, c)
     total = ((cells[0] + cells[1]) + (cells[2] + cells[3])) + (cells[4] + cells[5])
     products = [m * v for m, v in zip(mobility, cells)]
@@ -362,57 +397,30 @@
     return h_ref[a, b, c] * (m_ref[a + 1, b + 1, c + 1] * total + other)
 
 
-def over_pairs(n, step):
-    if n == 2:
-        for a, b in np.ndindex(2, 2):
-            step(a, b)
-        return
-
-    def body(i, carry):
-        step(lax.div(i, n), lax.rem(i, n))
-        return carry
-
-    lax.fori_loop(0, n * n, body, 0)
-
-
-def descend(plan, n, factor, inside, m_ref, r_ref, v_ref, w_ref, d_ref, h_ref, e_ref, k_ref):
+def descend(plan, n, factor, inside, m_ref, r_ref, d_ref, h_ref, e_ref, k_ref):
     fill_rim(plan, m_ref, n)
-
-    def first(a, b):
-        for c in range(n):
-            s = around(m_ref, a, b, c)
-            d = 3.0 * m_ref[a + 1, b + 1, c + 1] + 0.5 * (
-                ((s[0] + s[1]) + (s[2] + s[3])) + (s[4] + s[5])
-            )
-            h = jnp.where(inside, 0.4 / d, 0.0)
-            e = (2.0 / factor) * h * r_ref[a, b, c]
-            d_ref[a, b, c] = d
-            h_ref[a, b, c] = h
-            e_ref[a, b, c] = e
-            v_ref[a + 1, b + 1, c + 1] = e
-
-    over_pairs(n, first)
-    fill_rim(plan, v_ref, n)
-
-    def second(a, b):
-        for c in range(n):
-            value = 1.2 * e_ref[a, b, c] + pull(m_ref, v_ref, h_ref, a, b, c)
-            w_ref[a + 1, b + 1, c + 1] = value
-            k_ref[a, b, c] = value
-
-    over_pairs(n, second)
-    fill_rim(plan, w_ref, n)
-
-
-def leftover(factor, m_ref, r_ref, w_ref, d_ref, h_ref, a, b, c):
-    away = w_ref[a + 1, b + 1, c + 1] - 1.25 * pull(m_ref, w_ref, h_ref, a, b, c)
+    for a, b, c in np.ndindex(n, n, n):
+        s = around(m_ref, a, b, c)
+        d = 3.0 * m_ref[a + 1, b + 1, c + 1] + 0.5 * (
+            ((s[0] + s[1]) + (s[2] + s[3])) + (s[4] + s[5])
+        )
+        h = jnp.where(inside, 0.4 / d, 0.0)
+        d_ref[a, b, c] = d
+        h_ref[a, b, c] = h
+        e_ref[a, b, c] = (2.0 / factor) * h * r_ref[a, b, c]
+    for a, b, c in np.ndindex(n, n, n):
+        k_ref[a, b, c] = 1.2 * e_ref[a, b, c] + pull(plan, n, m_ref, e_ref, h_ref, a, b, c)
+
+
+def leftover(plan, n, factor, m_ref, r_ref, d_ref, h_ref, k_ref, a, b, c):
+    away = k_ref[a, b, c] - 1.25 * pull(plan, n, m_ref, k_ref, h_ref, a, b, c)
     return r_ref[a, b, c] - factor * (d_ref[a, b, c] * away)
 
 
 def down_kernel(plan, *refs):
-    own_ref, even_own, odd_own, even_ref, odd_ref = refs[:5]
+    own_ref, odd_own, even_own, odd_ref, even_ref = refs[:5]
     chunk, m0, h0, e0, k0, m1, h1, e1, k1 = refs[5:14]
-    r0, v0, w0, d0, r1, v1, w1, d1, planes, sides = refs[14:]
+    r0, d0, r1, d1, planes, sides = refs[14:]
     near, tile = plan.near, plan.tile
     own_row, places = plan.y_places()
     z_even = is_even("grp")
@@ -453,70 +461,70 @@
             row = plan.starts[4] + pz * plan.rows
             sides[side, pz] = read(slice(row, row + plan.rows))
 
-    first = [HALO, (HALO + 4) * XW + HALO - 256]
-    index = [
-        [[every_lane(first[side] + z * XW, px, tile) for px in range(4)] for z in range(HALO)]
-        for side in range(2)
-    ]
-    here = [
-        [between(first[side] + z * XW, first[side] + z * XW + 32, tile) for z in range(HALO)]
-        for side in range(2)
-    ]
-    from_edge = {(s, a): edge_far_lanes(s, a, tile) for s in range(2) for a in range(2)}
+    index = [[halo_lanes(side, z, tile) for z in range(HALO)] for side in range(2)]
+    turns = [[halo_turn(side, px, tile) for px in range(4)] for side in range(2)]
+    edge_index = [[edge_far_lanes(side, a, tile) for a in range(2)] for side in range(2)]
+    keep = []
+    for side, t in ((0, 0), (1, 2)):
+        z, _ = window_cells(t, tile)
+        z = (z < HALO) if side == 0 else (z >= HALO + 4)
+        keep.append(z & inside[:, 128 * t : 128 * t + 128])
 
     def place(pz, carry):
         for a in range(2):
             for py in range(4):
-                cells = [
-                    [every_fourth(plan, planes, (s, a, 4 * z + pz), py) for z in range(HALO)]
-                    for s in range(2)
-                ]
-                edge = [every_fourth(plan, sides, (s, pz), py) for s in range(2)]
-                for px in range(4):
-                    for t in range(3):
-                        lanes = slice(128 * t, 128 * t + 128)
-                        value = own_ref[a, pz, py, px, :, lanes]
-                        if t != 1:
-                            s = t // 2
-                            for z in range(HALO):
-                                part = gather(cells[s][z], index[s][z][px])
-                                value = jnp.where(here[s][z], part, value)
-                            place_of, at_edge = from_edge[s, a]
-                            part = gather(edge[s], place_of + px)
-                            value = jnp.where(at_edge, part, value)
-                        value = jnp.where(inside[:, lanes], value, 0.0)
+                for side, t in ((0, 0), (1, 2)):
+                    lanes = slice(128 * t, 128 * t + 128)
+                    parts = [
+                        gather(
+                            every_fourth(plan, planes, (side, a, 4 * z + pz), py), index[side][z]
+                        )
+                        for z in range(HALO)
+                    ]
+                    edge = gather(
+                        every_fourth(plan, sides, (side, pz), py), edge_index[side][a]
+                    )
+                    for px in range(4):
+                        turn = turns[side][px]
+                        value = jnp.where(turn == 1, parts[1], parts[0])
+                        value = jnp.where(turn == 2, parts[2], value)
+                        value = jnp.where(turn == 3, edge, value)
+                        if px > 0:
+                            value = pltpu.roll(value, 128 - 32 * px, 1)
+                        value = jnp.where(
+                            keep[side], value, own_ref[a, pz, py, px, :, lanes]
+                        )
                         if a == 1:
                             m0[pz + 1, py + 1, px + 1, :, lanes] = value
                         else:
                             r0[pz, py, px, :, lanes] = value
+                for px in range(4):
+                    lanes = slice(128, 256)
+                    value = own_ref[a, pz, py, px, :, lanes]
+                    if a == 1:
+                        m0[pz + 1, py + 1, px + 1, :, lanes] = value
+                    else:
+                        r0[pz, py, px, :, lanes] = value
         return carry
 
     lax.fori_loop(0, 4, place, 0)
 
-    descend(plan, 4, 1.0, inside, m0, r0, v0, w0, d0, h0, e0, k0)
-
-    def restrict(a, b):
-        for c in range(2):
-            rest = jnp.zeros((tile, LW), F32)
-            mobility = jnp.zeros((tile, LW), F32)
-            for da in range(2):
-                for db in range(2):
-                    for dc in range(2):
-                        i, j, k = 2 * a + da, 2 * b + db, 2 * c + dc
-                        rest = rest + leftover(1.0, m0, r0, w0, d0, h0, i, j, k)
-                        mobility = mobility + m0[i + 1, j + 1, k + 1]
-            r1[a, b, c] = 0.125 * rest
-            m1[a + 1, b + 1, c + 1] = 0.125 * mobility
-
-    over_pairs(2, restrict)
-    descend(plan, 2, 0.25, inside, m1, r1, v1, w1, d1, h1, e1, k1)
+    descend(plan, 4, 1.0, inside, m0, r0, d0, h0, e0, k0)
+    for a, b, c in np.ndindex(2, 2, 2):
+        rest = jnp.zeros((tile, LW), F32)
+        mobility = jnp.zeros((tile, LW), F32)
+        for da, db, dc in np.ndindex(2, 2, 2):
+            i, j, k = 2 * a + da, 2 * b + db, 2 * c + dc
+            rest = rest + leftover(plan, 4, 1.0, m0, r0, d0, h0, k0, i, j, k)
+            mobility = mobility + m0[i + 1, j + 1, k + 1]
+        r1[a, b, c] = 0.125 * rest
+        m1[a + 1, b + 1, c + 1] = 0.125 * mobility
+    descend(plan, 2, 0.25, inside, m1, r1, d1, h1, e1, k1)
     rest = jnp.zeros((tile, LW), F32)
     mobility = jnp.zeros((tile, LW), F32)
-    for a in range(2):
-        for b in range(2):
-            for c in range(2):
-                rest = rest + leftover(0.25, m1, r1, w1, d1, h1, a, b, c)
-                mobility = mobility + m1[a + 1, b + 1, c + 1]
+    for a, b, c in np.ndindex(2, 2, 2):
+        rest = rest + leftover(plan, 2, 0.25, m1, r1, d1, h1, k1, a, b, c)
+        mobility = mobility + m1[a + 1, b + 1, c + 1]
     both = []
     for total in (rest, mobility):
         packed = jnp.zeros((tile, 128), F32)
@@ -634,37 +642,16 @@
     return jnp.broadcast_to(rows[:, None], (z, 2, fine.tile, 128)).reshape(fine.shape)
 
 
-def ascend(plan, n, m_ref, h_ref, e_ref, k_ref, below, v_ref, w_ref, emit):
-    def start(a, b):
-        for c in range(n):
-            v_ref[a + 1, b + 1, c + 1] = k_ref[a, b, c] + below(a, b, c)
-
-    over_pairs(n, start)
-    fill_rim(plan, v_ref, n)
-
-    def middle(a, b):
-        for c in range(n):
-            w_ref[a + 1, b + 1, c + 1] = (
-                0.2 * v_ref[a + 1, b + 1, c + 1]
+def ascend(plan, n, m_ref, h_ref, e_ref, k_ref, below, v_ref, w_ref):
+    for a, b, c in np.ndindex(n, n, n):
+        v_ref[a, b, c] = k_ref[a, b, c] + below(a, b, c)
+    for old, new in ((v_ref, w_ref), (w_ref, v_ref)):
+        for a, b, c in np.ndindex(n, n, n):
+            new[a, b, c] = (
+                0.2 * old[a, b, c]
                 + e_ref[a, b, c]
-                + pull(m_ref, v_ref, h_ref, a, b, c)
+                + pull(plan, n, m_ref, old, h_ref, a, b, c)
             )
-
-    over_pairs(n, middle)
-    fill_rim(plan, w_ref, n)
-
-    def last(a, b):
-        for c in range(n):
-            emit(
-                a,
-                b,
-                c,
-                0.2 * w_ref[a + 1, b + 1, c + 1]
-                + e_ref[a, b, c]
-                + pull(m_ref, w_ref, h_ref, a, b, c),
-            )
-
-    over_pairs(n, last)
 
 
 def up_kernel(plan, *refs):
@@ -740,29 +727,24 @@
 
     below = window[...]
 
-    def keep(a, b, c, value):
-        v1[a + 1, b + 1, c + 1] = value
-
-    ascend(plan, 2, m1, h1, e1, k1, lambda a, b, c: below, v1, w1, keep)
-
-    def from_half(a, b, c):
-        return v1[lax.shift_right_logical(a, 1) + 1, lax.shift_right_logical(b, 1) + 1, c // 2 + 1]
-
-    def finish(a, b, c, value):
-        v0[a + 1, b + 1, c + 1] = value
-
-    ascend(plan, 4, m0, h0, e0, k0, from_half, v0, w0, finish)
+    ascend(plan, 2, m1, h1, e1, k1, lambda a, b, c: below, v1, w1)
+    ascend(plan, 4, m0, h0, e0, k0, lambda a, b, c: v1[a // 2, b // 2, c // 2], v0, w0)
 
     lane = lane_iota(tile)
-    turns = [(lane & 3) == px for px in range(4)]
+    natural = 32 * (lane & 3) + lax.shift_right_logical(lane, 2)
     starts = [(z + HALO) * XW + HALO for z in range(4)]
-    index = [(lax.shift_right_logical(lane, 2) + start % 128) & 127 for start in starts]
+    places_of = [(lane - start) & 127 for start in starts]
+    index = [(natural + start) & 127 for start in starts]
 
     def store(pz, carry):
         for py in range(4):
             parts = [
-                [v0[pz + 1, py + 1, px + 1, :, 128 * t : 128 * t + 128] for t in range(3)]
+                [v0[pz, py, px, :, 128 * t : 128 * t + 128] for t in range(3)]
                 for px in range(4)
+            ]
+            parts = [
+                [part if px == 0 else pltpu.roll(part, 32 * px, 1) for part in row]
+                for px, row in enumerate(parts)
             ]
             for z, start in enumerate(starts):
                 low, high = start // 128, (start + 31) // 128
@@ -770,13 +752,15 @@
                 for px in range(4):
                     part = parts[px][low]
                     if low != high:
-                        part = jnp.where(lane >= 64, part, parts[px][high])
-                    part = gather(part, index[z])
-                    value = part if value is None else jnp.where(turns[px], part, value)
+                        first = (places_of[z] & 31) < 128 - start % 128
+                        part = jnp.where(first, part, parts[px][high])
+                    turn = lax.shift_right_logical(places_of[z], 5) == px
+                    value = part if value is None else jnp.where(turn, part, value)
+                value = gather(value, index[z])
                 out[4 * z + pz, pl.ds(py, 4, 4), :] = own_rows(plan, value)
         return carry
 
-    lax.fori_loop(0, 4, store, 0)
+    lax.fori_loop(0, 4, store, 0, unroll=4)
 
 
 def call(plan, kernel, outs, scratch, *args):
@@ -813,7 +797,7 @@
             cells,
         )
         arrived = [swap(values, None, y, None) for y, values in enumerate(rows)]
-        z_own = [swap(even, 0, None, None), swap(odd, 1, None, None)]
+        z_own = [swap(odd, 1, None, None), swap(even, 0, None, None)][::-1]
         *beside, even, odd = call(
             plan,
             lambda *refs: edges_kernel(plan, *refs),
@@ -822,17 +806,17 @@
             cells,
             *arrived,
         )
-        edges = [swap(even, None, None, 0), swap(odd, None, None, 1)]
+        edges = [swap(odd, None, None, 1), swap(even, None, None, 0)][::-1]
         sends = call(
             plan,
             lambda *refs: z_pack_kernel(plan, *refs),
             [(plan.payload, 128)] * 2,
             [],
             *beside,
-            *edges,
+            *edges[::-1],
             *z_own,
         )
-        arrived = [swap(sends[0], 0, None, None), swap(sends[1], 1, None, None)]
+        arrived = [swap(sends[1], 1, None, None), swap(sends[0], 0, None, None)][::-1]
         (own,) = call(
             plan,
             lambda *refs: own_kernel(plan, *refs),
@@ -840,18 +824,18 @@
             [(2, 16, plan.rows, 128), (2, 4, plan.rows, 128)],
             cells,
             *beside,
-            *edges,
+            *edges[::-1],
         )
         chunk, *state = call(
             plan,
             lambda *refs: down_kernel(plan, *refs),
             [(plan.devices, 8, 128)] + [full_rim] + [full] * 3 + [half_rim] + [half] * 3,
-            [full, full_rim, full_rim, full]
-            + [half, half_rim, half_rim, half]
+            [full] * 2
+            + [half] * 2
             + [(2, 2, EDGE, plan.rows, 128), (2, 4, plan.rows, 128)],
             own,
-            *z_own,
-            *arrived,
+            *z_own[::-1],
+            *arrived[::-1],
         )
         joined = lax.all_to_all(chunk, AXES, 0, 0, tiled=True)
         levels = [Level(plan, level) for level in range(2, LEVELS + 1)]
@@ -860,8 +844,8 @@
             plan,
             lambda *refs: up_kernel(plan, *refs),
             [(16, 16, 128)],
-            [full_rim] * 2
-            + [half_rim] * 2
+            [full] * 2
+            + [half] * 2
             + [(tile, LW)]
             + [(z2, y2, 128)] * 2
             + [(z2 + 2 * HALO, y2 + margin, 128)]

time: 47.6 us -> 43.6 us (0.916)
  Pallas kernels: 16.7 us -> 13.1 us
  starting transfers between devices: 8.48 us -> 11.7 us
  blocking collectives: 14.3 us -> 12.5 us
  waiting for transfers between devices: 6.85 us -> 5.05 us
    pallas_call x6, Pallas kernels: 16.7 us -> 13.1 us  [call(): pl.pallas_call(kernel, out_shape=[jax.ShapeDtypeStruct(shape, F32) for sh...]
    ppermute x7, starting transfers between devices: 8.48 us -> 11.7 us  [swap(): return lax.ppermute(values, AXES, plan.pairs(swaps))]
    all_to_all x1, blocking collectives: 14.3 us -> 12.5 us  [on_device(): joined = lax.all_to_all(chunk, AXES, 0, 0, tiled=True)]
    ppermute x7, waiting for transfers between devices: 6.85 us -> 5.05 us  [swap(): return lax.ppermute(values, AXES, plan.pairs(swaps))]
  transfers between devices with their start and end apart: 7 -> 7, of which waited for: 3 -> 4; matrix products, arithmetic and copies ran while one was open for 0% -> 0% of each run, Pallas kernels for 7% -> 8%
where the time goes in v5:
time: 43.6 us; the launch traced here: 43.4 us
  Pallas kernels  13.1 us (30%)
  blocking collectives  12.5 us (29%)
  starting transfers between devices  11.7 us (27%)
  waiting for transfers between devices  5.05 us (12%)
  other arithmetic  0.99 us (2%)
    pallas_call x6, Pallas kernels, call(): pl.pallas_call(kernel, out_shape=[jax.ShapeDtypeStruct(shape, F32) for sh...  13.1 us
    all_to_all x1, blocking collectives, on_device(): joined = lax.all_to_all(chunk, AXES, 0, 0, tiled=True)  12.5 us
    ppermute x7, starting transfers between devices, swap(): return lax.ppermute(values, AXES, plan.pairs(swaps))  11.7 us
    ppermute x7, waiting for transfers between devices, swap(): return lax.ppermute(values, AXES, plan.pairs(swaps))  5.05 us
    another operation x1, other arithmetic, on_device(): cells = jnp.stack([residual, mobility])  0.99 us
  transfers between devices with their start and end apart: 7, of which 4 were waited for; matrix products, arithmetic and copies ran while one was open for 0% of the time, Pallas kernels for 8%

profile of v5, /device:TPU:0, one launch (start us, length us, event | category | flops | bytes accessed | tf_op | source)
XLA Modules:
  0.0 43.4 jit_solution(5996423759422843658)
XLA Ops:
  0.0 1.0 %pad_maximum_fusion.refs_0_ = f32[2,16,16,128]{3,2,1,0:T(8,128)S(1)} fusion(f32[1,16,16,128]{3,2,1,0:T(8,128)} %bitcast.2, f32[1,16,16,128]{3,2,1,0:T(8,128)} %bitcast.3), kind=kLoop, calls=%fused_computation | loop fusion | flops 65536 | bytes 524288 | tf_op jit(solution)/shard_map/stack | solution.py:791
  1.0 0.1 shard_map.28
  1.1 3.0 %collective-permute-start = (f32[352,128]{1,0:T(8,128)S(1)}, f32[352,128]{1,0:T(8,128)S(1)}, u32[]{:S(2)}, u32[]{:S(2)}) collective-permute-start(f32[352,128]{1,0:T(8,128)S(1)} %get-tuple-element.22), channel_id=1, source_target_pairs={{0,4},{1,5},{2,6},{3,7},{4,0},{5,1},{6,2},{7,3},{8,12},{9,13},{10,... | collective-permute-start | bytes 540680 | tf_op jit(solution)/shard_map/ppermute | solution.py:787
  4.1 0.0 collective-permute-start.3
  4.1 3.1 %collective-permute-start.4 = (f32[336,128]{1,0:T(8,128)S(1)}, f32[336,128]{1,0:T(8,128)S(1)}, u32[]{:S(2)}, u32[]{:S(2)}) collective-permute-start(f32[336,128]{1,0:T(8,128)S(1)} %get-tuple-element.27), channel_id=1, source_target_pairs={{0,8},{1,9},{2,10},{3,11},{4,12},{5,13},{6,14},{7,15},{8,0},{9,1},... | collective-permute-start | bytes 516104 | tf_op jit(solution)/shard_map/ppermute | solution.py:787
  7.2 1.4 %collective-permute-done.refs_1_ = f32[352,128]{1,0:T(8,128)S(1)} collective-permute-done((f32[352,128]{1,0:T(8,128)S(1)}, f32[352,128]{1,0:T(8,128)S(1)}, u32[]{:S(2)}, u32[]{:S(2)}) %collective-permute-start) | collective-permute-done | bytes 180256 | tf_op jit(solution)/shard_map/ppermute | solution.py:787
  8.6 0.3 shard_map.29
  9.0 0.3 collective-permute-start.1
  9.3 1.5 %collective-permute-start.2 = (f32[4,32,128]{2,1,0:T(8,128)S(1)}, f32[4,32,128]{2,1,0:T(8,128)S(1)}, u32[]{:S(2)}, u32[]{:S(2)}) collective-permute-start(f32[4,32,128]{2,1,0:T(8,128)S(1)} %get-tuple-element.25), channel_id=1, source_target_pairs={{0,1},{1,0},{2,3},{3,2},{4,5},{5,4},{6,7},{7,6},{8,9},{9,8},{10,11... | collective-permute-start | bytes 196616 | tf_op jit(solution)/shard_map/ppermute | solution.py:787
  10.9 0.0 collective-permute-done.3.refs_4_.refs_1_
  10.9 0.2 collective-permute-done.4.refs_3_.refs_2_
  11.1 2.1 %collective-permute-done.1.refs_2_.refs_1_ = f32[4,32,128]{2,1,0:T(8,128)S(1)} collective-permute-done((f32[4,32,128]{2,1,0:T(8,128)S(1)}, f32[4,32,128]{2,1,0:T(8,128)S(1)}, u32[]{:S(2)}, u32[]{:S(2)}) %collective-permute-start.1) | collective-permute-done | bytes 65568 | tf_op jit(solution)/shard_map/ppermute | solution.py:787
  13.2 0.0 collective-permute-done.2.refs_3_.refs_2_
  13.2 0.2 shard_map.31
  13.3 0.2 collective-permute-start.5
  13.5 3.5 %collective-permute-start.6 = (f32[352,128]{1,0:T(8,128)S(1)}, f32[352,128]{1,0:T(8,128)S(1)}, u32[]{:S(2)}, u32[]{:S(2)}) collective-permute-start(f32[352,128]{1,0:T(8,128)S(1)} %get-tuple-element.29), channel_id=1, source_target_pairs={{0,8},{1,9},{2,10},{3,11},{4,12},{5,13},{6,14},{7,15},{8,0},{9,1},... | collective-permute-start | bytes 540680 | tf_op jit(solution)/shard_map/ppermute | solution.py:787
  17.0 3.2 %shard_map.30.refs_0_ = f32[2,4,4,4,8,384]{5,4,3,2,1,0:T(8,128)S(1)} custom-call(f32[2,16,16,128]{3,2,1,0:T(8,128)S(1)} %pad_maximum_fusion.refs_0_, f32[2,16,16,128]{3,2,1,0:T(8,128)S(1)} %get-tuple-element.23.refs_1_.refs_0_, f32[4,32,128]{2,1,0:T(8,128)S(1)} %collective-permute-done.1.refs_2_.refs_1_, f32[4,32,128]{2,1,0:T(8,128)S(1)} %collective-permute-done.2.refs_3_.refs_2_), custom_call_target="tpu_custom_call" | custom-call | tf_op jit(solution)/shard_map/pallas_call | solution.py:767
  20.2 0.0 collective-permute-done.5.refs_3_
  20.2 1.3 %collective-permute-done.6.refs_4_ = f32[352,128]{1,0:T(8,128)S(1)} collective-permute-done((f32[352,128]{1,0:T(8,128)S(1)}, f32[352,128]{1,0:T(8,128)S(1)}, u32[]{:S(2)}, u32[]{:S(2)}) %collective-permute-start.6) | collective-permute-done | bytes 180256 | tf_op jit(solution)/shard_map/ppermute | solution.py:787
  21.5 4.1 %shard_map.32 = (f32[32,8,128]{2,1,0:T(8,128)S(1)}, f32[6,6,6,8,384]{4,3,2,1,0:T(8,128)S(1)}, f32[4,4,4,8,384]{4,3,2,1,0:T(8,128)S(1)}, f32[4,4,4,8,384]{4,3,2,1...) custom-call(f32[2,4,4,4,8,384]{5,4,3,2,1,0:T(8,128)S(1)} %shard_map., ...), custom_call_target="tpu_custom_call" | custom-call | tf_op jit(solution)/shard_map/pallas_call | solution.py:767
  25.6 12.5 %all_to_all.5.refs_0_ = f32[32,8,128]{2,1,0:T(8,128)S(1)} all-to-all(f32[32,8,128]{2,1,0:T(8,128)S(1)} %get-tuple-element.30), channel_id=1, replica_groups=mesh['grp'=4,'gy'=2,'gx'=4] {'grp','gy','gx'}, dimensions={0} | all-to-all | bytes 262144 | tf_op jit(solution)/shard_map/all_to_all | solution.py:840
  38.1 5.3 %shard_map.33 = f32[16,16,128]{2,1,0:T(8,128)} custom-call(f32[32,8,128]{2,1,0:T(8,128)S(1)} %all_to_all.5.refs_0_, f32[6,6,6,8,384]{4,3,2,1,0:T(8,128)S(1)} %get-tuple-element.31.refs_1_, f32[4,4,4,8,384]{4,3,2,1,0:T(8,128)S(1)} %get-tuple-element.32.refs_2_, f32[4,4,4,8,384]{4,3,2,1,0:T(8,128)S(1)} %get-tuple-element.33.refs_3_, ...), custom_call_target="tpu_custom_call" | custom-call | tf_op jit(solution)/shard_map/pallas_call | solution.py:767
Async XLA Ops:
  1.1 7.6 %collective-permute-start = (f32[352,128]{1,0:T(8,128)S(1)}, f32[352,128]{1,0:T(8,128)S(1)}, u32[]{:S(2)}, u32[]{:S(2)}) collective-permute-start(f32[352,128]{1,0:T(8,128)S(1)} %get-tuple-element.22), channel_id=1, source_target_pairs={{0,4},{1,5},{2,6},{3,7},{4,0},{5,1},{6,2},{7,3},{8,12},{9,13},{10,... | collective-permute-start | bytes 540680 | tf_op jit(solution)/shard_map/ppermute | solution.py:787
  4.1 6.8 %collective-permute-start.3 = (f32[336,128]{1,0:T(8,128)S(1)}, f32[336,128]{1,0:T(8,128)S(1)}, u32[]{:S(2)}, u32[]{:S(2)}) collective-permute-start(f32[336,128]{1,0:T(8,128)S(1)} %get-tuple-element.26), channel_id=1, source_target_pairs={{0,1},{1,0},{2,3},{3,2},{4,5},{5,4},{6,7},{7,6},{8,16},{9,17},{10,... | collective-permute-start | bytes 516104 | tf_op jit(solution)/shard_map/ppermute | solution.py:787
  4.1 7.0 %collective-permute-start.4 = (f32[336,128]{1,0:T(8,128)S(1)}, f32[336,128]{1,0:T(8,128)S(1)}, u32[]{:S(2)}, u32[]{:S(2)}) collective-permute-start(f32[336,128]{1,0:T(8,128)S(1)} %get-tuple-element.27), channel_id=1, source_target_pairs={{0,8},{1,9},{2,10},{3,11},{4,12},{5,13},{6,14},{7,15},{8,0},{9,1},... | collective-permute-start | bytes 516104 | tf_op jit(solution)/shard_map/ppermute | solution.py:787
  9.0 4.2 %collective-permute-start.1 = (f32[4,32,128]{2,1,0:T(8,128)S(1)}, f32[4,32,128]{2,1,0:T(8,128)S(1)}, u32[]{:S(2)}, u32[]{:S(2)}) collective-permute-start(f32[4,32,128]{2,1,0:T(8,128)S(1)} %get-tuple-element.24), channel_id=1, source_target_pairs={{0,3},{1,2},{2,1},{3,0},{4,7},{5,6},{6,5},{7,4},{8,11},{9,10},{10,... | collective-permute-start | bytes 196616 | tf_op jit(solution)/shard_map/ppermute | solution.py:787
  9.3 3.8 %collective-permute-start.2 = (f32[4,32,128]{2,1,0:T(8,128)S(1)}, f32[4,32,128]{2,1,0:T(8,128)S(1)}, u32[]{:S(2)}, u32[]{:S(2)}) collective-permute-start(f32[4,32,128]{2,1,0:T(8,128)S(1)} %get-tuple-element.25), channel_id=1, source_target_pairs={{0,1},{1,0},{2,3},{3,2},{4,5},{5,4},{6,7},{7,6},{8,9},{9,8},{10,11... | collective-permute-start | bytes 196616 | tf_op jit(solution)/shard_map/ppermute | solution.py:787
  13.3 6.8 %collective-permute-start.5 = (f32[352,128]{1,0:T(8,128)S(1)}, f32[352,128]{1,0:T(8,128)S(1)}, u32[]{:S(2)}, u32[]{:S(2)}) collective-permute-start(f32[352,128]{1,0:T(8,128)S(1)} %get-tuple-element.28), channel_id=1, source_target_pairs={{0,1},{1,0},{2,3},{3,2},{4,5},{5,4},{6,7},{7,6},{8,16},{9,17},{10,... | collective-permute-start | bytes 540680 | tf_op jit(solution)/shard_map/ppermute | solution.py:787
  13.5 8.0 %collective-permute-start.6 = (f32[352,128]{1,0:T(8,128)S(1)}, f32[352,128]{1,0:T(8,128)S(1)}, u32[]{:S(2)}, u32[]{:S(2)}) collective-permute-start(f32[352,128]{1,0:T(8,128)S(1)} %get-tuple-element.29), channel_id=1, source_target_pairs={{0,8},{1,9},{2,10},{3,11},{4,12},{5,13},{6,14},{7,15},{8,0},{9,1},... | collective-permute-start | bytes 540680 | tf_op jit(solution)/shard_map/ppermute | solution.py:787

commit v6 on v5

--- a/solution.py
+++ b/solution.py
@@ -17,6 +17,15 @@
 LW = 384
 EDGE = 4 * HALO
 M_DEEP, M_FAR, R_DEEP, R_FAR = 11, 4, 10, 3
+
+NEAR_TILES = (
+    [[(1, d, 0)] for d in range(1, 7)]
+    + [[(0, d, 0)] for d in range(1, 6)]
+    + [[(1, 7, 0), (1, 11, 6)], [(1, 8, 0), (1, 10, 5)], [(0, 6, 0), (0, 10, 6)]]
+    + [[(0, 7, 0), (0, 9, 5)], [(1, 9, 0), (0, 8, 4)]]
+)
+FAR_TILES = [[(1, 1, 0), (1, 2, 3), (0, 1, 6)], [(0, 2, 0), (1, 3, 2), (0, 3, 4), (1, 4, 5)]]
+BESIDE_ROWS = 8 * (len(NEAR_TILES) + len(FAR_TILES) + 1)
 M_EDGE, R_EDGE = 11, 10
 Y_FAR = 3
 Y_ROWS = 16 * (8 + Y_FAR)
@@ -119,16 +128,8 @@
         self.rows = 16 * (1 + self.near)
         self.cells = self.rows // 4
         self.tile = -(-self.cells // 8) * 8
-        self.z_rows = 8 * self.near
-        sizes = [
-            M_DEEP * self.z_rows,
-            M_FAR * self.z_rows,
-            R_DEEP * self.z_rows,
-            R_FAR * self.z_rows,
-            4 * self.rows,
-        ]
-        self.starts = [sum(sizes[:i]) for i in range(len(sizes))]
-        self.payload = sum(sizes)
+        self.edge_start = BESIDE_ROWS * self.near
+        self.payload = self.edge_start + 32 * (2 + self.near)
         self.devices = self.counts[0] * self.counts[1] * self.counts[2]
         self.coarse = (4 * self.counts[0], 4 * self.counts[1], 32 * self.counts[2])
 
@@ -229,38 +230,63 @@
                 odd_ref[pz, rows, :] = jnp.where(even, to_left, to_right)
 
 
+def packed(pieces, following):
+    row = lax.broadcasted_iota(jnp.int32, (8, 128), 0)
+    row = jnp.where(following, row, 7 - row)
+    out = None
+    for value, first in pieces:
+        if out is None:
+            out = value
+        else:
+            moved = pltpu.roll(value, jnp.where(following, first, 8 - first), 0)
+            out = jnp.where(row >= first, moved, out)
+    return out
+
+
+def unpacked(value, first, following):
+    if first == 0:
+        return value
+    return pltpu.roll(value, jnp.where(following, 8 - first, first), 0)
+
+
 def z_pack_kernel(plan, *refs):
     near = plan.near
     beside = refs[:near]
     x_odd_ref, x_even_ref = refs[near : near + 2]
     outs = refs[-2:]
-    places = plan.y_places()[1]
+    own_row, places = plan.y_places()
     x_even = is_even("gx")
     z_even = is_even("grp")
     lanes_0, use_right = edge_send_lanes()
     for swap, out in enumerate(outs):
         top = z_even if swap == 0 else jnp.logical_not(z_even)
-        for a, deep, far, start, far_start in (
-            (1, M_DEEP, M_FAR, plan.starts[0], plan.starts[1]),
-            (0, R_DEEP, R_FAR, plan.starts[2], plan.starts[3]),
-        ):
-            for d in range(1, deep + 1):
-                plane = jnp.where(top, 16 - d, d - 1)
-                row = (d - 1) * plan.z_rows
-                for i, (side, _) in enumerate(places):
-                    to = start + row + 8 * i
-                    out[to : to + 8, :] = beside[i][a, plane, at(8 * (1 - side), 8), :]
-                    if d <= far:
-                        to = far_start + row + 8 * i
-                        out[to : to + 8, :] = beside[i][a, plane, at(8 * side, 8), :]
         lanes = lanes_0 + jnp.where(top, 12, 0)
+
+        def edge(pz, row):
+            even, odd = x_even_ref[pz, at(row, 8), :], x_odd_ref[pz, at(row, 8), :]
+            left = gather(jnp.where(x_even, odd, even), lanes)
+            right = gather(jnp.where(x_even, even, odd), lanes)
+            return jnp.where(use_right, right, left)
+
+        for i, (side, base) in enumerate(places):
+            following = side == 1
+            to = i * BESIDE_ROWS
+            for tiles, row in ((NEAR_TILES, 8 * (1 - side)), (FAR_TILES, 8 * side)):
+                for pieces in tiles:
+                    values = [
+                        (beside[i][a, jnp.where(top, 16 - d, d - 1), at(row, 8), :], first)
+                        for a, d, first in pieces
+                    ]
+                    out[to : to + 8, :] = packed(values, following)
+                    to += 8
+            values = [(edge(pz, base + 8 * side), 2 * pz) for pz in range(4)]
+            out[to : to + 8, :] = packed(values, following)
+        to = plan.edge_start
+        rows = [own_row, own_row + 8] + [base + 8 * (1 - side) for side, base in places]
         for pz in range(4):
-            for row in range(0, plan.rows, 8):
-                even, odd = x_even_ref[pz, row : row + 8, :], x_odd_ref[pz, row : row + 8, :]
-                left = gather(jnp.where(x_even, odd, even), lanes)
-                right = gather(jnp.where(x_even, even, odd), lanes)
-                to = plan.starts[4] + pz * plan.rows + row
-                out[to : to + 8, :] = jnp.where(use_right, right, left)
+            for row in rows:
+                out[to : to + 8, :] = edge(pz, row)
+                to += 8
 
 
 def padded_rows(plan, cells):
@@ -321,20 +347,22 @@
     lax.fori_loop(0, 4, body, 0)
 
 
+def inside_tile(plan, t):
+    tile = plan.tile
+    z, x = window_cells(t, tile)
+    here = z < ZW
+    z = z + (4 * lax.axis_index("grp") - HALO)
+    x = x + (32 * lax.axis_index("gx") - HALO)
+    here = here & (z >= 0) & (z < plan.coarse[0]) & (x >= 0) & (x < plan.coarse[2])
+    if plan.near == 2:
+        row = lax.broadcasted_iota(jnp.int32, (tile, 128), 0)
+        y = row + (4 * lax.axis_index("gy") - 4)
+        here = here & (row < plan.cells) & (y >= 0) & (y < plan.coarse[1])
+    return here
+
+
 def inside_mask(plan):
-    tile = plan.tile
-    masks = []
-    for t in range(3):
-        z, x = window_cells(t, tile)
-        here = z < ZW
-        z = z + (4 * lax.axis_index("grp") - HALO)
-        x = x + (32 * lax.axis_index("gx") - HALO)
-        here = here & (z >= 0) & (z < plan.coarse[0]) & (x >= 0) & (x < plan.coarse[2])
-        if plan.near == 2:
-            row = lax.broadcasted_iota(jnp.int32, (tile, 128), 0)
-            y = row + (4 * lax.axis_index("gy") - 4)
-            here = here & (row < plan.cells) & (y >= 0) & (y < plan.coarse[1])
-        masks.append(jnp.where(here, 1.0, 0.0))
+    masks = [jnp.where(inside_tile(plan, t), 1.0, 0.0) for t in range(3)]
     return jnp.concatenate(masks, axis=1) > 0.5
 
 
@@ -417,97 +445,107 @@
     return r_ref[a, b, c] - factor * (d_ref[a, b, c] * away)
 
 
-def down_kernel(plan, *refs):
-    own_ref, odd_own, even_own, odd_ref, even_ref = refs[:5]
-    chunk, m0, h0, e0, k0, m1, h1, e1, k1 = refs[5:14]
-    r0, d0, r1, d1, planes, sides = refs[14:]
+def place_halo(plan, swap, own_ref, z_own_ref, z_ref, planes, sides, emit):
     near, tile = plan.near, plan.tile
     own_row, places = plan.y_places()
-    z_even = is_even("grp")
-    inside = inside_mask(plan)
-
-    for side in range(2):
-        use_even = jnp.logical_not(z_even) if side == 0 else z_even
-
-        def read(rows, even=even_ref, odd=odd_ref):
-            return jnp.where(use_even, even[rows, :], odd[rows, :])
-
-        for a, deep, far, start, far_start, own_start in (
-            (1, M_DEEP, M_FAR, plan.starts[0], plan.starts[1], 0),
-            (0, R_DEEP, R_FAR, plan.starts[2], plan.starts[3], 16 * M_DEEP),
-        ):
-            for d in range(1, EDGE + 1):
-                plane = EDGE - d if side == 0 else d - 1
-                if d > far:
-                    planes[side, a, plane] = jnp.zeros((plan.rows, 128), F32)
-                if d > deep:
-                    continue
-                row = own_start + 16 * (d - 1)
-                planes[side, a, plane, at(own_row, 16), :] = read(
-                    slice(row, row + 16), even_own, odd_own
-                )
-                row = (d - 1) * plan.z_rows
-                for i, (y_side, base) in enumerate(places):
-                    row_i = start + row + 8 * i
-                    planes[side, a, plane, at(base + 8 * (1 - y_side), 8), :] = read(
-                        slice(row_i, row_i + 8)
+    upper = is_even("grp")
+    if swap == 1:
+        upper = jnp.logical_not(upper)
+
+    def choose(make):
+        return jnp.where(upper, make(1), make(0))
+
+    def plane_of(d):
+        return jnp.where(upper, d - 1, EDGE - d)
+
+    for a, deep, far in ((1, M_DEEP, M_FAR), (0, R_DEEP, R_FAR)):
+        for d in range(far + 1, EDGE + 1):
+            planes[a, plane_of(d)] = jnp.zeros((plan.rows, 128), F32)
+        for d in range(1, deep + 1):
+            row = 16 * (d - 1) if a == 1 else 16 * (M_DEEP + d - 1)
+            planes[a, plane_of(d), at(own_row, 16), :] = z_own_ref[row : row + 16, :]
+    for i, (side, base) in enumerate(places):
+        following = side == 1
+        row = i * BESIDE_ROWS
+        for tiles, to in ((NEAR_TILES, base + 8 * (1 - side)), (FAR_TILES, base + 8 * side)):
+            for pieces in tiles:
+                for a, d, first in pieces:
+                    planes[a, plane_of(d), at(to, 8), :] = unpacked(
+                        z_ref[row : row + 8, :], first, following
                     )
-                    if d <= far:
-                        row_i = far_start + row + 8 * i
-                        planes[side, a, plane, at(base + 8 * y_side, 8), :] = read(
-                            slice(row_i, row_i + 8)
-                        )
+                row += 8
         for pz in range(4):
-            row = plan.starts[4] + pz * plan.rows
-            sides[side, pz] = read(slice(row, row + plan.rows))
-
-    index = [[halo_lanes(side, z, tile) for z in range(HALO)] for side in range(2)]
-    turns = [[halo_turn(side, px, tile) for px in range(4)] for side in range(2)]
-    edge_index = [[edge_far_lanes(side, a, tile) for a in range(2)] for side in range(2)]
-    keep = []
-    for side, t in ((0, 0), (1, 2)):
-        z, _ = window_cells(t, tile)
+            sides[pz, at(base + 8 * side, 8), :] = unpacked(
+                z_ref[row : row + 8, :], 2 * pz, following
+            )
+    row = plan.edge_start
+    rows = [own_row, own_row + 8] + [base + 8 * (1 - side) for side, base in places]
+    for pz in range(4):
+        for to in rows:
+            sides[pz, at(to, 8), :] = z_ref[row : row + 8, :]
+            row += 8
+
+    index = [choose(lambda side: halo_lanes(side, z, tile)) for z in range(HALO)]
+    turns = [choose(lambda side: halo_turn(side, px, tile)) for px in range(4)]
+    edge_index = [choose(lambda side: edge_far_lanes(side, a, tile)) for a in range(2)]
+
+    def kept(side):
+        z, _ = window_cells(2 * side, tile)
         z = (z < HALO) if side == 0 else (z >= HALO + 4)
-        keep.append(z & inside[:, 128 * t : 128 * t + 128])
+        return (z & inside_tile(plan, 2 * side)).astype(jnp.int32)
+
+    keep = choose(kept) > 0
+    lanes = pl.ds(pl.multiple_of(jnp.where(upper, 256, 0), 128), 128)
 
     def place(pz, carry):
         for a in range(2):
             for py in range(4):
-                for side, t in ((0, 0), (1, 2)):
-                    lanes = slice(128 * t, 128 * t + 128)
-                    parts = [
-                        gather(
-                            every_fourth(plan, planes, (side, a, 4 * z + pz), py), index[side][z]
-                        )
-                        for z in range(HALO)
-                    ]
-                    edge = gather(
-                        every_fourth(plan, sides, (side, pz), py), edge_index[side][a]
-                    )
-                    for px in range(4):
-                        turn = turns[side][px]
-                        value = jnp.where(turn == 1, parts[1], parts[0])
-                        value = jnp.where(turn == 2, parts[2], value)
-                        value = jnp.where(turn == 3, edge, value)
-                        if px > 0:
-                            value = pltpu.roll(value, 128 - 32 * px, 1)
-                        value = jnp.where(
-                            keep[side], value, own_ref[a, pz, py, px, :, lanes]
-                        )
-                        if a == 1:
-                            m0[pz + 1, py + 1, px + 1, :, lanes] = value
-                        else:
-                            r0[pz, py, px, :, lanes] = value
+                parts = [
+                    gather(every_fourth(plan, planes, (a, 4 * z + pz), py), index[z])
+                    for z in range(HALO)
+                ]
+                edge = gather(every_fourth(plan, sides, (pz,), py), edge_index[a])
                 for px in range(4):
-                    lanes = slice(128, 256)
-                    value = own_ref[a, pz, py, px, :, lanes]
-                    if a == 1:
-                        m0[pz + 1, py + 1, px + 1, :, lanes] = value
-                    else:
-                        r0[pz, py, px, :, lanes] = value
+                    turn = turns[px]
+                    value = jnp.where(turn == 1, parts[1], parts[0])
+                    value = jnp.where(turn == 2, parts[2], value)
+                    value = jnp.where(turn == 3, edge, value)
+                    if px > 0:
+                        value = pltpu.roll(value, 128 - 32 * px, 1)
+                    value = jnp.where(keep, value, own_ref[a, pz, py, px, :, lanes])
+                    emit(a, pz, py, px, lanes, value)
         return carry
 
     lax.fori_loop(0, 4, place, 0)
+
+
+def place_kernel(plan, own_ref, z_own_ref, z_ref, out, planes, sides):
+    def emit(a, pz, py, px, lanes, value):
+        out[a, pz, py, px] = value
+
+    place_halo(plan, 1, own_ref, z_own_ref, z_ref, planes, sides, emit)
+
+
+def down_kernel(plan, *refs):
+    own_ref, other_ref, z_own_ref, z_ref = refs[:4]
+    chunk, m0, h0, e0, k0, m1, h1, e1, k1 = refs[4:13]
+    r0, d0, r1, d1, planes, sides = refs[13:]
+    tile = plan.tile
+    inside = inside_mask(plan)
+    rest = pl.ds(pl.multiple_of(jnp.where(is_even("grp"), 0, 256), 128), 128)
+
+    def emit(a, pz, py, px, lanes, value):
+        for lanes_i, value_i in (
+            (lanes, value),
+            (rest, other_ref[a, pz, py, px]),
+            (slice(128, 256), own_ref[a, pz, py, px, :, 128:256]),
+        ):
+            if a == 1:
+                m0[pz + 1, py + 1, px + 1, :, lanes_i] = value_i
+            else:
+                r0[pz, py, px, :, lanes_i] = value_i
+
+    place_halo(plan, 0, own_ref, z_own_ref, z_ref, planes, sides, emit)
 
     descend(plan, 4, 1.0, inside, m0, r0, d0, h0, e0, k0)
     for a, b, c in np.ndindex(2, 2, 2):
@@ -826,16 +864,27 @@
             *beside,
             *edges[::-1],
         )
+        halo_scratch = [(2, EDGE, plan.rows, 128), (4, plan.rows, 128)]
+        (other,) = call(
+            plan,
+            lambda *refs: place_kernel(plan, *refs),
+            [(2, 4, 4, 4, tile, 128)],
+            halo_scratch,
+            own,
+            z_own[1],
+            arrived[1],
+        )
         chunk, *state = call(
             plan,
             lambda *refs: down_kernel(plan, *refs),
             [(plan.devices, 8, 128)] + [full_rim] + [full] * 3 + [half_rim] + [half] * 3,
             [full] * 2
             + [half] * 2
-            + [(2, 2, EDGE, plan.rows, 128), (2, 4, plan.rows, 128)],
+            + halo_scratch,
             own,
-            *z_own[::-1],
-            *arrived[::-1],
+            other,
+            z_own[0],
+            arrived[0],
         )
         joined = lax.all_to_all(chunk, AXES, 0, 0, tiled=True)
         levels = [Level(plan, level) for level in range(2, LEVELS + 1)]

time: 43.6 us -> 42.1 us (0.966)
  waiting for transfers between devices: 5.05 us -> 3.7 us
  blocking collectives: 12.5 us -> 11.8 us
  Pallas kernels: 13.1 us -> 13.6 us
    ppermute x7, waiting for transfers between devices: 5.05 us -> 3.7 us  [swap(): return lax.ppermute(values, AXES, plan.pairs(swaps))]
    all_to_all x1, blocking collectives: 12.5 us -> 11.8 us  [on_device(): joined = lax.all_to_all(chunk, AXES, 0, 0, tiled=True)]
    pallas_call x6 -> x7, Pallas kernels: 13.1 us -> 13.6 us  [call(): pl.pallas_call(kernel, out_shape=[jax.ShapeDtypeStruct(shape, F32) for sh...]
  transfers between devices with their start and end apart: 7 -> 7, of which waited for: 4 -> 3; matrix products, arithmetic and copies ran while one was open for 0% -> 0% of each run, Pallas kernels for 8% -> 11%
where the time goes in v6:
time: 42.1 us; the launch traced here: 41.9 us
  Pallas kernels  13.6 us (32%)
  blocking collectives  11.8 us (28%)
  starting transfers between devices  11.7 us (28%)
  waiting for transfers between devices  3.7 us (9%)
  other arithmetic  0.99 us (2%)
    pallas_call x7, Pallas kernels, call(): pl.pallas_call(kernel, out_shape=[jax.ShapeDtypeStruct(shape, F32) for sh...  13.6 us
    all_to_all x1, blocking collectives, on_device(): joined = lax.all_to_all(chunk, AXES, 0, 0, tiled=True)  11.8 us
    ppermute x7, starting transfers between devices, swap(): return lax.ppermute(values, AXES, plan.pairs(swaps))  11.7 us
    ppermute x7, waiting for transfers between devices, swap(): return lax.ppermute(values, AXES, plan.pairs(swaps))  3.7 us
    another operation x1, other arithmetic, on_device(): cells = jnp.stack([residual, mobility])  0.99 us
  transfers between devices with their start and end apart: 7, of which 3 were waited for; matrix products, arithmetic and copies ran while one was open for 0% of the time, Pallas kernels for 11%

profile of v6, /device:TPU:0, one launch (start us, length us, event | category | flops | bytes accessed | tf_op | source)
XLA Modules:
  0.0 41.9 jit_solution(1869788501257054909)
XLA Ops:
  0.0 1.0 %pad_maximum_fusion.refs_0_ = f32[2,16,16,128]{3,2,1,0:T(8,128)S(1)} fusion(f32[1,16,16,128]{3,2,1,0:T(8,128)} %bitcast.2, f32[1,16,16,128]{3,2,1,0:T(8,128)} %bitcast.3), kind=kLoop, calls=%fused_computation | loop fusion | flops 65536 | bytes 524288 | tf_op jit(solution)/shard_map/stack | solution.py:829
  1.0 0.1 shard_map.28
  1.1 3.0 %collective-permute-start = (f32[352,128]{1,0:T(8,128)S(1)}, f32[352,128]{1,0:T(8,128)S(1)}, u32[]{:S(2)}, u32[]{:S(2)}) collective-permute-start(f32[352,128]{1,0:T(8,128)S(1)} %get-tuple-element.22), channel_id=1, source_target_pairs={{0,4},{1,5},{2,6},{3,7},{4,0},{5,1},{6,2},{7,3},{8,12},{9,13},{10,... | collective-permute-start | bytes 540680 | tf_op jit(solution)/shard_map/ppermute | solution.py:825
  4.1 0.0 collective-permute-start.3
  4.1 3.1 %collective-permute-start.4 = (f32[336,128]{1,0:T(8,128)S(1)}, f32[336,128]{1,0:T(8,128)S(1)}, u32[]{:S(2)}, u32[]{:S(2)}) collective-permute-start(f32[336,128]{1,0:T(8,128)S(1)} %get-tuple-element.27), channel_id=1, source_target_pairs={{0,8},{1,9},{2,10},{3,11},{4,12},{5,13},{6,14},{7,15},{8,0},{9,1},... | collective-permute-start | bytes 516104 | tf_op jit(solution)/shard_map/ppermute | solution.py:825
  7.2 1.4 %collective-permute-done.refs_1_ = f32[352,128]{1,0:T(8,128)S(1)} collective-permute-done((f32[352,128]{1,0:T(8,128)S(1)}, f32[352,128]{1,0:T(8,128)S(1)}, u32[]{:S(2)}, u32[]{:S(2)}) %collective-permute-start) | collective-permute-done | bytes 180256 | tf_op jit(solution)/shard_map/ppermute | solution.py:825
  8.6 0.3 shard_map.29
  9.0 0.3 collective-permute-start.1
  9.3 1.5 %collective-permute-start.2 = (f32[4,32,128]{2,1,0:T(8,128)S(1)}, f32[4,32,128]{2,1,0:T(8,128)S(1)}, u32[]{:S(2)}, u32[]{:S(2)}) collective-permute-start(f32[4,32,128]{2,1,0:T(8,128)S(1)} %get-tuple-element.25), channel_id=1, source_target_pairs={{0,1},{1,0},{2,3},{3,2},{4,5},{5,4},{6,7},{7,6},{8,9},{9,8},{10,11... | collective-permute-start | bytes 196616 | tf_op jit(solution)/shard_map/ppermute | solution.py:825
  10.9 0.0 collective-permute-done.3.refs_4_.refs_1_
  10.9 0.2 collective-permute-done.4.refs_3_.refs_2_
  11.1 2.1 %collective-permute-done.1.refs_2_.refs_1_ = f32[4,32,128]{2,1,0:T(8,128)S(1)} collective-permute-done((f32[4,32,128]{2,1,0:T(8,128)S(1)}, f32[4,32,128]{2,1,0:T(8,128)S(1)}, u32[]{:S(2)}, u32[]{:S(2)}) %collective-permute-start.1) | collective-permute-done | bytes 65568 | tf_op jit(solution)/shard_map/ppermute | solution.py:825
  13.2 0.0 collective-permute-done.2.refs_3_.refs_2_
  13.2 0.2 shard_map.31
  13.3 0.2 collective-permute-start.5
  13.5 3.5 %collective-permute-start.6 = (f32[248,128]{1,0:T(8,128)S(1)}, f32[248,128]{1,0:T(8,128)S(1)}, u32[]{:S(2)}, u32[]{:S(2)}) collective-permute-start(f32[248,128]{1,0:T(8,128)S(1)} %get-tuple-element.29), channel_id=1, source_target_pairs={{0,8},{1,9},{2,10},{3,11},{4,12},{5,13},{6,14},{7,15},{8,0},{9,1},... | collective-permute-start | bytes 380936 | tf_op jit(solution)/shard_map/ppermute | solution.py:825
  17.0 3.2 %shard_map.30.refs_0_ = f32[2,4,4,4,8,384]{5,4,3,2,1,0:T(8,128)S(1)} custom-call(f32[2,16,16,128]{3,2,1,0:T(8,128)S(1)} %pad_maximum_fusion.refs_0_, f32[2,16,16,128]{3,2,1,0:T(8,128)S(1)} %get-tuple-element.23.refs_1_.refs_0_, f32[4,32,128]{2,1,0:T(8,128)S(1)} %collective-permute-done.1.refs_2_.refs_1_, f32[4,32,128]{2,1,0:T(8,128)S(1)} %collective-permute-done.2.refs_3_.refs_2_), custom_call_target="tpu_custom_call" | custom-call | tf_op jit(solution)/shard_map/pallas_call | solution.py:805
  20.2 0.0 collective-permute-done.5.refs_2_
  20.2 0.9 %shard_map.32.refs_1_ = f32[2,4,4,4,8,128]{5,4,3,2,1,0:T(8,128)S(1)} custom-call(f32[2,4,4,4,8,384]{5,4,3,2,1,0:T(8,128)S(1)} %shard_map.30.refs_0_, f32[336,128]{1,0:T(8,128)S(1)} %collective-permute-done.3.refs_4_.refs_1_, f32[248,128]{1,0:T(8,128)S(1)} %collective-permute-done.5.refs_2_), custom_call_target="tpu_custom_call" | custom-call | tf_op jit(solution)/shard_map/pallas_call | solution.py:805
  21.1 0.0 collective-permute-done.6.refs_3_
  21.1 3.3 %shard_map.33 = (f32[32,8,128]{2,1,0:T(8,128)S(1)}, f32[6,6,6,8,384]{4,3,2,1,0:T(8,128)S(1)}, f32[4,4,4,8,384]{4,3,2,1,0:T(8,128)S(1)}, f32[4,4,4,8,384]{4,3,2,1...) custom-call(f32[2,4,4,4,8,384]{5,4,3,2,1,0:T(8,128)S(1)} %shard_map., ...), custom_call_target="tpu_custom_call" | custom-call | tf_op jit(solution)/shard_map/pallas_call | solution.py:805
  24.4 11.8 %all_to_all.5.refs_0_ = f32[32,8,128]{2,1,0:T(8,128)S(1)} all-to-all(f32[32,8,128]{2,1,0:T(8,128)S(1)} %get-tuple-element.30), channel_id=1, replica_groups=mesh['grp'=4,'gy'=2,'gx'=4] {'grp','gy','gx'}, dimensions={0} | all-to-all | bytes 262144 | tf_op jit(solution)/shard_map/all_to_all | solution.py:889
  36.2 5.7 %shard_map.34 = f32[16,16,128]{2,1,0:T(8,128)} custom-call(f32[32,8,128]{2,1,0:T(8,128)S(1)} %all_to_all.5.refs_0_, f32[6,6,6,8,384]{4,3,2,1,0:T(8,128)S(1)} %get-tuple-element.31.refs_1_, f32[4,4,4,8,384]{4,3,2,1,0:T(8,128)S(1)} %get-tuple-element.32.refs_2_, f32[4,4,4,8,384]{4,3,2,1,0:T(8,128)S(1)} %get-tuple-element.33.refs_3_, ...), custom_call_target="tpu_custom_call" | custom-call | tf_op jit(solution)/shard_map/pallas_call | solution.py:805
Async XLA Ops:
  1.1 7.6 %collective-permute-start = (f32[352,128]{1,0:T(8,128)S(1)}, f32[352,128]{1,0:T(8,128)S(1)}, u32[]{:S(2)}, u32[]{:S(2)}) collective-permute-start(f32[352,128]{1,0:T(8,128)S(1)} %get-tuple-element.22), channel_id=1, source_target_pairs={{0,4},{1,5},{2,6},{3,7},{4,0},{5,1},{6,2},{7,3},{8,12},{9,13},{10,... | collective-permute-start | bytes 540680 | tf_op jit(solution)/shard_map/ppermute | solution.py:825
  4.1 6.8 %collective-permute-start.3 = (f32[336,128]{1,0:T(8,128)S(1)}, f32[336,128]{1,0:T(8,128)S(1)}, u32[]{:S(2)}, u32[]{:S(2)}) collective-permute-start(f32[336,128]{1,0:T(8,128)S(1)} %get-tuple-element.26), channel_id=1, source_target_pairs={{0,1},{1,0},{2,3},{3,2},{4,5},{5,4},{6,7},{7,6},{8,16},{9,17},{10,... | collective-permute-start | bytes 516104 | tf_op jit(solution)/shard_map/ppermute | solution.py:825
  4.1 7.0 %collective-permute-start.4 = (f32[336,128]{1,0:T(8,128)S(1)}, f32[336,128]{1,0:T(8,128)S(1)}, u32[]{:S(2)}, u32[]{:S(2)}) collective-permute-start(f32[336,128]{1,0:T(8,128)S(1)} %get-tuple-element.27), channel_id=1, source_target_pairs={{0,8},{1,9},{2,10},{3,11},{4,12},{5,13},{6,14},{7,15},{8,0},{9,1},... | collective-permute-start | bytes 516104 | tf_op jit(solution)/shard_map/ppermute | solution.py:825
  9.0 4.2 %collective-permute-start.1 = (f32[4,32,128]{2,1,0:T(8,128)S(1)}, f32[4,32,128]{2,1,0:T(8,128)S(1)}, u32[]{:S(2)}, u32[]{:S(2)}) collective-permute-start(f32[4,32,128]{2,1,0:T(8,128)S(1)} %get-tuple-element.24), channel_id=1, source_target_pairs={{0,3},{1,2},{2,1},{3,0},{4,7},{5,6},{6,5},{7,4},{8,11},{9,10},{10,... | collective-permute-start | bytes 196616 | tf_op jit(solution)/shard_map/ppermute | solution.py:825
  9.3 3.8 %collective-permute-start.2 = (f32[4,32,128]{2,1,0:T(8,128)S(1)}, f32[4,32,128]{2,1,0:T(8,128)S(1)}, u32[]{:S(2)}, u32[]{:S(2)}) collective-permute-start(f32[4,32,128]{2,1,0:T(8,128)S(1)} %get-tuple-element.25), channel_id=1, source_target_pairs={{0,1},{1,0},{2,3},{3,2},{4,5},{5,4},{6,7},{7,6},{8,9},{9,8},{10,11... | collective-permute-start | bytes 196616 | tf_op jit(solution)/shard_map/ppermute | solution.py:825
  13.3 6.9 %collective-permute-start.5 = (f32[248,128]{1,0:T(8,128)S(1)}, f32[248,128]{1,0:T(8,128)S(1)}, u32[]{:S(2)}, u32[]{:S(2)}) collective-permute-start(f32[248,128]{1,0:T(8,128)S(1)} %get-tuple-element.28), channel_id=1, source_target_pairs={{0,1},{1,0},{2,3},{3,2},{4,5},{5,4},{6,7},{7,6},{8,16},{9,17},{10,... | collective-permute-start | bytes 380936 | tf_op jit(solution)/shard_map/ppermute | solution.py:825
  13.5 7.6 %collective-permute-start.6 = (f32[248,128]{1,0:T(8,128)S(1)}, f32[248,128]{1,0:T(8,128)S(1)}, u32[]{:S(2)}, u32[]{:S(2)}) collective-permute-start(f32[248,128]{1,0:T(8,128)S(1)} %get-tuple-element.29), channel_id=1, source_target_pairs={{0,8},{1,9},{2,10},{3,11},{4,12},{5,13},{6,14},{7,15},{8,0},{9,1},... | collective-permute-start | bytes 380936 | tf_op jit(solution)/shard_map/ppermute | solution.py:825

commit v7 on v6

--- a/solution.py
+++ b/solution.py
@@ -171,7 +171,27 @@
     return pl.ds(pl.multiple_of(start, 8), size)
 
 
+def x_edge(block, pz, half, to_right):
+    out = jnp.zeros((8, 128), F32)
+    for a in range(2):
+        for z in range(4):
+            cells = block[a, 4 * z + pz, 8 * half : 8 * half + 8, :]
+            base = a * 48 + z * 12
+            moved = jnp.where(
+                to_right, pltpu.roll(cells, (base - (128 - EDGE)) % 128, 1), pltpu.roll(cells, base, 1)
+            )
+            out = jnp.where(between(base, base + EDGE), moved, out)
+    return out
+
+
 def first_kernel(plan, cells_ref, *outs):
+    *outs, edge_ref = outs
+    for pz in range(4):
+        for half in range(2):
+            rows = slice(8 * half, 8 * half + 8)
+            edge_ref[pz, rows, :] = x_edge(
+                cells_ref, pz, half, jnp.logical_not(is_even("gx"))
+            )
     z_even = is_even("grp")
     for swap, out in enumerate(outs[:2]):
         top = z_even if swap == 0 else jnp.logical_not(z_even)
@@ -194,8 +214,10 @@
 
 def edges_kernel(plan, *refs):
     cells_ref = refs[0]
-    arrived = refs[1 : 1 + plan.near]
-    beside = refs[1 + plan.near : 1 + 2 * plan.near]
+    near = plan.near
+    arrived = refs[1 : 1 + near]
+    x_arrived = refs[1 + near : 2 + 2 * near]
+    beside = refs[2 + 2 * near : 2 + 3 * near]
     even_ref, odd_ref = refs[-2:]
     own_row, places = plan.y_places()
     even = is_even("gx")
@@ -213,21 +235,10 @@
                 out[a, plane, 8:16, :] = jnp.where(following, after, rows)
     for i, block in enumerate((cells_ref, *beside)):
         start = own_row if i == 0 else places[i - 1][1]
+        odd_ref[:, at(start, 16), :] = x_arrived[i][...]
         for pz in range(4):
             for half in range(2):
-                to_right = jnp.zeros((8, 128), F32)
-                to_left = jnp.zeros((8, 128), F32)
-                for a in range(2):
-                    for z in range(4):
-                        cells = block[a, 4 * z + pz, 8 * half : 8 * half + 8, :]
-                        base = a * 48 + z * 12
-                        here = between(base, base + EDGE)
-                        shift = (base - (128 - EDGE)) % 128
-                        to_right = jnp.where(here, pltpu.roll(cells, shift, 1), to_right)
-                        to_left = jnp.where(here, pltpu.roll(cells, base, 1), to_left)
-                rows = at(start + 8 * half, 8)
-                even_ref[pz, rows, :] = jnp.where(even, to_right, to_left)
-                odd_ref[pz, rows, :] = jnp.where(even, to_left, to_right)
+                even_ref[pz, at(start + 8 * half, 8), :] = x_edge(block, pz, half, even)
 
 
 def packed(pieces, following):
@@ -827,14 +838,15 @@
     def on_device(residual, mobility):
         assert residual.shape == (16, 16, 128)
         cells = jnp.stack([residual, mobility])
-        even, odd, *rows = call(
+        even, odd, *rows, x_odd = call(
             plan,
             lambda *refs: first_kernel(plan, *refs),
-            [(16 * (M_DEEP + R_DEEP), 128)] * 2 + [(2 * Y_ROWS, 128)] * near,
+            [(16 * (M_DEEP + R_DEEP), 128)] * 2 + [(2 * Y_ROWS, 128)] * near + [(4, 16, 128)],
             [],
             cells,
         )
         arrived = [swap(values, None, y, None) for y, values in enumerate(rows)]
+        x_arrived = [swap(x_odd, None, y, 1) for y in (None, *range(near))]
         z_own = [swap(odd, 1, None, None), swap(even, 0, None, None)][::-1]
         *beside, even, odd = call(
             plan,
@@ -843,8 +855,9 @@
             [],
             cells,
             *arrived,
+            *x_arrived,
         )
-        edges = [swap(odd, None, None, 1), swap(even, None, None, 0)][::-1]
+        edges = [swap(even, None, None, 0), odd]
         sends = call(
             plan,
             lambda *refs: z_pack_kernel(plan, *refs),

time: 42.1 us -> 40.5 us (0.962)
  starting transfers between devices: 11.7 us -> 10.5 us
    ppermute x7 -> x8, starting transfers between devices: 11.7 us -> 10.5 us  [swap(): return lax.ppermute(values, AXES, plan.pairs(swaps))]
    ppermute x7 -> x8, waiting for transfers between devices: 3.7 us -> 3.46 us  [swap(): return lax.ppermute(values, AXES, plan.pairs(swaps))]
  transfers between devices with their start and end apart: 7 -> 8, of which waited for: 3 -> 2; matrix products, arithmetic and copies ran while one was open for 0% -> 0% of each run, Pallas kernels for 11% -> 11%
where the time goes in v7:
time: 40.5 us; the launch traced here: 40.3 us
  Pallas kernels  13.8 us (34%)
  blocking collectives  11.5 us (28%)
  starting transfers between devices  10.5 us (26%)
  waiting for transfers between devices  3.46 us (9%)
  other arithmetic  0.99 us (2%)
    pallas_call x7, Pallas kernels, call(): pl.pallas_call(kernel, out_shape=[jax.ShapeDtypeStruct(shape, F32) for sh...  13.8 us
    all_to_all x1, blocking collectives, on_device(): joined = lax.all_to_all(chunk, AXES, 0, 0, tiled=True)  11.5 us
    ppermute x8, starting transfers between devices, swap(): return lax.ppermute(values, AXES, plan.pairs(swaps))  10.5 us
    ppermute x8, waiting for transfers between devices, swap(): return lax.ppermute(values, AXES, plan.pairs(swaps))  3.46 us
    another operation x1, other arithmetic, on_device(): cells = jnp.stack([residual, mobility])  0.99 us
  transfers between devices with their start and end apart: 8, of which 2 were waited for; matrix products, arithmetic and copies ran while one was open for 0% of the time, Pallas kernels for 11%

profile of v7, /device:TPU:0, one launch (start us, length us, event | category | flops | bytes accessed | tf_op | source)
XLA Modules:
  0.0 40.3 jit_solution(8053903392256687381)
XLA Ops:
  0.0 1.0 %pad_maximum_fusion.refs_0_ = f32[2,16,16,128]{3,2,1,0:T(8,128)S(1)} fusion(f32[1,16,16,128]{3,2,1,0:T(8,128)} %bitcast.2, f32[1,16,16,128]{3,2,1,0:T(8,128)} %bitcast.3), kind=kLoop, calls=%fused_computation | loop fusion | flops 65536 | bytes 524288 | tf_op jit(solution)/shard_map/stack | solution.py:840
  1.0 0.2 shard_map.28
  1.2 3.0 %collective-permute-start = (f32[352,128]{1,0:T(8,128)S(1)}, f32[352,128]{1,0:T(8,128)S(1)}, u32[]{:S(2)}, u32[]{:S(2)}) collective-permute-start(f32[352,128]{1,0:T(8,128)S(1)} %get-tuple-element.23), channel_id=1, source_target_pairs={{0,4},{1,5},{2,6},{3,7},{4,0},{5,1},{6,2},{7,3},{8,12},{9,13},{10,... | collective-permute-start | bytes 540680 | tf_op jit(solution)/shard_map/ppermute | solution.py:836
  4.2 0.0 collective-permute-start.4
  4.2 3.1 %collective-permute-start.5 = (f32[336,128]{1,0:T(8,128)S(1)}, f32[336,128]{1,0:T(8,128)S(1)}, u32[]{:S(2)}, u32[]{:S(2)}) collective-permute-start(f32[336,128]{1,0:T(8,128)S(1)} %get-tuple-element.29), channel_id=1, source_target_pairs={{0,8},{1,9},{2,10},{3,11},{4,12},{5,13},{6,14},{7,15},{8,0},{9,1},... | collective-permute-start | bytes 516104 | tf_op jit(solution)/shard_map/ppermute | solution.py:836
  7.4 0.0 collective-permute-start.2
  7.4 1.7 %collective-permute-start.1 = (f32[4,16,128]{2,1,0:T(8,128)S(1)}, f32[4,16,128]{2,1,0:T(8,128)S(1)}, u32[]{:S(2)}, u32[]{:S(2)}) collective-permute-start(f32[4,16,128]{2,1,0:T(8,128)S(1)} %get-tuple-element.24), channel_id=1, source_target_pairs={{0,3},{1,2},{2,1},{3,0},{4,7},{5,6},{6,5},{7,4},{8,11},{9,10},{10,... | collective-permute-start | bytes 98312 | tf_op jit(solution)/shard_map/ppermute | solution.py:836
  9.1 2.5 %collective-permute-done.2.refs_3_ = f32[4,16,128]{2,1,0:T(8,128)S(1)} collective-permute-done((f32[4,16,128]{2,1,0:T(8,128)S(1)}, f32[4,16,128]{2,1,0:T(8,128)S(1)}, u32[]{:S(2)}, u32[]{:S(2)}) %collective-permute-start.2) | collective-permute-done | bytes 32800 | tf_op jit(solution)/shard_map/ppermute | solution.py:836
  11.6 0.0 collective-permute-done.1.refs_2_
  11.6 0.0 collective-permute-done.refs_1_
  11.6 0.3 shard_map.29
  12.0 0.7 %collective-permute-start.3 = (f32[4,32,128]{2,1,0:T(8,128)S(1)}, f32[4,32,128]{2,1,0:T(8,128)S(1)}, u32[]{:S(2)}, u32[]{:S(2)}) collective-permute-start(f32[4,32,128]{2,1,0:T(8,128)S(1)} %get-tuple-element.27), channel_id=1, source_target_pairs={{0,1},{1,0},{2,3},{3,2},{4,5},{5,4},{6,7},{7,6},{8,9},{9,8},{10,11... | collective-permute-start | bytes 196616 | tf_op jit(solution)/shard_map/ppermute | solution.py:836
  12.7 0.0 collective-permute-done.4.refs_4_.refs_1_
  12.7 0.0 collective-permute-done.5.refs_3_.refs_2_
  12.7 0.9 %collective-permute-done.3.refs_3_.refs_2_ = f32[4,32,128]{2,1,0:T(8,128)S(1)} collective-permute-done((f32[4,32,128]{2,1,0:T(8,128)S(1)}, f32[4,32,128]{2,1,0:T(8,128)S(1)}, u32[]{:S(2)}, u32[]{:S(2)}) %collective-permute-start.3) | collective-permute-done | bytes 65568 | tf_op jit(solution)/shard_map/ppermute | solution.py:836
  13.6 0.2 shard_map.31
  13.7 0.4 %collective-permute-start.6 = (f32[248,128]{1,0:T(8,128)S(1)}, f32[248,128]{1,0:T(8,128)S(1)}, u32[]{:S(2)}, u32[]{:S(2)}) collective-permute-start(f32[248,128]{1,0:T(8,128)S(1)} %get-tuple-element.30), channel_id=1, source_target_pairs={{0,1},{1,0},{2,3},{3,2},{4,5},{5,4},{6,7},{7,6},{8,16},{9,17},{10,... | collective-permute-start | bytes 380936 | tf_op jit(solution)/shard_map/ppermute | solution.py:836
  14.2 1.5 %collective-permute-start.7 = (f32[248,128]{1,0:T(8,128)S(1)}, f32[248,128]{1,0:T(8,128)S(1)}, u32[]{:S(2)}, u32[]{:S(2)}) collective-permute-start(f32[248,128]{1,0:T(8,128)S(1)} %get-tuple-element.31), channel_id=1, source_target_pairs={{0,8},{1,9},{2,10},{3,11},{4,12},{5,13},{6,14},{7,15},{8,0},{9,1},... | collective-permute-start | bytes 380936 | tf_op jit(solution)/shard_map/ppermute | solution.py:836
  15.6 3.2 %shard_map.30.refs_0_ = f32[2,4,4,4,8,384]{5,4,3,2,1,0:T(8,128)S(1)} custom-call(f32[2,16,16,128]{3,2,1,0:T(8,128)S(1)} %pad_maximum_fusion.refs_0_, f32[2,16,16,128]{3,2,1,0:T(8,128)S(1)} %get-tuple-element.25.refs_1_.refs_0_, f32[4,32,128]{2,1,0:T(8,128)S(1)} %get-tuple-element.26.refs_2_.refs_1_, f32[4,32,128]{2,1,0:T(8,128)S(1)} %collective-permute-done.3.refs_3_.refs_2_), custom_call_target="tpu_custom_call" | custom-call | tf_op jit(solution)/shard_map/pallas_call | solution.py:816
  18.8 0.0 collective-permute-done.6.refs_2_
  18.8 0.9 %shard_map.32.refs_1_ = f32[2,4,4,4,8,128]{5,4,3,2,1,0:T(8,128)S(1)} custom-call(f32[2,4,4,4,8,384]{5,4,3,2,1,0:T(8,128)S(1)} %shard_map.30.refs_0_, f32[336,128]{1,0:T(8,128)S(1)} %collective-permute-done.4.refs_4_.refs_1_, f32[248,128]{1,0:T(8,128)S(1)} %collective-permute-done.6.refs_2_), custom_call_target="tpu_custom_call" | custom-call | tf_op jit(solution)/shard_map/pallas_call | solution.py:816
  19.8 0.0 collective-permute-done.7.refs_3_
  19.8 3.3 %shard_map.33 = (f32[32,8,128]{2,1,0:T(8,128)S(1)}, f32[6,6,6,8,384]{4,3,2,1,0:T(8,128)S(1)}, f32[4,4,4,8,384]{4,3,2,1,0:T(8,128)S(1)}, f32[4,4,4,8,384]{4,3,2,1...) custom-call(f32[2,4,4,4,8,384]{5,4,3,2,1,0:T(8,128)S(1)} %shard_map., ...), custom_call_target="tpu_custom_call" | custom-call | tf_op jit(solution)/shard_map/pallas_call | solution.py:816
  23.1 11.5 %all_to_all.5.refs_0_ = f32[32,8,128]{2,1,0:T(8,128)S(1)} all-to-all(f32[32,8,128]{2,1,0:T(8,128)S(1)} %get-tuple-element.32), channel_id=1, replica_groups=mesh['grp'=4,'gy'=2,'gx'=4] {'grp','gy','gx'}, dimensions={0} | all-to-all | bytes 262144 | tf_op jit(solution)/shard_map/all_to_all | solution.py:902
  34.6 5.7 %shard_map.34 = f32[16,16,128]{2,1,0:T(8,128)} custom-call(f32[32,8,128]{2,1,0:T(8,128)S(1)} %all_to_all.5.refs_0_, f32[6,6,6,8,384]{4,3,2,1,0:T(8,128)S(1)} %get-tuple-element.33.refs_1_, f32[4,4,4,8,384]{4,3,2,1,0:T(8,128)S(1)} %get-tuple-element.34.refs_2_, f32[4,4,4,8,384]{4,3,2,1,0:T(8,128)S(1)} %get-tuple-element.35.refs_3_, ...), custom_call_target="tpu_custom_call" | custom-call | tf_op jit(solution)/shard_map/pallas_call | solution.py:816
Async XLA Ops:
  1.2 10.4 %collective-permute-start = (f32[352,128]{1,0:T(8,128)S(1)}, f32[352,128]{1,0:T(8,128)S(1)}, u32[]{:S(2)}, u32[]{:S(2)}) collective-permute-start(f32[352,128]{1,0:T(8,128)S(1)} %get-tuple-element.23), channel_id=1, source_target_pairs={{0,4},{1,5},{2,6},{3,7},{4,0},{5,1},{6,2},{7,3},{8,12},{9,13},{10,... | collective-permute-start | bytes 540680 | tf_op jit(solution)/shard_map/ppermute | solution.py:836
  4.2 8.4 %collective-permute-start.4 = (f32[336,128]{1,0:T(8,128)S(1)}, f32[336,128]{1,0:T(8,128)S(1)}, u32[]{:S(2)}, u32[]{:S(2)}) collective-permute-start(f32[336,128]{1,0:T(8,128)S(1)} %get-tuple-element.28), channel_id=1, source_target_pairs={{0,1},{1,0},{2,3},{3,2},{4,5},{5,4},{6,7},{7,6},{8,16},{9,17},{10,... | collective-permute-start | bytes 516104 | tf_op jit(solution)/shard_map/ppermute | solution.py:836
  4.2 8.4 %collective-permute-start.5 = (f32[336,128]{1,0:T(8,128)S(1)}, f32[336,128]{1,0:T(8,128)S(1)}, u32[]{:S(2)}, u32[]{:S(2)}) collective-permute-start(f32[336,128]{1,0:T(8,128)S(1)} %get-tuple-element.29), channel_id=1, source_target_pairs={{0,8},{1,9},{2,10},{3,11},{4,12},{5,13},{6,14},{7,15},{8,0},{9,1},... | collective-permute-start | bytes 516104 | tf_op jit(solution)/shard_map/ppermute | solution.py:836
  7.4 4.2 %collective-permute-start.2 = (f32[4,16,128]{2,1,0:T(8,128)S(1)}, f32[4,16,128]{2,1,0:T(8,128)S(1)}, u32[]{:S(2)}, u32[]{:S(2)}) collective-permute-start(f32[4,16,128]{2,1,0:T(8,128)S(1)} %get-tuple-element.24), channel_id=1, source_target_pairs={{0,7},{1,6},{2,5},{3,4},{4,3},{5,2},{6,1},{7,0},{8,15},{9,14},{10,... | collective-permute-start | bytes 98312 | tf_op jit(solution)/shard_map/ppermute | solution.py:836
  7.4 4.2 %collective-permute-start.1 = (f32[4,16,128]{2,1,0:T(8,128)S(1)}, f32[4,16,128]{2,1,0:T(8,128)S(1)}, u32[]{:S(2)}, u32[]{:S(2)}) collective-permute-start(f32[4,16,128]{2,1,0:T(8,128)S(1)} %get-tuple-element.24), channel_id=1, source_target_pairs={{0,3},{1,2},{2,1},{3,0},{4,7},{5,6},{6,5},{7,4},{8,11},{9,10},{10,... | collective-permute-start | bytes 98312 | tf_op jit(solution)/shard_map/ppermute | solution.py:836
  12.0 1.6 %collective-permute-start.3 = (f32[4,32,128]{2,1,0:T(8,128)S(1)}, f32[4,32,128]{2,1,0:T(8,128)S(1)}, u32[]{:S(2)}, u32[]{:S(2)}) collective-permute-start(f32[4,32,128]{2,1,0:T(8,128)S(1)} %get-tuple-element.27), channel_id=1, source_target_pairs={{0,1},{1,0},{2,3},{3,2},{4,5},{5,4},{6,7},{7,6},{8,9},{9,8},{10,11... | collective-permute-start | bytes 196616 | tf_op jit(solution)/shard_map/ppermute | solution.py:836
  13.7 5.1 %collective-permute-start.6 = (f32[248,128]{1,0:T(8,128)S(1)}, f32[248,128]{1,0:T(8,128)S(1)}, u32[]{:S(2)}, u32[]{:S(2)}) collective-permute-start(f32[248,128]{1,0:T(8,128)S(1)} %get-tuple-element.30), channel_id=1, source_target_pairs={{0,1},{1,0},{2,3},{3,2},{4,5},{5,4},{6,7},{7,6},{8,16},{9,17},{10,... | collective-permute-start | bytes 380936 | tf_op jit(solution)/shard_map/ppermute | solution.py:836
  14.2 5.6 %collective-permute-start.7 = (f32[248,128]{1,0:T(8,128)S(1)}, f32[248,128]{1,0:T(8,128)S(1)}, u32[]{:S(2)}, u32[]{:S(2)}) collective-permute-start(f32[248,128]{1,0:T(8,128)S(1)} %get-tuple-element.31), channel_id=1, source_target_pairs={{0,8},{1,9},{2,10},{3,11},{4,12},{5,13},{6,14},{7,15},{8,0},{9,1},... | collective-permute-start | bytes 380936 | tf_op jit(solution)/shard_map/ppermute | solution.py:836

commit v8 on v7

--- a/solution.py
+++ b/solution.py
@@ -27,8 +27,10 @@
 FAR_TILES = [[(1, 1, 0), (1, 2, 3), (0, 1, 6)], [(0, 2, 0), (1, 3, 2), (0, 3, 4), (1, 4, 5)]]
 BESIDE_ROWS = 8 * (len(NEAR_TILES) + len(FAR_TILES) + 1)
 M_EDGE, R_EDGE = 11, 10
-Y_FAR = 3
-Y_ROWS = 16 * (8 + Y_FAR)
+Y_FAR = (2, 3)
+Y_STARTS = (0, 16 * (8 + Y_FAR[0]))
+Y_ROWS = Y_STARTS[1] + 16 * (8 + Y_FAR[1])
+DIAGONAL_ROWS = 48
 
 
 def lane_iota(rows=8):
@@ -185,12 +187,19 @@
 
 
 def first_kernel(plan, cells_ref, *outs):
-    *outs, edge_ref = outs
+    outs, edge_ref, diagonal = outs[: 2 + plan.near], outs[2 + plan.near], outs[3 + plan.near :]
+    to_right = jnp.logical_not(is_even("gx"))
+    edges = [[x_edge(cells_ref, pz, half, to_right) for half in range(2)] for pz in range(4)]
     for pz in range(4):
-        for half in range(2):
-            rows = slice(8 * half, 8 * half + 8)
-            edge_ref[pz, rows, :] = x_edge(
-                cells_ref, pz, half, jnp.logical_not(is_even("gx"))
+        edge_ref[pz, 0:8, :], edge_ref[pz, 8:16, :] = edges[pz]
+    for out, (side, _) in zip(diagonal, plan.y_places()[1]):
+        last = side == 1
+        for pz in range(4):
+            out[8 * pz : 8 * pz + 8, :] = jnp.where(last, edges[pz][1], edges[pz][0])
+        for i in range(2):
+            far = [jnp.where(last, edges[pz][0], edges[pz][1]) for pz in (2 * i, 2 * i + 1)]
+            out[32 + 8 * i : 40 + 8 * i, :] = packed(
+                [(far[0], 0), (far[1], 3)], jnp.logical_not(last)
             )
     z_even = is_even("grp")
     for swap, out in enumerate(outs[:2]):
@@ -203,13 +212,13 @@
     for out, (side, _) in zip(outs[2:], plan.y_places()[1]):
         last = side == 1
         for a in range(2):
-            near, far = a * Y_ROWS, a * Y_ROWS + 128
+            near, far, deep = Y_STARTS[a], Y_STARTS[a] + 128, Y_FAR[a]
             for plane in range(16):
                 cells = cells_ref[a, plane]
                 rows = jnp.where(last, cells[8:16], cells[0:8])
                 out[near + 8 * plane : near + 8 * plane + 8, :] = rows
-                rows = jnp.where(last, cells[8 - Y_FAR : 8], cells[8 : 8 + Y_FAR])
-                out[far + Y_FAR * plane : far + Y_FAR * (plane + 1), :] = rows
+                rows = jnp.where(last, cells[8 - deep : 8], cells[8 : 8 + deep])
+                out[far + deep * plane : far + deep * (plane + 1), :] = rows
 
 
 def edges_kernel(plan, *refs):
@@ -224,18 +233,28 @@
     for ref, out, (side, _) in zip(arrived, beside, places):
         following = side == 1
         for a in range(2):
-            near, far = a * Y_ROWS, a * Y_ROWS + 128
+            near_row, far, deep = Y_STARTS[a], Y_STARTS[a] + 128, Y_FAR[a]
             for plane in range(16):
-                rows = ref[near + 8 * plane : near + 8 * plane + 8, :]
-                more = ref[far + Y_FAR * plane : far + Y_FAR * (plane + 1), :]
-                none = jnp.zeros((8 - Y_FAR, 128), F32)
+                rows = ref[near_row + 8 * plane : near_row + 8 * plane + 8, :]
+                more = ref[far + deep * plane : far + deep * (plane + 1), :]
+                none = jnp.zeros((8 - deep, 128), F32)
                 after = jnp.concatenate([more, none], axis=0)
                 before = jnp.concatenate([none, more], axis=0)
                 out[a, plane, 0:8, :] = jnp.where(following, rows, before)
                 out[a, plane, 8:16, :] = jnp.where(following, after, rows)
     for i, block in enumerate((cells_ref, *beside)):
         start = own_row if i == 0 else places[i - 1][1]
-        odd_ref[:, at(start, 16), :] = x_arrived[i][...]
+        if i == 0:
+            odd_ref[:, at(start, 16), :] = x_arrived[0][...]
+        else:
+            side = places[i - 1][0]
+            ref = x_arrived[i]
+            for pz in range(4):
+                odd_ref[pz, at(start + 8 * (1 - side), 8), :] = ref[8 * pz : 8 * pz + 8, :]
+                row = 32 + 8 * (pz // 2)
+                odd_ref[pz, at(start + 8 * side, 8), :] = unpacked(
+                    ref[row : row + 8, :], 3 * (pz % 2), side == 1
+                )
         for pz in range(4):
             for half in range(2):
                 even_ref[pz, at(start + 8 * half, 8), :] = x_edge(block, pz, half, even)
@@ -668,16 +687,15 @@
     return gather(flat, index(lane)).reshape(values.shape)
 
 
-def coarsen(values, fine, coarse, fine_ref, coarse_ref):
+def coarsen(values, coarse, fine_ref):
     z, y, x = coarse.size
-    tile = fine.tile
-    pairs = values.reshape(z, 2, tile, 128)
-    fine_ref[0:z] = pairs[:, 0] + pairs[:, 1]
-    rows = fine_ref[0:z, pl.ds(0, y, 2), :] + fine_ref[0:z, pl.ds(1, y, 2), :]
-    coarse_ref[0:z, 0:y, :] = rows
-    full = coarse_ref[0:z]
-    full = full + pltpu.roll(full, 127, 2)
-    full = lanes_2d(full, lambda lane: (2 * lane) & 127)
+    pairs = values.reshape(z, 2, values.shape[1], 128)
+    fine_ref[0:z, 0 : values.shape[1], :] = pairs[:, 0] + pairs[:, 1]
+    tile = coarse.tile
+    full = fine_ref[0:z, pl.ds(0, tile, 2), :] + fine_ref[0:z, pl.ds(1, tile, 2), :]
+    full = lanes_2d(full, lambda lane: (2 * lane) & 127) + lanes_2d(
+        full, lambda lane: (2 * lane + 1) & 127
+    )
     lane = lax.broadcasted_iota(jnp.int32, full.shape, 2)
     return jnp.where(lane < x, 0.125 * full, 0.0)
 
@@ -687,7 +705,7 @@
     wide = lanes_2d(values, lambda lane: lax.shift_right_logical(lane, 1))
     fine_ref[0:z, pl.ds(0, y, 2), :] = wide[:, 0:y]
     fine_ref[0:z, pl.ds(1, y, 2), :] = wide[:, 0:y]
-    rows = fine_ref[0:z]
+    rows = fine_ref[0:z, 0 : fine.tile, :]
     return jnp.broadcast_to(rows[:, None], (z, 2, fine.tile, 128)).reshape(fine.shape)
 
 
@@ -707,7 +725,6 @@
     joined, m0, h0, e0, k0, m1, h1, e1, k1, out = refs[:10]
     v0, w0, v1, w1, window, r2, m2, v2 = refs[10:18]
     fine_refs = refs[18:21]
-    coarse_refs = refs[21:24]
     tile = plan.tile
     gz, gy, gx = plan.counts
     iz, iy, ix = (lax.axis_index(axis) for axis in AXES)
@@ -729,8 +746,8 @@
                 m2[4 * z_block + z, rows, :] = value[4:8]
         return carry
 
-    lax.fori_loop(0, gz, unpack, 0)
-    for ref in (*fine_refs, *coarse_refs):
+    lax.fori_loop(0, gz, unpack, 0, unroll=4)
+    for ref in fine_refs:
         ref[...] = jnp.zeros(ref.shape, F32)
 
     levels = [Level(plan, level) for level in range(2, LEVELS + 1)]
@@ -741,7 +758,7 @@
         if i < len(levels) - 1:
             e = level.first + level.first * 0.2 + level.pull(level.first)
             kept.append(e)
-            args = (level, levels[i + 1], fine_refs[i], coarse_refs[i])
+            args = (levels[i + 1], fine_refs[i])
             mobility = coarsen(mobility, *args)
             source = coarsen(level.leftover(e), *args)
     level = levels[-1]
@@ -838,15 +855,18 @@
     def on_device(residual, mobility):
         assert residual.shape == (16, 16, 128)
         cells = jnp.stack([residual, mobility])
-        even, odd, *rows, x_odd = call(
+        even, odd, *sent = call(
             plan,
             lambda *refs: first_kernel(plan, *refs),
-            [(16 * (M_DEEP + R_DEEP), 128)] * 2 + [(2 * Y_ROWS, 128)] * near + [(4, 16, 128)],
+            [(16 * (M_DEEP + R_DEEP), 128)] * 2 + [(Y_ROWS, 128)] * near
+            + [(4, 16, 128)]
+            + [(DIAGONAL_ROWS, 128)] * near,
             [],
             cells,
         )
-        arrived = [swap(values, None, y, None) for y, values in enumerate(rows)]
-        x_arrived = [swap(x_odd, None, y, 1) for y in (None, *range(near))]
+        arrived = [swap(sent[y], None, y, None) for y in range(near)]
+        x_arrived = [swap(sent[near], None, None, 1)]
+        x_arrived += [swap(sent[1 + near + y], None, y, 1) for y in range(near)]
         z_own = [swap(odd, 1, None, None), swap(even, 0, None, None)][::-1]
         *beside, even, odd = call(
             plan,
@@ -911,8 +931,10 @@
             + [(tile, LW)]
             + [(z2, y2, 128)] * 2
             + [(z2 + 2 * HALO, y2 + margin, 128)]
-            + [level.shape for level in levels[:-1]]
-            + [level.shape for level in levels[1:]],
+            + [
+                (fine.size[0], max(fine.tile, 2 * coarse.tile), 128)
+                for fine, coarse in zip(levels[:-1], levels[1:])
+            ],
             joined,
             *state,
         )

time: 40.5 us -> 39.7 us (0.980)
  blocking collectives: 11.5 us -> 10.4 us
  starting transfers between devices: 10.5 us -> 11.2 us
    all_to_all x1, blocking collectives: 11.5 us -> 10.4 us  [on_device(): joined = lax.all_to_all(chunk, AXES, 0, 0, tiled=True)]
    ppermute x8, starting transfers between devices: 10.5 us -> 11.2 us  [swap(): return lax.ppermute(values, AXES, plan.pairs(swaps))]
  transfers between devices with their start and end apart: 8 -> 8, of which waited for: 2 -> 3; matrix products, arithmetic and copies ran while one was open for 0% -> 0% of each run, Pallas kernels for 11% -> 11%
where the time goes in v8:
time: 39.7 us; the launch traced here: 39.6 us
  Pallas kernels  13.4 us (34%)
  starting transfers between devices  11.2 us (28%)
  blocking collectives  10.4 us (26%)
  waiting for transfers between devices  3.52 us (9%)
  other arithmetic  0.99 us (2%)
    pallas_call x7, Pallas kernels, call(): pl.pallas_call(kernel, out_shape=[jax.ShapeDtypeStruct(shape, F32) for sh...  13.4 us
    ppermute x8, starting transfers between devices, swap(): return lax.ppermute(values, AXES, plan.pairs(swaps))  11.2 us
    all_to_all x1, blocking collectives, on_device(): joined = lax.all_to_all(chunk, AXES, 0, 0, tiled=True)  10.4 us
    ppermute x8, waiting for transfers between devices, swap(): return lax.ppermute(values, AXES, plan.pairs(swaps))  3.52 us
    another operation x1, other arithmetic, on_device(): cells = jnp.stack([residual, mobility])  0.99 us
  transfers between devices with their start and end apart: 8, of which 3 were waited for; matrix products, arithmetic and copies ran while one was open for 0% of the time, Pallas kernels for 11%

profile of v8, /device:TPU:0, one launch (start us, length us, event | category | flops | bytes accessed | tf_op | source)
XLA Modules:
  0.0 39.6 jit_solution(1010216146957776719)
XLA Ops:
  0.0 1.0 %pad_maximum_fusion.refs_0_ = f32[2,16,16,128]{3,2,1,0:T(8,128)S(1)} fusion(f32[1,16,16,128]{3,2,1,0:T(8,128)} %bitcast.2, f32[1,16,16,128]{3,2,1,0:T(8,128)} %bitcast.3), kind=kLoop, calls=%fused_computation | loop fusion | flops 65536 | bytes 524288 | tf_op jit(solution)/shard_map/stack | solution.py:857
  1.0 0.2 shard_map.28
  1.2 3.0 %collective-permute-start = (f32[336,128]{1,0:T(8,128)S(1)}, f32[336,128]{1,0:T(8,128)S(1)}, u32[]{:S(2)}, u32[]{:S(2)}) collective-permute-start(f32[336,128]{1,0:T(8,128)S(1)} %get-tuple-element.24), channel_id=1, source_target_pairs={{0,4},{1,5},{2,6},{3,7},{4,0},{5,1},{6,2},{7,3},{8,12},{9,13},{10,... | collective-permute-start | bytes 516104 | tf_op jit(solution)/shard_map/ppermute | solution.py:853
  4.2 0.0 collective-permute-start.4
  4.2 3.1 %collective-permute-start.5 = (f32[336,128]{1,0:T(8,128)S(1)}, f32[336,128]{1,0:T(8,128)S(1)}, u32[]{:S(2)}, u32[]{:S(2)}) collective-permute-start(f32[336,128]{1,0:T(8,128)S(1)} %get-tuple-element.31), channel_id=1, source_target_pairs={{0,8},{1,9},{2,10},{3,11},{4,12},{5,13},{6,14},{7,15},{8,0},{9,1},... | collective-permute-start | bytes 516104 | tf_op jit(solution)/shard_map/ppermute | solution.py:853
  7.4 0.1 collective-permute-start.1
  7.5 1.6 %collective-permute-start.2 = (f32[48,128]{1,0:T(8,128)S(1)}, f32[48,128]{1,0:T(8,128)S(1)}, u32[]{:S(2)}, u32[]{:S(2)}) collective-permute-start(f32[48,128]{1,0:T(8,128)S(1)} %get-tuple-element.26), channel_id=1, source_target_pairs={{0,7},{1,6},{2,5},{3,4},{4,3},{5,2},{6,1},{7,0},{8,15},{9,14},{10,... | collective-permute-start | bytes 73736 | tf_op jit(solution)/shard_map/ppermute | solution.py:853
  9.1 2.6 %collective-permute-done.2.refs_3_ = f32[48,128]{1,0:T(8,128)S(1)} collective-permute-done((f32[48,128]{1,0:T(8,128)S(1)}, f32[48,128]{1,0:T(8,128)S(1)}, u32[]{:S(2)}, u32[]{:S(2)}) %collective-permute-start.2) | collective-permute-done | bytes 24608 | tf_op jit(solution)/shard_map/ppermute | solution.py:853
  11.6 0.0 collective-permute-done.1.refs_2_
  11.6 0.0 collective-permute-done.refs_1_
  11.6 0.3 shard_map.29
  12.0 1.6 %collective-permute-start.3 = (f32[4,32,128]{2,1,0:T(8,128)S(1)}, f32[4,32,128]{2,1,0:T(8,128)S(1)}, u32[]{:S(2)}, u32[]{:S(2)}) collective-permute-start(f32[4,32,128]{2,1,0:T(8,128)S(1)} %get-tuple-element.29), channel_id=1, source_target_pairs={{0,1},{1,0},{2,3},{3,2},{4,5},{5,4},{6,7},{7,6},{8,9},{9,8},{10,11... | collective-permute-start | bytes 196616 | tf_op jit(solution)/shard_map/ppermute | solution.py:853
  13.5 0.0 collective-permute-done.4.refs_4_.refs_1_
  13.5 0.0 collective-permute-done.5.refs_3_.refs_2_
  13.6 0.9 %collective-permute-done.3.refs_3_.refs_2_ = f32[4,32,128]{2,1,0:T(8,128)S(1)} collective-permute-done((f32[4,32,128]{2,1,0:T(8,128)S(1)}, f32[4,32,128]{2,1,0:T(8,128)S(1)}, u32[]{:S(2)}, u32[]{:S(2)}) %collective-permute-start.3) | collective-permute-done | bytes 65568 | tf_op jit(solution)/shard_map/ppermute | solution.py:853
  14.4 0.2 shard_map.31
  14.6 0.4 %collective-permute-start.6 = (f32[248,128]{1,0:T(8,128)S(1)}, f32[248,128]{1,0:T(8,128)S(1)}, u32[]{:S(2)}, u32[]{:S(2)}) collective-permute-start(f32[248,128]{1,0:T(8,128)S(1)} %get-tuple-element.32), channel_id=1, source_target_pairs={{0,1},{1,0},{2,3},{3,2},{4,5},{5,4},{6,7},{7,6},{8,16},{9,17},{10,... | collective-permute-start | bytes 380936 | tf_op jit(solution)/shard_map/ppermute | solution.py:853
  15.0 1.3 %collective-permute-start.7 = (f32[248,128]{1,0:T(8,128)S(1)}, f32[248,128]{1,0:T(8,128)S(1)}, u32[]{:S(2)}, u32[]{:S(2)}) collective-permute-start(f32[248,128]{1,0:T(8,128)S(1)} %get-tuple-element.33), channel_id=1, source_target_pairs={{0,8},{1,9},{2,10},{3,11},{4,12},{5,13},{6,14},{7,15},{8,0},{9,1},... | collective-permute-start | bytes 380936 | tf_op jit(solution)/shard_map/ppermute | solution.py:853
  16.3 3.2 %shard_map.30.refs_0_ = f32[2,4,4,4,8,384]{5,4,3,2,1,0:T(8,128)S(1)} custom-call(f32[2,16,16,128]{3,2,1,0:T(8,128)S(1)} %pad_maximum_fusion.refs_0_, f32[2,16,16,128]{3,2,1,0:T(8,128)S(1)} %get-tuple-element.27.refs_1_.refs_0_, f32[4,32,128]{2,1,0:T(8,128)S(1)} %get-tuple-element.28.refs_2_.refs_1_, f32[4,32,128]{2,1,0:T(8,128)S(1)} %collective-permute-done.3.refs_3_.refs_2_), custom_call_target="tpu_custom_call" | custom-call | tf_op jit(solution)/shard_map/pallas_call | solution.py:833
  19.5 0.0 collective-permute-done.6.refs_2_
  19.5 0.9 %shard_map.32.refs_1_ = f32[2,4,4,4,8,128]{5,4,3,2,1,0:T(8,128)S(1)} custom-call(f32[2,4,4,4,8,384]{5,4,3,2,1,0:T(8,128)S(1)} %shard_map.30.refs_0_, f32[336,128]{1,0:T(8,128)S(1)} %collective-permute-done.4.refs_4_.refs_1_, f32[248,128]{1,0:T(8,128)S(1)} %collective-permute-done.6.refs_2_), custom_call_target="tpu_custom_call" | custom-call | tf_op jit(solution)/shard_map/pallas_call | solution.py:833
  20.4 0.1 collective-permute-done.7.refs_3_
  20.5 3.3 %shard_map.33 = (f32[32,8,128]{2,1,0:T(8,128)S(1)}, f32[6,6,6,8,384]{4,3,2,1,0:T(8,128)S(1)}, f32[4,4,4,8,384]{4,3,2,1,0:T(8,128)S(1)}, f32[4,4,4,8,384]{4,3,2,1...) custom-call(f32[2,4,4,4,8,384]{5,4,3,2,1,0:T(8,128)S(1)} %shard_map., ...), custom_call_target="tpu_custom_call" | custom-call | tf_op jit(solution)/shard_map/pallas_call | solution.py:833
  23.8 10.4 %all_to_all.5.refs_0_ = f32[32,8,128]{2,1,0:T(8,128)S(1)} all-to-all(f32[32,8,128]{2,1,0:T(8,128)S(1)} %get-tuple-element.34), channel_id=1, replica_groups=mesh['grp'=4,'gy'=2,'gx'=4] {'grp','gy','gx'}, dimensions={0} | all-to-all | bytes 262144 | tf_op jit(solution)/shard_map/all_to_all | solution.py:922
  34.3 5.3 %shard_map.34 = f32[16,16,128]{2,1,0:T(8,128)} custom-call(f32[32,8,128]{2,1,0:T(8,128)S(1)} %all_to_all.5.refs_0_, f32[6,6,6,8,384]{4,3,2,1,0:T(8,128)S(1)} %get-tuple-element.35.refs_1_, f32[4,4,4,8,384]{4,3,2,1,0:T(8,128)S(1)} %get-tuple-element.36.refs_2_, f32[4,4,4,8,384]{4,3,2,1,0:T(8,128)S(1)} %get-tuple-element.37.refs_3_, ...), custom_call_target="tpu_custom_call" | custom-call | tf_op jit(solution)/shard_map/pallas_call | solution.py:833
Async XLA Ops:
  1.2 10.4 %collective-permute-start = (f32[336,128]{1,0:T(8,128)S(1)}, f32[336,128]{1,0:T(8,128)S(1)}, u32[]{:S(2)}, u32[]{:S(2)}) collective-permute-start(f32[336,128]{1,0:T(8,128)S(1)} %get-tuple-element.24), channel_id=1, source_target_pairs={{0,4},{1,5},{2,6},{3,7},{4,0},{5,1},{6,2},{7,3},{8,12},{9,13},{10,... | collective-permute-start | bytes 516104 | tf_op jit(solution)/shard_map/ppermute | solution.py:853
  4.2 9.3 %collective-permute-start.4 = (f32[336,128]{1,0:T(8,128)S(1)}, f32[336,128]{1,0:T(8,128)S(1)}, u32[]{:S(2)}, u32[]{:S(2)}) collective-permute-start(f32[336,128]{1,0:T(8,128)S(1)} %get-tuple-element.30), channel_id=1, source_target_pairs={{0,1},{1,0},{2,3},{3,2},{4,5},{5,4},{6,7},{7,6},{8,16},{9,17},{10,... | collective-permute-start | bytes 516104 | tf_op jit(solution)/shard_map/ppermute | solution.py:853
  4.2 9.3 %collective-permute-start.5 = (f32[336,128]{1,0:T(8,128)S(1)}, f32[336,128]{1,0:T(8,128)S(1)}, u32[]{:S(2)}, u32[]{:S(2)}) collective-permute-start(f32[336,128]{1,0:T(8,128)S(1)} %get-tuple-element.31), channel_id=1, source_target_pairs={{0,8},{1,9},{2,10},{3,11},{4,12},{5,13},{6,14},{7,15},{8,0},{9,1},... | collective-permute-start | bytes 516104 | tf_op jit(solution)/shard_map/ppermute | solution.py:853
  7.4 4.2 %collective-permute-start.1 = (f32[4,16,128]{2,1,0:T(8,128)S(1)}, f32[4,16,128]{2,1,0:T(8,128)S(1)}, u32[]{:S(2)}, u32[]{:S(2)}) collective-permute-start(f32[4,16,128]{2,1,0:T(8,128)S(1)} %get-tuple-element.25), channel_id=1, source_target_pairs={{0,3},{1,2},{2,1},{3,0},{4,7},{5,6},{6,5},{7,4},{8,11},{9,10},{10,... | collective-permute-start | bytes 98312 | tf_op jit(solution)/shard_map/ppermute | solution.py:853
  7.5 4.2 %collective-permute-start.2 = (f32[48,128]{1,0:T(8,128)S(1)}, f32[48,128]{1,0:T(8,128)S(1)}, u32[]{:S(2)}, u32[]{:S(2)}) collective-permute-start(f32[48,128]{1,0:T(8,128)S(1)} %get-tuple-element.26), channel_id=1, source_target_pairs={{0,7},{1,6},{2,5},{3,4},{4,3},{5,2},{6,1},{7,0},{8,15},{9,14},{10,... | collective-permute-start | bytes 73736 | tf_op jit(solution)/shard_map/ppermute | solution.py:853
  12.0 2.5 %collective-permute-start.3 = (f32[4,32,128]{2,1,0:T(8,128)S(1)}, f32[4,32,128]{2,1,0:T(8,128)S(1)}, u32[]{:S(2)}, u32[]{:S(2)}) collective-permute-start(f32[4,32,128]{2,1,0:T(8,128)S(1)} %get-tuple-element.29), channel_id=1, source_target_pairs={{0,1},{1,0},{2,3},{3,2},{4,5},{5,4},{6,7},{7,6},{8,9},{9,8},{10,11... | collective-permute-start | bytes 196616 | tf_op jit(solution)/shard_map/ppermute | solution.py:853
  14.6 4.9 %collective-permute-start.6 = (f32[248,128]{1,0:T(8,128)S(1)}, f32[248,128]{1,0:T(8,128)S(1)}, u32[]{:S(2)}, u32[]{:S(2)}) collective-permute-start(f32[248,128]{1,0:T(8,128)S(1)} %get-tuple-element.32), channel_id=1, source_target_pairs={{0,1},{1,0},{2,3},{3,2},{4,5},{5,4},{6,7},{7,6},{8,16},{9,17},{10,... | collective-permute-start | bytes 380936 | tf_op jit(solution)/shard_map/ppermute | solution.py:853
  15.0 5.5 %collective-permute-start.7 = (f32[248,128]{1,0:T(8,128)S(1)}, f32[248,128]{1,0:T(8,128)S(1)}, u32[]{:S(2)}, u32[]{:S(2)}) collective-permute-start(f32[248,128]{1,0:T(8,128)S(1)} %get-tuple-element.33), channel_id=1, source_target_pairs={{0,8},{1,9},{2,10},{3,11},{4,12},{5,13},{6,14},{7,15},{8,0},{9,1},... | collective-permute-start | bytes 380936 | tf_op jit(solution)/shard_map/ppermute | solution.py:853

commit v9 on v8

--- a/solution.py
+++ b/solution.py
@@ -15,6 +15,7 @@
 ZW = 4 + 2 * HALO
 XW = 32 + 2 * HALO
 LW = 384
+NARROW = 256
 EDGE = 4 * HALO
 M_DEEP, M_FAR, R_DEEP, R_FAR = 11, 4, 10, 3
 
@@ -33,6 +34,10 @@
 DIAGONAL_ROWS = 48
 
 
+def lane_of(z):
+    return ((z - 2) * XW) % LW
+
+
 def lane_iota(rows=8):
     return lax.broadcasted_iota(jnp.int32, (rows, 128), 1)
 
@@ -63,6 +68,7 @@
 
 def window_cells(t, rows):
     cell = lane_iota(rows) + 128 * t
+    cell = jnp.where(cell >= lane_of(0), cell - lane_of(0), cell + 2 * XW)
     z = jnp.zeros((rows, 128), jnp.int32)
     for k in range(1, ZW + 1):
         z = z + (cell >= k * XW).astype(jnp.int32)
@@ -92,7 +98,7 @@
 
 
 def halo_start(side):
-    return 0 if side == 0 else (HALO + 4) * XW - 256
+    return lane_of(0 if side == 0 else HALO + 4) % 128
 
 
 def halo_cells(side, px, rows):
@@ -347,9 +353,9 @@
     sides[1] = jnp.where(x_even, even, odd)
 
     inside = inside_mask(plan)
-    offsets = [(z + HALO) * XW + HALO for z in range(4)]
+    offsets = [lane_of(z + HALO) + HALO for z in range(4)]
     index = [[every_lane(offset, px, tile) for px in range(4)] for offset in offsets]
-    from_edge = {(s, t): edge_own_lanes(s, t, tile) for s, t in ((0, 0), (0, 1), (1, 1), (1, 2))}
+    from_edge = {(s, t): edge_own_lanes(s, t, tile) for s in range(2) for t in range(2)}
 
     def body(pz, carry):
         for a in range(2):
@@ -358,7 +364,7 @@
                 side = [every_fourth(plan, sides, (s, pz), py) for s in range(2)]
                 for px in range(4):
                     parts = [gather(cells[z], index[z][px]) for z in range(4)]
-                    for t in range(3):
+                    for t in range(2):
                         value = jnp.zeros((tile, 128), F32)
                         for z in range(4):
                             offset = offsets[z] - 128 * t
@@ -397,7 +403,7 @@
 
 
 def roll_lanes(value, shift):
-    return pltpu.roll(value, shift % LW, 1)
+    return pltpu.roll(value, shift % value.shape[1], 1)
 
 
 def fill_rim(plan, ref, n):
@@ -418,41 +424,51 @@
             ref[i, j, n + 1] = roll_lanes(x_high, -1)
 
 
-def around(ref, a, b, c):
+def around(ref, a, b, c, width=LW):
+    lanes = slice(0, width)
     return (
-        ref[a, b + 1, c + 1],
-        ref[a + 2, b + 1, c + 1],
-        ref[a + 1, b, c + 1],
-        ref[a + 1, b + 2, c + 1],
-        ref[a + 1, b + 1, c],
-        ref[a + 1, b + 1, c + 2],
+        ref[a, b + 1, c + 1, :, lanes],
+        ref[a + 2, b + 1, c + 1, :, lanes],
+        ref[a + 1, b, c + 1, :, lanes],
+        ref[a + 1, b + 2, c + 1, :, lanes],
+        ref[a + 1, b + 1, c, :, lanes],
+        ref[a + 1, b + 1, c + 2, :, lanes],
     )
 
 
-def around_rimless(plan, ref, n, a, b, c):
+def around_rimless(plan, ref, n, a, b, c, width):
     tile = plan.tile
-    row = lax.broadcasted_iota(jnp.int32, (tile, LW), 0)
+    row = lax.broadcasted_iota(jnp.int32, (tile, width), 0)
+
+    def cells(i, j, k):
+        return ref[i, j, k, :, 0:width]
+
+    def first_row(value):
+        return jnp.where(row == 0, 0.0, pltpu.roll(value, 1, 0))
+
+    def last_row(value):
+        return jnp.where(row == tile - 1, 0.0, pltpu.roll(value, tile - 1, 0))
+
     return (
-        ref[a - 1, b, c] if a > 0 else roll_lanes(ref[n - 1, b, c], XW),
-        ref[a + 1, b, c] if a < n - 1 else roll_lanes(ref[0, b, c], -XW),
-        ref[a, b - 1, c] if b > 0 else jnp.where(row == 0, 0.0, pltpu.roll(ref[a, n - 1, c], 1, 0)),
-        ref[a, b + 1, c]
-        if b < n - 1
-        else jnp.where(row == tile - 1, 0.0, pltpu.roll(ref[a, 0, c], tile - 1, 0)),
-        ref[a, b, c - 1] if c > 0 else roll_lanes(ref[a, b, n - 1], 1),
-        ref[a, b, c + 1] if c < n - 1 else roll_lanes(ref[a, b, 0], -1),
+        cells(a - 1, b, c) if a > 0 else roll_lanes(cells(n - 1, b, c), XW),
+        cells(a + 1, b, c) if a < n - 1 else roll_lanes(cells(0, b, c), -XW),
+        cells(a, b - 1, c) if b > 0 else first_row(cells(a, n - 1, c)),
+        cells(a, b + 1, c) if b < n - 1 else last_row(cells(a, 0, c)),
+        cells(a, b, c - 1) if c > 0 else roll_lanes(cells(a, b, n - 1), 1),
+        cells(a, b, c + 1) if c < n - 1 else roll_lanes(cells(a, b, 0), -1),
     )
 
 
-def pull(plan, n, m_ref, v_ref, h_ref, a, b, c):
-    cells = around_rimless(plan, v_ref, n, a, b, c)
-    mobility = around(m_ref, a, b, c)
+def pull(plan, n, m_ref, v_ref, h_ref, a, b, c, width=LW):
+    cells = around_rimless(plan, v_ref, n, a, b, c, width)
+    mobility = around(m_ref, a, b, c, width)
     total = ((cells[0] + cells[1]) + (cells[2] + cells[3])) + (cells[4] + cells[5])
     products = [m * v for m, v in zip(mobility, cells)]
     other = ((products[0] + products[1]) + (products[2] + products[3])) + (
         products[4] + products[5]
     )
-    return h_ref[a, b, c] * (m_ref[a + 1, b + 1, c + 1] * total + other)
+    centre = m_ref[a + 1, b + 1, c + 1, :, 0:width]
+    return h_ref[a, b, c, :, 0:width] * (centre * total + other)
 
 
 def descend(plan, n, factor, inside, m_ref, r_ref, d_ref, h_ref, e_ref, k_ref):
@@ -475,7 +491,7 @@
     return r_ref[a, b, c] - factor * (d_ref[a, b, c] * away)
 
 
-def place_halo(plan, swap, own_ref, z_own_ref, z_ref, planes, sides, emit):
+def place_halo(plan, swap, z_own_ref, z_ref, planes, sides, emit):
     near, tile = plan.near, plan.tile
     own_row, places = plan.y_places()
     upper = is_even("grp")
@@ -519,14 +535,6 @@
     turns = [choose(lambda side: halo_turn(side, px, tile)) for px in range(4)]
     edge_index = [choose(lambda side: edge_far_lanes(side, a, tile)) for a in range(2)]
 
-    def kept(side):
-        z, _ = window_cells(2 * side, tile)
-        z = (z < HALO) if side == 0 else (z >= HALO + 4)
-        return (z & inside_tile(plan, 2 * side)).astype(jnp.int32)
-
-    keep = choose(kept) > 0
-    lanes = pl.ds(pl.multiple_of(jnp.where(upper, 256, 0), 128), 128)
-
     def place(pz, carry):
         for a in range(2):
             for py in range(4):
@@ -542,18 +550,17 @@
                     value = jnp.where(turn == 3, edge, value)
                     if px > 0:
                         value = pltpu.roll(value, 128 - 32 * px, 1)
-                    value = jnp.where(keep, value, own_ref[a, pz, py, px, :, lanes])
-                    emit(a, pz, py, px, lanes, value)
+                    emit(a, pz, py, px, value)
         return carry
 
     lax.fori_loop(0, 4, place, 0)
 
 
-def place_kernel(plan, own_ref, z_own_ref, z_ref, out, planes, sides):
-    def emit(a, pz, py, px, lanes, value):
+def place_kernel(plan, z_own_ref, z_ref, out, planes, sides):
+    def emit(a, pz, py, px, value):
         out[a, pz, py, px] = value
 
-    place_halo(plan, 1, own_ref, z_own_ref, z_ref, planes, sides, emit)
+    place_halo(plan, 1, z_own_ref, z_ref, planes, sides, emit)
 
 
 def down_kernel(plan, *refs):
@@ -562,20 +569,29 @@
     r0, d0, r1, d1, planes, sides = refs[13:]
     tile = plan.tile
     inside = inside_mask(plan)
-    rest = pl.ds(pl.multiple_of(jnp.where(is_even("grp"), 0, 256), 128), 128)
-
-    def emit(a, pz, py, px, lanes, value):
-        for lanes_i, value_i in (
-            (lanes, value),
-            (rest, other_ref[a, pz, py, px]),
-            (slice(128, 256), own_ref[a, pz, py, px, :, 128:256]),
-        ):
+    z_even = is_even("grp")
+    z = [window_cells(t, tile)[0] for t in range(3)]
+    here = [inside_tile(plan, t) for t in range(3)]
+    lower_0, upper_1 = (z[0] < HALO) & here[0], (z[1] >= HALO + 4) & here[1]
+    lower_2, upper_2 = (z[2] < HALO) & here[2], (z[2] >= HALO + 4) & here[2]
+
+    def emit(a, pz, py, px, value):
+        other = other_ref[a, pz, py, px]
+        lower = jnp.where(z_even, other, value)
+        upper = jnp.where(z_even, value, other)
+        tiles = (
+            jnp.where(lower_0, lower, own_ref[a, pz, py, px, :, 0:128]),
+            jnp.where(upper_1, upper, own_ref[a, pz, py, px, :, 128:256]),
+            jnp.where(lower_2, lower, jnp.where(upper_2, upper, 0.0)),
+        )
+        for t, cells in enumerate(tiles):
+            lanes = slice(128 * t, 128 * t + 128)
             if a == 1:
-                m0[pz + 1, py + 1, px + 1, :, lanes_i] = value_i
+                m0[pz + 1, py + 1, px + 1, :, lanes] = cells
             else:
-                r0[pz, py, px, :, lanes_i] = value_i
-
-    place_halo(plan, 0, own_ref, z_own_ref, z_ref, planes, sides, emit)
+                r0[pz, py, px, :, lanes] = cells
+
+    place_halo(plan, 0, z_own_ref, z_ref, planes, sides, emit)
 
     descend(plan, 4, 1.0, inside, m0, r0, d0, h0, e0, k0)
     for a, b, c in np.ndindex(2, 2, 2):
@@ -599,7 +615,7 @@
         for t in range(3):
             part = 0.125 * total[:, 128 * t : 128 * t + 128]
             for z in range(4):
-                offset = (z + HALO) * XW + HALO - 128 * t
+                offset = lane_of(z + HALO) + HALO - 128 * t
                 low, high = max(offset, 0), min(offset + 32, 128)
                 if low < high:
                     move = 32 * z - offset
@@ -709,15 +725,16 @@
     return jnp.broadcast_to(rows[:, None], (z, 2, fine.tile, 128)).reshape(fine.shape)
 
 
-def ascend(plan, n, m_ref, h_ref, e_ref, k_ref, below, v_ref, w_ref):
+def ascend(plan, n, width, m_ref, h_ref, e_ref, k_ref, below, v_ref, w_ref):
+    lanes = slice(0, width)
     for a, b, c in np.ndindex(n, n, n):
-        v_ref[a, b, c] = k_ref[a, b, c] + below(a, b, c)
+        v_ref[a, b, c] = k_ref[a, b, c, :, lanes] + below(a, b, c)
     for old, new in ((v_ref, w_ref), (w_ref, v_ref)):
         for a, b, c in np.ndindex(n, n, n):
             new[a, b, c] = (
                 0.2 * old[a, b, c]
-                + e_ref[a, b, c]
-                + pull(plan, n, m_ref, old, h_ref, a, b, c)
+                + e_ref[a, b, c, :, lanes]
+                + pull(plan, n, m_ref, old, h_ref, a, b, c, width)
             )
 
 
@@ -781,7 +798,7 @@
     for t in range(3):
         value = jnp.zeros((tile, 128), F32)
         for z in range(ZW):
-            offset = z * XW - 128 * t
+            offset = lane_of(z) - 128 * t
             low, high = max(offset, 0), min(offset + XW, 128)
             if low < high:
                 shift = lax.rem(offset % 128 + HALO - 32 * ix + 256, 128)
@@ -793,19 +810,23 @@
 
     below = window[...]
 
-    ascend(plan, 2, m1, h1, e1, k1, lambda a, b, c: below, v1, w1)
-    ascend(plan, 4, m0, h0, e0, k0, lambda a, b, c: v1[a // 2, b // 2, c // 2], v0, w0)
+    ascend(plan, 2, LW, m1, h1, e1, k1, lambda a, b, c: below, v1, w1)
+
+    def from_half(a, b, c):
+        return v1[a // 2, b // 2, c // 2, :, 0:NARROW]
+
+    ascend(plan, 4, NARROW, m0, h0, e0, k0, from_half, v0, w0)
 
     lane = lane_iota(tile)
     natural = 32 * (lane & 3) + lax.shift_right_logical(lane, 2)
-    starts = [(z + HALO) * XW + HALO for z in range(4)]
+    starts = [lane_of(z + HALO) + HALO for z in range(4)]
     places_of = [(lane - start) & 127 for start in starts]
     index = [(natural + start) & 127 for start in starts]
 
     def store(pz, carry):
         for py in range(4):
             parts = [
-                [v0[pz, py, px, :, 128 * t : 128 * t + 128] for t in range(3)]
+                [v0[pz, py, px, :, 128 * t : 128 * t + 128] for t in range(2)]
                 for px in range(4)
             ]
             parts = [
@@ -845,6 +866,7 @@
     near, tile = plan.near, plan.tile
     z2, y2, x2 = plan.coarse
     full = (4, 4, 4, tile, LW)
+    narrow = (4, 4, 4, tile, NARROW)
     half = (2, 2, 2, tile, LW)
     full_rim = (6, 6, 6, tile, LW)
     half_rim = (4, 4, 4, tile, LW)
@@ -891,7 +913,7 @@
         (own,) = call(
             plan,
             lambda *refs: own_kernel(plan, *refs),
-            [(2, *full)],
+            [(2, *narrow)],
             [(2, 16, plan.rows, 128), (2, 4, plan.rows, 128)],
             cells,
             *beside,
@@ -903,7 +925,6 @@
             lambda *refs: place_kernel(plan, *refs),
             [(2, 4, 4, 4, tile, 128)],
             halo_scratch,
-            own,
             z_own[1],
             arrived[1],
         )
@@ -926,7 +947,7 @@
             plan,
             lambda *refs: up_kernel(plan, *refs),
             [(16, 16, 128)],
-            [full] * 2
+            [narrow] * 2
             + [half] * 2
             + [(tile, LW)]
             + [(z2, y2, 128)] * 2

time: 39.7 us -> 38.9 us (0.980)
  Pallas kernels: 13.4 us -> 12.5 us
    pallas_call x7, Pallas kernels: 13.4 us -> 12.5 us  [call(): pl.pallas_call(kernel, out_shape=[jax.ShapeDtypeStruct(shape, F32) for sh...]
where the time goes in v9:
time: 38.9 us; the launch traced here: 38.7 us
  Pallas kernels  12.5 us (32%)
  starting transfers between devices  11.2 us (29%)
  blocking collectives  10.4 us (27%)
  waiting for transfers between devices  3.55 us (9%)
  other arithmetic  0.99 us (3%)
    pallas_call x7, Pallas kernels, call(): pl.pallas_call(kernel, out_shape=[jax.ShapeDtypeStruct(shape, F32) for sh...  12.5 us
    ppermute x8, starting transfers between devices, swap(): return lax.ppermute(values, AXES, plan.pairs(swaps))  11.2 us
    all_to_all x1, blocking collectives, on_device(): joined = lax.all_to_all(chunk, AXES, 0, 0, tiled=True)  10.4 us
    ppermute x8, waiting for transfers between devices, swap(): return lax.ppermute(values, AXES, plan.pairs(swaps))  3.55 us
    another operation x1, other arithmetic, on_device(): cells = jnp.stack([residual, mobility])  0.99 us
  transfers between devices with their start and end apart: 8, of which 3 were waited for; matrix products, arithmetic and copies ran while one was open for 0% of the time, Pallas kernels for 11%

profile of v9, /device:TPU:0, one launch (start us, length us, event | category | flops | bytes accessed | tf_op | source)
XLA Modules:
  0.0 38.7 jit_solution(2875035545991905419)
XLA Ops:
  0.0 1.0 %pad_maximum_fusion.refs_0_ = f32[2,16,16,128]{3,2,1,0:T(8,128)S(1)} fusion(f32[1,16,16,128]{3,2,1,0:T(8,128)} %bitcast.2, f32[1,16,16,128]{3,2,1,0:T(8,128)} %bitcast.3), kind=kLoop, calls=%fused_computation | loop fusion | flops 65536 | bytes 524288 | tf_op jit(solution)/shard_map/stack | solution.py:879
  1.0 0.2 shard_map.28
  1.2 3.0 %collective-permute-start = (f32[336,128]{1,0:T(8,128)S(1)}, f32[336,128]{1,0:T(8,128)S(1)}, u32[]{:S(2)}, u32[]{:S(2)}) collective-permute-start(f32[336,128]{1,0:T(8,128)S(1)} %get-tuple-element.24), channel_id=1, source_target_pairs={{0,4},{1,5},{2,6},{3,7},{4,0},{5,1},{6,2},{7,3},{8,12},{9,13},{10,... | collective-permute-start | bytes 516104 | tf_op jit(solution)/shard_map/ppermute | solution.py:875
  4.2 0.0 collective-permute-start.4
  4.2 3.1 %collective-permute-start.5 = (f32[336,128]{1,0:T(8,128)S(1)}, f32[336,128]{1,0:T(8,128)S(1)}, u32[]{:S(2)}, u32[]{:S(2)}) collective-permute-start(f32[336,128]{1,0:T(8,128)S(1)} %get-tuple-element.31), channel_id=1, source_target_pairs={{0,8},{1,9},{2,10},{3,11},{4,12},{5,13},{6,14},{7,15},{8,0},{9,1},... | collective-permute-start | bytes 516104 | tf_op jit(solution)/shard_map/ppermute | solution.py:875
  7.4 0.1 collective-permute-start.1
  7.5 1.6 %collective-permute-start.2 = (f32[48,128]{1,0:T(8,128)S(1)}, f32[48,128]{1,0:T(8,128)S(1)}, u32[]{:S(2)}, u32[]{:S(2)}) collective-permute-start(f32[48,128]{1,0:T(8,128)S(1)} %get-tuple-element.26), channel_id=1, source_target_pairs={{0,7},{1,6},{2,5},{3,4},{4,3},{5,2},{6,1},{7,0},{8,15},{9,14},{10,... | collective-permute-start | bytes 73736 | tf_op jit(solution)/shard_map/ppermute | solution.py:875
  9.1 2.6 %collective-permute-done.2.refs_3_ = f32[48,128]{1,0:T(8,128)S(1)} collective-permute-done((f32[48,128]{1,0:T(8,128)S(1)}, f32[48,128]{1,0:T(8,128)S(1)}, u32[]{:S(2)}, u32[]{:S(2)}) %collective-permute-start.2) | collective-permute-done | bytes 24608 | tf_op jit(solution)/shard_map/ppermute | solution.py:875
  11.6 0.0 collective-permute-done.1.refs_2_
  11.6 0.0 collective-permute-done.refs_1_
  11.6 0.3 shard_map.29
  12.0 1.6 %collective-permute-start.3 = (f32[4,32,128]{2,1,0:T(8,128)S(1)}, f32[4,32,128]{2,1,0:T(8,128)S(1)}, u32[]{:S(2)}, u32[]{:S(2)}) collective-permute-start(f32[4,32,128]{2,1,0:T(8,128)S(1)} %get-tuple-element.29), channel_id=1, source_target_pairs={{0,1},{1,0},{2,3},{3,2},{4,5},{5,4},{6,7},{7,6},{8,9},{9,8},{10,11... | collective-permute-start | bytes 196616 | tf_op jit(solution)/shard_map/ppermute | solution.py:875
  13.5 0.0 collective-permute-done.4.refs_4_.refs_0_
  13.5 0.0 collective-permute-done.5.refs_3_.refs_2_
  13.6 0.9 %collective-permute-done.3.refs_3_.refs_2_ = f32[4,32,128]{2,1,0:T(8,128)S(1)} collective-permute-done((f32[4,32,128]{2,1,0:T(8,128)S(1)}, f32[4,32,128]{2,1,0:T(8,128)S(1)}, u32[]{:S(2)}, u32[]{:S(2)}) %collective-permute-start.3) | collective-permute-done | bytes 65568 | tf_op jit(solution)/shard_map/ppermute | solution.py:875
  14.4 0.2 shard_map.31
  14.6 0.4 %collective-permute-start.6 = (f32[248,128]{1,0:T(8,128)S(1)}, f32[248,128]{1,0:T(8,128)S(1)}, u32[]{:S(2)}, u32[]{:S(2)}) collective-permute-start(f32[248,128]{1,0:T(8,128)S(1)} %get-tuple-element.32), channel_id=1, source_target_pairs={{0,1},{1,0},{2,3},{3,2},{4,5},{5,4},{6,7},{7,6},{8,16},{9,17},{10,... | collective-permute-start | bytes 380936 | tf_op jit(solution)/shard_map/ppermute | solution.py:875
  15.0 1.3 %collective-permute-start.7 = (f32[248,128]{1,0:T(8,128)S(1)}, f32[248,128]{1,0:T(8,128)S(1)}, u32[]{:S(2)}, u32[]{:S(2)}) collective-permute-start(f32[248,128]{1,0:T(8,128)S(1)} %get-tuple-element.33), channel_id=1, source_target_pairs={{0,8},{1,9},{2,10},{3,11},{4,12},{5,13},{6,14},{7,15},{8,0},{9,1},... | collective-permute-start | bytes 380936 | tf_op jit(solution)/shard_map/ppermute | solution.py:875
  16.3 3.2 %shard_map.30.refs_0_ = f32[2,4,4,4,8,256]{5,4,3,2,1,0:T(8,128)S(1)} custom-call(f32[2,16,16,128]{3,2,1,0:T(8,128)S(1)} %pad_maximum_fusion.refs_0_, f32[2,16,16,128]{3,2,1,0:T(8,128)S(1)} %get-tuple-element.27.refs_1_.refs_0_, f32[4,32,128]{2,1,0:T(8,128)S(1)} %get-tuple-element.28.refs_2_.refs_1_, f32[4,32,128]{2,1,0:T(8,128)S(1)} %collective-permute-done.3.refs_3_.refs_2_), custom_call_target="tpu_custom_call" | custom-call | tf_op jit(solution)/shard_map/pallas_call | solution.py:854
  19.5 0.0 collective-permute-done.6.refs_1_
  19.5 0.9 %shard_map.32.refs_1_ = f32[2,4,4,4,8,128]{5,4,3,2,1,0:T(8,128)S(1)} custom-call(f32[336,128]{1,0:T(8,128)S(1)} %collective-permute-done.4.refs_4_.refs_0_, f32[248,128]{1,0:T(8,128)S(1)} %collective-permute-done.6.refs_1_), custom_call_target="tpu_custom_call" | custom-call | tf_op jit(solution)/shard_map/pallas_call | solution.py:854
  20.4 0.1 collective-permute-done.7.refs_3_
  20.5 3.3 %shard_map.33 = (f32[32,8,128]{2,1,0:T(8,128)S(1)}, f32[6,6,6,8,384]{4,3,2,1,0:T(8,128)S(1)}, f32[4,4,4,8,384]{4,3,2,1,0:T(8,128)S(1)}, f32[4,4,4,8,384]{4,3,2,1...) custom-call(f32[2,4,4,4,8,256]{5,4,3,2,1,0:T(8,128)S(1)} %shard_map., ...), custom_call_target="tpu_custom_call" | custom-call | tf_op jit(solution)/shard_map/pallas_call | solution.py:854
  23.8 10.4 %all_to_all.5.refs_0_ = f32[32,8,128]{2,1,0:T(8,128)S(1)} all-to-all(f32[32,8,128]{2,1,0:T(8,128)S(1)} %get-tuple-element.34), channel_id=1, replica_groups=mesh['grp'=4,'gy'=2,'gx'=4] {'grp','gy','gx'}, dimensions={0} | all-to-all | bytes 262144 | tf_op jit(solution)/shard_map/all_to_all | solution.py:943
  34.2 4.5 %shard_map.34 = f32[16,16,128]{2,1,0:T(8,128)} custom-call(f32[32,8,128]{2,1,0:T(8,128)S(1)} %all_to_all.5.refs_0_, f32[6,6,6,8,384]{4,3,2,1,0:T(8,128)S(1)} %get-tuple-element.35.refs_1_, f32[4,4,4,8,384]{4,3,2,1,0:T(8,128)S(1)} %get-tuple-element.36.refs_2_, f32[4,4,4,8,384]{4,3,2,1,0:T(8,128)S(1)} %get-tuple-element.37.refs_3_, ...), custom_call_target="tpu_custom_call" | custom-call | tf_op jit(solution)/shard_map/pallas_call | solution.py:854
Async XLA Ops:
  1.2 10.4 %collective-permute-start = (f32[336,128]{1,0:T(8,128)S(1)}, f32[336,128]{1,0:T(8,128)S(1)}, u32[]{:S(2)}, u32[]{:S(2)}) collective-permute-start(f32[336,128]{1,0:T(8,128)S(1)} %get-tuple-element.24), channel_id=1, source_target_pairs={{0,4},{1,5},{2,6},{3,7},{4,0},{5,1},{6,2},{7,3},{8,12},{9,13},{10,... | collective-permute-start | bytes 516104 | tf_op jit(solution)/shard_map/ppermute | solution.py:875
  4.2 9.3 %collective-permute-start.4 = (f32[336,128]{1,0:T(8,128)S(1)}, f32[336,128]{1,0:T(8,128)S(1)}, u32[]{:S(2)}, u32[]{:S(2)}) collective-permute-start(f32[336,128]{1,0:T(8,128)S(1)} %get-tuple-element.30), channel_id=1, source_target_pairs={{0,1},{1,0},{2,3},{3,2},{4,5},{5,4},{6,7},{7,6},{8,16},{9,17},{10,... | collective-permute-start | bytes 516104 | tf_op jit(solution)/shard_map/ppermute | solution.py:875
  4.2 9.3 %collective-permute-start.5 = (f32[336,128]{1,0:T(8,128)S(1)}, f32[336,128]{1,0:T(8,128)S(1)}, u32[]{:S(2)}, u32[]{:S(2)}) collective-permute-start(f32[336,128]{1,0:T(8,128)S(1)} %get-tuple-element.31), channel_id=1, source_target_pairs={{0,8},{1,9},{2,10},{3,11},{4,12},{5,13},{6,14},{7,15},{8,0},{9,1},... | collective-permute-start | bytes 516104 | tf_op jit(solution)/shard_map/ppermute | solution.py:875
  7.4 4.2 %collective-permute-start.1 = (f32[4,16,128]{2,1,0:T(8,128)S(1)}, f32[4,16,128]{2,1,0:T(8,128)S(1)}, u32[]{:S(2)}, u32[]{:S(2)}) collective-permute-start(f32[4,16,128]{2,1,0:T(8,128)S(1)} %get-tuple-element.25), channel_id=1, source_target_pairs={{0,3},{1,2},{2,1},{3,0},{4,7},{5,6},{6,5},{7,4},{8,11},{9,10},{10,... | collective-permute-start | bytes 98312 | tf_op jit(solution)/shard_map/ppermute | solution.py:875
  7.5 4.2 %collective-permute-start.2 = (f32[48,128]{1,0:T(8,128)S(1)}, f32[48,128]{1,0:T(8,128)S(1)}, u32[]{:S(2)}, u32[]{:S(2)}) collective-permute-start(f32[48,128]{1,0:T(8,128)S(1)} %get-tuple-element.26), channel_id=1, source_target_pairs={{0,7},{1,6},{2,5},{3,4},{4,3},{5,2},{6,1},{7,0},{8,15},{9,14},{10,... | collective-permute-start | bytes 73736 | tf_op jit(solution)/shard_map/ppermute | solution.py:875
  12.0 2.5 %collective-permute-start.3 = (f32[4,32,128]{2,1,0:T(8,128)S(1)}, f32[4,32,128]{2,1,0:T(8,128)S(1)}, u32[]{:S(2)}, u32[]{:S(2)}) collective-permute-start(f32[4,32,128]{2,1,0:T(8,128)S(1)} %get-tuple-element.29), channel_id=1, source_target_pairs={{0,1},{1,0},{2,3},{3,2},{4,5},{5,4},{6,7},{7,6},{8,9},{9,8},{10,11... | collective-permute-start | bytes 196616 | tf_op jit(solution)/shard_map/ppermute | solution.py:875
  14.6 4.9 %collective-permute-start.6 = (f32[248,128]{1,0:T(8,128)S(1)}, f32[248,128]{1,0:T(8,128)S(1)}, u32[]{:S(2)}, u32[]{:S(2)}) collective-permute-start(f32[248,128]{1,0:T(8,128)S(1)} %get-tuple-element.32), channel_id=1, source_target_pairs={{0,1},{1,0},{2,3},{3,2},{4,5},{5,4},{6,7},{7,6},{8,16},{9,17},{10,... | collective-permute-start | bytes 380936 | tf_op jit(solution)/shard_map/ppermute | solution.py:875
  15.0 5.5 %collective-permute-start.7 = (f32[248,128]{1,0:T(8,128)S(1)}, f32[248,128]{1,0:T(8,128)S(1)}, u32[]{:S(2)}, u32[]{:S(2)}) collective-permute-start(f32[248,128]{1,0:T(8,128)S(1)} %get-tuple-element.33), channel_id=1, source_target_pairs={{0,8},{1,9},{2,10},{3,11},{4,12},{5,13},{6,14},{7,15},{8,0},{9,1},... | collective-permute-start | bytes 380936 | tf_op jit(solution)/shard_map/ppermute | solution.py:875

commit v10 on v9

--- a/solution.py
+++ b/solution.py
@@ -185,10 +185,8 @@
         for z in range(4):
             cells = block[a, 4 * z + pz, 8 * half : 8 * half + 8, :]
             base = a * 48 + z * 12
-            moved = jnp.where(
-                to_right, pltpu.roll(cells, (base - (128 - EDGE)) % 128, 1), pltpu.roll(cells, base, 1)
-            )
-            out = jnp.where(between(base, base + EDGE), moved, out)
+            shift = jnp.where(to_right, (base - (128 - EDGE)) % 128, base)
+            out = jnp.where(between(base, base + EDGE), pltpu.roll(cells, shift, 1), out)
     return out
 
 
@@ -244,10 +242,10 @@
                 rows = ref[near_row + 8 * plane : near_row + 8 * plane + 8, :]
                 more = ref[far + deep * plane : far + deep * (plane + 1), :]
                 none = jnp.zeros((8 - deep, 128), F32)
-                after = jnp.concatenate([more, none], axis=0)
-                before = jnp.concatenate([none, more], axis=0)
-                out[a, plane, 0:8, :] = jnp.where(following, rows, before)
-                out[a, plane, 8:16, :] = jnp.where(following, after, rows)
+                more = jnp.concatenate([more, none], axis=0)
+                more = pltpu.roll(more, jnp.where(following, 0, 8 - deep), 0)
+                out[a, plane, at(8 * (1 - side), 8), :] = rows
+                out[a, plane, at(8 * side, 8), :] = more
     for i, block in enumerate((cells_ref, *beside)):
         start = own_row if i == 0 else places[i - 1][1]
         if i == 0:
@@ -686,7 +684,11 @@
         self.source = source
 
     def pull(self, v):
-        t = [w * near for w, near in zip(self.weights, self.shifts(v))]
+        shifts = list(self.shifts(v))
+        if self.size[1] == 1:
+            t = [self.weights[i] * shifts[i] for i in (0, 1, 4, 5)]
+            return (t[0] + t[1]) + (t[2] + t[3])
+        t = [w * near for w, near in zip(self.weights, shifts)]
         return ((t[0] + t[1]) + (t[2] + t[3])) + (t[4] + t[5])
 
     def relax(self, v):

time: 38.9 us -> 38.8 us (level)
  no operation moved by 1% of the time
where the time goes in v10:
time: 38.8 us; the launch traced here: 38.6 us
  Pallas kernels  12.4 us (32%)
  starting transfers between devices  11.2 us (29%)
  blocking collectives  10.4 us (27%)
  waiting for transfers between devices  3.54 us (9%)
  other arithmetic  0.99 us (3%)
    pallas_call x7, Pallas kernels, call(): pl.pallas_call(kernel, out_shape=[jax.ShapeDtypeStruct(shape, F32) for sh...  12.4 us
    ppermute x8, starting transfers between devices, swap(): return lax.ppermute(values, AXES, plan.pairs(swaps))  11.2 us
    all_to_all x1, blocking collectives, on_device(): joined = lax.all_to_all(chunk, AXES, 0, 0, tiled=True)  10.4 us
    ppermute x8, waiting for transfers between devices, swap(): return lax.ppermute(values, AXES, plan.pairs(swaps))  3.54 us
    another operation x1, other arithmetic, on_device(): cells = jnp.stack([residual, mobility])  0.99 us
  transfers between devices with their start and end apart: 8, of which 3 were waited for; matrix products, arithmetic and copies ran while one was open for 0% of the time, Pallas kernels for 11%

profile of v10, /device:TPU:0, one launch (start us, length us, event | category | flops | bytes accessed | tf_op | source)
XLA Modules:
  0.0 38.6 jit_solution(4866089632444739660)
XLA Ops:
  0.0 1.0 %pad_maximum_fusion.refs_0_ = f32[2,16,16,128]{3,2,1,0:T(8,128)S(1)} fusion(f32[1,16,16,128]{3,2,1,0:T(8,128)} %bitcast.2, f32[1,16,16,128]{3,2,1,0:T(8,128)} %bitcast.3), kind=kLoop, calls=%fused_computation | loop fusion | flops 65536 | bytes 524288 | tf_op jit(solution)/shard_map/stack | solution.py:881
  1.0 0.2 shard_map.28
  1.2 3.0 %collective-permute-start = (f32[336,128]{1,0:T(8,128)S(1)}, f32[336,128]{1,0:T(8,128)S(1)}, u32[]{:S(2)}, u32[]{:S(2)}) collective-permute-start(f32[336,128]{1,0:T(8,128)S(1)} %get-tuple-element.24), channel_id=1, source_target_pairs={{0,4},{1,5},{2,6},{3,7},{4,0},{5,1},{6,2},{7,3},{8,12},{9,13},{10,... | collective-permute-start | bytes 516104 | tf_op jit(solution)/shard_map/ppermute | solution.py:877
  4.2 0.0 collective-permute-start.4
  4.2 3.1 %collective-permute-start.5 = (f32[336,128]{1,0:T(8,128)S(1)}, f32[336,128]{1,0:T(8,128)S(1)}, u32[]{:S(2)}, u32[]{:S(2)}) collective-permute-start(f32[336,128]{1,0:T(8,128)S(1)} %get-tuple-element.31), channel_id=1, source_target_pairs={{0,8},{1,9},{2,10},{3,11},{4,12},{5,13},{6,14},{7,15},{8,0},{9,1},... | collective-permute-start | bytes 516104 | tf_op jit(solution)/shard_map/ppermute | solution.py:877
  7.4 0.1 collective-permute-start.1
  7.4 1.6 %collective-permute-start.2 = (f32[48,128]{1,0:T(8,128)S(1)}, f32[48,128]{1,0:T(8,128)S(1)}, u32[]{:S(2)}, u32[]{:S(2)}) collective-permute-start(f32[48,128]{1,0:T(8,128)S(1)} %get-tuple-element.26), channel_id=1, source_target_pairs={{0,7},{1,6},{2,5},{3,4},{4,3},{5,2},{6,1},{7,0},{8,15},{9,14},{10,... | collective-permute-start | bytes 73736 | tf_op jit(solution)/shard_map/ppermute | solution.py:877
  9.0 2.6 %collective-permute-done.2.refs_3_ = f32[48,128]{1,0:T(8,128)S(1)} collective-permute-done((f32[48,128]{1,0:T(8,128)S(1)}, f32[48,128]{1,0:T(8,128)S(1)}, u32[]{:S(2)}, u32[]{:S(2)}) %collective-permute-start.2) | collective-permute-done | bytes 24608 | tf_op jit(solution)/shard_map/ppermute | solution.py:877
  11.6 0.0 collective-permute-done.1.refs_2_
  11.6 0.0 collective-permute-done.refs_1_
  11.6 0.2 shard_map.29
  11.8 1.6 %collective-permute-start.3 = (f32[4,32,128]{2,1,0:T(8,128)S(1)}, f32[4,32,128]{2,1,0:T(8,128)S(1)}, u32[]{:S(2)}, u32[]{:S(2)}) collective-permute-start(f32[4,32,128]{2,1,0:T(8,128)S(1)} %get-tuple-element.29), channel_id=1, source_target_pairs={{0,1},{1,0},{2,3},{3,2},{4,5},{5,4},{6,7},{7,6},{8,9},{9,8},{10,11... | collective-permute-start | bytes 196616 | tf_op jit(solution)/shard_map/ppermute | solution.py:877
  13.4 0.0 collective-permute-done.4.refs_4_.refs_0_
  13.4 0.0 collective-permute-done.5.refs_3_.refs_2_
  13.4 0.9 %collective-permute-done.3.refs_3_.refs_2_ = f32[4,32,128]{2,1,0:T(8,128)S(1)} collective-permute-done((f32[4,32,128]{2,1,0:T(8,128)S(1)}, f32[4,32,128]{2,1,0:T(8,128)S(1)}, u32[]{:S(2)}, u32[]{:S(2)}) %collective-permute-start.3) | collective-permute-done | bytes 65568 | tf_op jit(solution)/shard_map/ppermute | solution.py:877
  14.3 0.2 shard_map.31
  14.5 0.4 %collective-permute-start.6 = (f32[248,128]{1,0:T(8,128)S(1)}, f32[248,128]{1,0:T(8,128)S(1)}, u32[]{:S(2)}, u32[]{:S(2)}) collective-permute-start(f32[248,128]{1,0:T(8,128)S(1)} %get-tuple-element.32), channel_id=1, source_target_pairs={{0,1},{1,0},{2,3},{3,2},{4,5},{5,4},{6,7},{7,6},{8,16},{9,17},{10,... | collective-permute-start | bytes 380936 | tf_op jit(solution)/shard_map/ppermute | solution.py:877
  14.9 1.3 %collective-permute-start.7 = (f32[248,128]{1,0:T(8,128)S(1)}, f32[248,128]{1,0:T(8,128)S(1)}, u32[]{:S(2)}, u32[]{:S(2)}) collective-permute-start(f32[248,128]{1,0:T(8,128)S(1)} %get-tuple-element.33), channel_id=1, source_target_pairs={{0,8},{1,9},{2,10},{3,11},{4,12},{5,13},{6,14},{7,15},{8,0},{9,1},... | collective-permute-start | bytes 380936 | tf_op jit(solution)/shard_map/ppermute | solution.py:877
  16.2 3.2 %shard_map.30.refs_0_ = f32[2,4,4,4,8,256]{5,4,3,2,1,0:T(8,128)S(1)} custom-call(f32[2,16,16,128]{3,2,1,0:T(8,128)S(1)} %pad_maximum_fusion.refs_0_, f32[2,16,16,128]{3,2,1,0:T(8,128)S(1)} %get-tuple-element.27.refs_1_.refs_0_, f32[4,32,128]{2,1,0:T(8,128)S(1)} %get-tuple-element.28.refs_2_.refs_1_, f32[4,32,128]{2,1,0:T(8,128)S(1)} %collective-permute-done.3.refs_3_.refs_2_), custom_call_target="tpu_custom_call" | custom-call | tf_op jit(solution)/shard_map/pallas_call | solution.py:856
  19.4 0.0 collective-permute-done.6.refs_1_
  19.4 0.9 %shard_map.32.refs_1_ = f32[2,4,4,4,8,128]{5,4,3,2,1,0:T(8,128)S(1)} custom-call(f32[336,128]{1,0:T(8,128)S(1)} %collective-permute-done.4.refs_4_.refs_0_, f32[248,128]{1,0:T(8,128)S(1)} %collective-permute-done.6.refs_1_), custom_call_target="tpu_custom_call" | custom-call | tf_op jit(solution)/shard_map/pallas_call | solution.py:856
  20.3 0.1 collective-permute-done.7.refs_3_
  20.4 3.3 %shard_map.33 = (f32[32,8,128]{2,1,0:T(8,128)S(1)}, f32[6,6,6,8,384]{4,3,2,1,0:T(8,128)S(1)}, f32[4,4,4,8,384]{4,3,2,1,0:T(8,128)S(1)}, f32[4,4,4,8,384]{4,3,2,1...) custom-call(f32[2,4,4,4,8,256]{5,4,3,2,1,0:T(8,128)S(1)} %shard_map., ...), custom_call_target="tpu_custom_call" | custom-call | tf_op jit(solution)/shard_map/pallas_call | solution.py:856
  23.7 10.4 %all_to_all.5.refs_0_ = f32[32,8,128]{2,1,0:T(8,128)S(1)} all-to-all(f32[32,8,128]{2,1,0:T(8,128)S(1)} %get-tuple-element.34), channel_id=1, replica_groups=mesh['grp'=4,'gy'=2,'gx'=4] {'grp','gy','gx'}, dimensions={0} | all-to-all | bytes 262144 | tf_op jit(solution)/shard_map/all_to_all | solution.py:945
  34.1 4.5 %shard_map.34 = f32[16,16,128]{2,1,0:T(8,128)} custom-call(f32[32,8,128]{2,1,0:T(8,128)S(1)} %all_to_all.5.refs_0_, f32[6,6,6,8,384]{4,3,2,1,0:T(8,128)S(1)} %get-tuple-element.35.refs_1_, f32[4,4,4,8,384]{4,3,2,1,0:T(8,128)S(1)} %get-tuple-element.36.refs_2_, f32[4,4,4,8,384]{4,3,2,1,0:T(8,128)S(1)} %get-tuple-element.37.refs_3_, ...), custom_call_target="tpu_custom_call" | custom-call | tf_op jit(solution)/shard_map/pallas_call | solution.py:856
Async XLA Ops:
  1.2 10.4 %collective-permute-start = (f32[336,128]{1,0:T(8,128)S(1)}, f32[336,128]{1,0:T(8,128)S(1)}, u32[]{:S(2)}, u32[]{:S(2)}) collective-permute-start(f32[336,128]{1,0:T(8,128)S(1)} %get-tuple-element.24), channel_id=1, source_target_pairs={{0,4},{1,5},{2,6},{3,7},{4,0},{5,1},{6,2},{7,3},{8,12},{9,13},{10,... | collective-permute-start | bytes 516104 | tf_op jit(solution)/shard_map/ppermute | solution.py:877
  4.2 9.2 %collective-permute-start.4 = (f32[336,128]{1,0:T(8,128)S(1)}, f32[336,128]{1,0:T(8,128)S(1)}, u32[]{:S(2)}, u32[]{:S(2)}) collective-permute-start(f32[336,128]{1,0:T(8,128)S(1)} %get-tuple-element.30), channel_id=1, source_target_pairs={{0,1},{1,0},{2,3},{3,2},{4,5},{5,4},{6,7},{7,6},{8,16},{9,17},{10,... | collective-permute-start | bytes 516104 | tf_op jit(solution)/shard_map/ppermute | solution.py:877
  4.2 9.2 %collective-permute-start.5 = (f32[336,128]{1,0:T(8,128)S(1)}, f32[336,128]{1,0:T(8,128)S(1)}, u32[]{:S(2)}, u32[]{:S(2)}) collective-permute-start(f32[336,128]{1,0:T(8,128)S(1)} %get-tuple-element.31), channel_id=1, source_target_pairs={{0,8},{1,9},{2,10},{3,11},{4,12},{5,13},{6,14},{7,15},{8,0},{9,1},... | collective-permute-start | bytes 516104 | tf_op jit(solution)/shard_map/ppermute | solution.py:877
  7.4 4.2 %collective-permute-start.1 = (f32[4,16,128]{2,1,0:T(8,128)S(1)}, f32[4,16,128]{2,1,0:T(8,128)S(1)}, u32[]{:S(2)}, u32[]{:S(2)}) collective-permute-start(f32[4,16,128]{2,1,0:T(8,128)S(1)} %get-tuple-element.25), channel_id=1, source_target_pairs={{0,3},{1,2},{2,1},{3,0},{4,7},{5,6},{6,5},{7,4},{8,11},{9,10},{10,... | collective-permute-start | bytes 98312 | tf_op jit(solution)/shard_map/ppermute | solution.py:877
  7.4 4.2 %collective-permute-start.2 = (f32[48,128]{1,0:T(8,128)S(1)}, f32[48,128]{1,0:T(8,128)S(1)}, u32[]{:S(2)}, u32[]{:S(2)}) collective-permute-start(f32[48,128]{1,0:T(8,128)S(1)} %get-tuple-element.26), channel_id=1, source_target_pairs={{0,7},{1,6},{2,5},{3,4},{4,3},{5,2},{6,1},{7,0},{8,15},{9,14},{10,... | collective-permute-start | bytes 73736 | tf_op jit(solution)/shard_map/ppermute | solution.py:877
  11.8 2.5 %collective-permute-start.3 = (f32[4,32,128]{2,1,0:T(8,128)S(1)}, f32[4,32,128]{2,1,0:T(8,128)S(1)}, u32[]{:S(2)}, u32[]{:S(2)}) collective-permute-start(f32[4,32,128]{2,1,0:T(8,128)S(1)} %get-tuple-element.29), channel_id=1, source_target_pairs={{0,1},{1,0},{2,3},{3,2},{4,5},{5,4},{6,7},{7,6},{8,9},{9,8},{10,11... | collective-permute-start | bytes 196616 | tf_op jit(solution)/shard_map/ppermute | solution.py:877
  14.5 4.9 %collective-permute-start.6 = (f32[248,128]{1,0:T(8,128)S(1)}, f32[248,128]{1,0:T(8,128)S(1)}, u32[]{:S(2)}, u32[]{:S(2)}) collective-permute-start(f32[248,128]{1,0:T(8,128)S(1)} %get-tuple-element.32), channel_id=1, source_target_pairs={{0,1},{1,0},{2,3},{3,2},{4,5},{5,4},{6,7},{7,6},{8,16},{9,17},{10,... | collective-permute-start | bytes 380936 | tf_op jit(solution)/shard_map/ppermute | solution.py:877
  14.9 5.5 %collective-permute-start.7 = (f32[248,128]{1,0:T(8,128)S(1)}, f32[248,128]{1,0:T(8,128)S(1)}, u32[]{:S(2)}, u32[]{:S(2)}) collective-permute-start(f32[248,128]{1,0:T(8,128)S(1)} %get-tuple-element.33), channel_id=1, source_target_pairs={{0,8},{1,9},{2,10},{3,11},{4,12},{5,13},{6,14},{7,15},{8,0},{9,1},... | collective-permute-start | bytes 380936 | tf_op jit(solution)/shard_map/ppermute | solution.py:877
